TPU v7x, 32 devices: a whole 2x2x4 slice. The times are simulated.
32 devices in a mesh: fsdp: 8 (over z, x), seq: 4 (over y, core).
Axes of the slice: x: 2, y: 2, z: 4, core: 2. Of those that a mesh axis runs over, the one named last changes fastest.
Arguments:
- block_in: float32 [8, 512, 768], P('fsdp', 'seq'), may hold values from -6 to 6
- expert_ids: int32 [8, 512, 2], P('fsdp', 'seq'), may hold values from 0 to 31, all different within a row; in each aligned block of 128 rows (0 to 127, 128 to 255, ..., all dimensions but the last counted through in order) at most 10 rows name the same one
- ln1_gain: bfloat16 [768], P(('fsdp', 'seq')), may hold values from 0.5 to 1.5
- ln1_bias: bfloat16 [768], P(('fsdp', 'seq')), may hold values from -1.796875 to 1.796875
- w_query: bfloat16 [768, 768], P(('fsdp', 'seq')), may hold values from -3 to 3
- w_key: bfloat16 [768, 768], P(('fsdp', 'seq')), may hold values from -3 to 3
- w_value: bfloat16 [768, 768], P(('fsdp', 'seq')), may hold values from -0.21875 to 0.21875
- w_output: bfloat16 [768, 768], P(('fsdp', 'seq')), may hold values from -6 to 6
- ln2_gain: bfloat16 [768], P(('fsdp', 'seq')), may hold values from 0.5 to 1.5
- ln2_bias: bfloat16 [768], P(('fsdp', 'seq')), may hold values from -1.796875 to 1.796875
- w_router: bfloat16 [768, 32], P(('fsdp', 'seq')), may hold values from -8 to 8
- w_expert_in: bfloat16 [64, 768, 1536], P('fsdp', None, 'seq'), may hold values from -0.21875 to 0.21875
- w_expert_out: bfloat16 [64, 1536, 768], P('fsdp', 'seq'), may hold values from -3 to 3
- cotangent: float32 [8, 512, 768], P('fsdp', 'seq'), may hold values from -6 to 6
Outputs:
- block_out: float32 [8, 512, 768], P('fsdp', 'seq')
- grad_in: float32 [8, 512, 768], P('fsdp', 'seq')
- grad_ln1_gain: float32 [768], P(('fsdp', 'seq'))
- grad_ln1_bias: float32 [768], P(('fsdp', 'seq'))
- grad_query: float32 [768, 768], P('fsdp', 'seq')
- grad_key: float32 [768, 768], P('fsdp', 'seq')
- grad_value: float32 [768, 768], P('fsdp', 'seq')
- grad_output: float32 [768, 768], P('seq', 'fsdp')
- grad_ln2_gain: float32 [768], P(('fsdp', 'seq'))
- grad_ln2_bias: float32 [768], P(('fsdp', 'seq'))
- grad_router: float32 [768, 32], P(('fsdp', 'seq'))
- grad_expert_in: float32 [64, 768, 1536], P('fsdp', None, 'seq')
- grad_expert_out: float32 [64, 1536, 768], P('fsdp', 'seq')
Inputs may be any that keep to these rules, and one draw needn't show every extreme that they name: `expert_ids`: each token names 2 different experts. Among the 128 tokens of one device (one aligned block), no expert is named more than 10 times.
All inputs are finite; a program needn't handle non-finite values.
Results may differ from a plain program's by a relative error of at most 0.025.
Values may be sent and summed in bfloat16 or wider, within the bound.
No kernel may reach another device: no remote copies, remote signals or barrier semaphores. Data moves between devices by JAX's collectives and lax.ppermute only.
A program may use at most 192 MiB of HBM per device.

v0:
```python
import functools

import jax
import jax.numpy as jnp
from jax import lax
from jax.experimental import pallas as pl
from jax.experimental.pallas import tpu as pltpu
from jax.sharding import PartitionSpec as P

D = 768
HEAD_DIM = 64
EXPERTS = 32
TOP = 2
CAP = 10


EPS = 1e-06
TANH_SCALE = 0.7978845608028654
CUBIC = 0.044715


def matmul(left_side, right_side):
    return jnp.dot(left_side, right_side, preferred_element_type=jnp.float32)


def matmul_t(left_side, right_side):
    return lax.dot_general(
        left_side, right_side, (((1,), (1,)), ((), ())), preferred_element_type=jnp.float32
    )


def t_matmul(left_side, right_side):
    return lax.dot_general(
        left_side, right_side, (((0,), (0,)), ((), ())), preferred_element_type=jnp.float32
    )


def norm_forward(values):
    centre = values - jnp.mean(values, -1, keepdims=True)
    inverse = lax.rsqrt(jnp.mean(centre * centre, -1, keepdims=True) + EPS)
    return (centre * inverse, inverse)


def norm_backward(grad_normed, normed, inverse):
    return inverse * (
        grad_normed
        - jnp.mean(grad_normed, -1, keepdims=True)
        - normed * jnp.mean(grad_normed * normed, -1, keepdims=True)
    )


def gelu_both(inner_act):
    square = inner_act * inner_act
    bent = jnp.tanh(TANH_SCALE * inner_act * (1.0 + CUBIC * square))
    value = 0.5 * inner_act * (1.0 + bent)
    slope = 0.5 * (1.0 + bent) + 0.5 * inner_act * (1.0 - bent * bent) * TANH_SCALE * (
        1.0 + 3.0 * CUBIC * square
    )
    return (value, slope)


SCALING = HEAD_DIM ** (-0.5)
MIB = 1024 * 1024
WHOLE = pl.BlockSpec(memory_space=pltpu.VMEM)


def call(kernel, outputs, operands, after=(), fresh=(), scratch=(), flops=0, mib=20):
    moved = sum(v.size * v.dtype.itemsize for v in operands)
    used = len(operands)

    def inner(*refs):
        kernel(*refs[:used], *refs[used + len(after) :])

    operands = [
        operand if index in fresh else in_hbm([operand])[0]
        for index, operand in enumerate(operands)
    ] + in_hbm(after)
    return pl.pallas_call(
        inner,
        out_shape=outputs,
        in_specs=[WHOLE] * used + [pl.BlockSpec(memory_space=pl.ANY)] * len(after),
        out_specs=[WHOLE] * len(outputs),
        scratch_shapes=scratch,
        cost_estimate=pl.CostEstimate(flops=flops, bytes_accessed=moved, transcendentals=0),
        compiler_params=pltpu.CompilerParams(vmem_limit_bytes=mib * MIB),
    )(*operands)


def shaped(dtype, *shape):
    return pltpu.HBM(shape, dtype)


def in_hbm(operands):
    return [pltpu.with_memory_space_constraint(operand, pltpu.HBM) for operand in operands]


def held_back(array, other):
    anywhere = pl.BlockSpec(memory_space=pl.ANY)
    return pl.pallas_call(
        lambda array_ref, other_ref, out_ref: None,
        out_shape=shaped(array.dtype, *array.shape),
        in_specs=[anywhere, anywhere],
        out_specs=anywhere,
        input_output_aliases={0: 0},
    )(*in_hbm([array]), other)


def attend_kernel(
    own, far, near, diag, held, normed_ref, normed_in_ref, qkv_ref, mixed_ref, logsum_ref, vec_ref
):
    bf16 = jnp.bfloat16
    f32 = jnp.float32
    columns = qkv_ref.shape[1]
    lanes = held.shape[1]
    wanted = lax.broadcasted_iota(jnp.int32, (8, lanes), 0) + (columns + EXPERTS)
    picker = (lax.broadcasted_iota(jnp.int32, (8, lanes), 1) == wanted).astype(bf16)
    vectors = matmul_t(picker, held[...])
    vec_ref[...] = vectors
    count = own.shape[0]
    for index, block in enumerate((own, far, near, diag)):
        normed, _ = norm_forward(block[...])
        rows = pl.ds(index * count, count)
        normed_ref[rows, :] = normed
        normed_in_ref[rows, :] = (normed * vectors[0:1] + vectors[1:2]).astype(bf16)
    qkv_ref[...] = matmul(normed_in_ref[...], held[:, :columns]).astype(bf16)
    width = columns // 3
    logsum_ref[...] = jnp.zeros_like(logsum_ref)
    for low in range(0, width, HEAD_DIM):
        query = qkv_ref[:, low : low + HEAD_DIM]
        key = qkv_ref[:, width + low : width + low + HEAD_DIM]
        value = qkv_ref[:, 2 * width + low : 2 * width + low + HEAD_DIM]
        scores = matmul_t(query, key) * SCALING
        highest = jnp.max(scores, -1, keepdims=True)
        raised = jnp.exp(scores - highest)
        total = jnp.sum(raised, -1, keepdims=True)
        head = low // HEAD_DIM
        logsum_ref[:, head : head + 1] = highest + jnp.log(total)
        weights = (raised * (1.0 / total)).astype(bf16)
        mixed_ref[:, low : low + HEAD_DIM] = matmul(weights, value).astype(bf16)


def attend_back_kernel(
    own,
    far,
    near,
    diag,
    w_out,
    held,
    qkv,
    mixed,
    logsum,
    normed,
    normed_in,
    small,
    gn_own,
    gn_far,
    gn_near,
    gn_diag,
    dw_ref,
    gr_ref,
    gqkv_ref,
):
    bf16 = jnp.bfloat16
    f32 = jnp.float32
    count = own.shape[0]
    columns = qkv.shape[1]
    width = columns // 3
    for index, block in enumerate((own, far, near, diag)):
        gr_ref[pl.ds(index * count, count), :] = block[...]
    grad_mixed = matmul_t(gr_ref[...], w_out[...]).astype(bf16)
    for low in range(0, width, HEAD_DIM):
        head = low // HEAD_DIM
        query = qkv[:, low : low + HEAD_DIM]
        key = qkv[:, width + low : width + low + HEAD_DIM]
        value = qkv[:, 2 * width + low : 2 * width + low + HEAD_DIM]
        grad_head = grad_mixed[:, low : low + HEAD_DIM]
        delta = jnp.sum(
            grad_head.astype(f32) * mixed[:, low : low + HEAD_DIM].astype(f32), -1, keepdims=True
        )
        probs = jnp.exp(matmul_t(query, key) * SCALING - logsum[:, head : head + 1])
        grad_probs = matmul_t(grad_head, value)
        grad_scores = (probs * (grad_probs - delta) * SCALING).astype(bf16)
        gqkv_ref[:, low : low + HEAD_DIM] = matmul(grad_scores, key).astype(bf16)
        gqkv_ref[:, width + low : width + low + HEAD_DIM] = t_matmul(grad_scores, query).astype(
            bf16
        )
        gqkv_ref[:, 2 * width + low : 2 * width + low + HEAD_DIM] = t_matmul(
            probs.astype(bf16), grad_head
        ).astype(bf16)
    grad_normed = matmul_t(gqkv_ref[...], held[:, :columns])
    for index, block in enumerate((gn_own, gn_far, gn_near, gn_diag)):
        block[...] = grad_normed[index * count : (index + 1) * count].astype(bf16)
    dw_ref[:, :columns] = t_matmul(normed_in[...], gqkv_ref[...]).astype(bf16)
    dw_ref[:, columns : columns + width] = t_matmul(gr_ref[...], mixed[...]).astype(bf16)
    gain_row = jnp.sum(grad_normed * normed[...], 0, keepdims=True)
    bias_row = jnp.sum(grad_normed, 0, keepdims=True)
    row = lax.broadcasted_iota(jnp.int32, (8, gain_row.shape[1]), 0)
    both = jnp.where(row == 0, gain_row, jnp.where(row == 1, bias_row, 0.0))
    sums = small[...] + columns_of(both, EXPERTS, small.shape[1])
    high = sums.astype(bf16)
    low = columns + width
    dw_ref[:, low:] = jnp.zeros((dw_ref.shape[0], dw_ref.shape[1] - low), bf16)
    dw_ref[:, low : low + sums.shape[1]] = high
    dw_ref[:, low + HEAD_DIM : low + HEAD_DIM + sums.shape[1]] = (
        sums - high.astype(f32)
    ).astype(bf16)


def columns_of(rows, first, lanes):
    count = rows.shape[0]
    spots = lax.broadcasted_iota(jnp.int32, (count, lanes), 1)
    placed = (spots == lax.broadcasted_iota(jnp.int32, (count, lanes), 0) + first).astype(
        jnp.float32
    )
    return lax.dot_general(
        rows,
        placed,
        (((0,), (0,)), ((), ())),
        preferred_element_type=jnp.float32,
        precision=lax.Precision.HIGHEST,
    )


def picks_of(position, choice, rows, copies):
    spots = lax.broadcasted_iota(jnp.int32, (position.shape[0], rows), 1)
    first = position[:, choice : choice + 1]
    hit = spots == first
    for copy in range(1, copies):
        hit = hit | (spots == first + copy * CAP)
    return hit.astype(jnp.float32)


def gates_of(probs, chosen, choice):
    spots = lax.broadcasted_iota(jnp.int32, probs.shape, 1)
    return jnp.sum(
        jnp.where(spots == chosen[:, choice : choice + 1], probs, 0.0), -1, keepdims=True
    )


def route_kernel(
    tokens_in, own, near, far, vectors, router, position, residual_ref, rows_ref, probs_ref, table_ref,
    *, copies
):
    bf16 = jnp.bfloat16
    f32 = jnp.float32
    residual = tokens_in[...] + (
        own[...].astype(f32) + near[...].astype(f32) + far[...].astype(f32)
    )
    residual_ref[...] = residual
    normed, _ = norm_forward(residual)
    rows = (normed * vectors[2:3, :] + vectors[3:4, :]).astype(bf16)
    rows_ref[...] = rows
    logits = matmul(rows, router[...])
    raised = jnp.exp(logits - jnp.max(logits, -1, keepdims=True))
    probs_ref[...] = raised / jnp.sum(raised, -1, keepdims=True)
    size = table_ref.shape[0]
    spots = picks_of(position[...], 0, size, copies) + picks_of(position[...], 1, size, copies)
    table_ref[...] = t_matmul(spots.astype(bf16), rows).astype(bf16)


def combine_kernel(
    residual, upstream, vectors, router, rows, probs, chosen, position, route_dots, table,
    own, near, far, regroup,
    grad_ref, half_ref, small_ref, settled_ref, *, copies
):
    bf16 = jnp.bfloat16
    f32 = jnp.float32
    size = table.shape[0]
    picks = [picks_of(position[...], choice, size, copies) for choice in range(TOP)]
    grad_probs = jnp.zeros(probs.shape, f32)
    spots = lax.broadcasted_iota(jnp.int32, probs.shape, 1)
    for choice in range(TOP):
        grad_gate = jnp.sum(picks[choice] * route_dots[0:1, :], -1, keepdims=True)
        grad_probs = grad_probs + jnp.where(
            spots == chosen[:, choice : choice + 1], grad_gate, 0.0
        )
    shares = probs[...]
    grad_logits = shares * (grad_probs - jnp.sum(shares * grad_probs, -1, keepdims=True))
    grad_logits = grad_logits.astype(bf16)
    grad_rows = matmul((picks[0] + picks[1]).astype(bf16), table[...]) + matmul_t(
        grad_logits, router[...]
    )
    normed, inverse = norm_forward(residual[...])
    grad = upstream[...] + norm_backward(grad_rows * vectors[2:3, :], normed, inverse)
    grad_ref[...] = grad
    half_ref[...] = grad.astype(bf16)
    gain_row = jnp.sum(grad_rows * normed, 0, keepdims=True)
    bias_row = jnp.sum(grad_rows, 0, keepdims=True)
    row = lax.broadcasted_iota(jnp.int32, (8, gain_row.shape[1]), 0)
    both = jnp.where(row == 0, gain_row, jnp.where(row == 1, bias_row, 0.0))
    lanes = small_ref.shape[1]
    small_ref[...] = columns_of(both, EXPERTS + 2, lanes)
    small_ref[:, :EXPERTS] = t_matmul(rows[...], grad_logits)
    settle_kernel(own, near, far, regroup, settled_ref)


def block_out_kernel(residual, probs, chosen, position, table, out_ref, *, copies):
    out = residual[...]
    for choice in range(TOP):
        pick = picks_of(position[...], choice, table.shape[0], copies).astype(jnp.bfloat16)
        out = out + gates_of(probs[...], chosen, choice) * matmul(pick, table[...])
    out_ref[...] = out


def expert_kernel(
    first,
    x_own, x_far, x_near, x_diag,
    c_own, c_far, c_near, c_diag,
    router, w_in, w_out,
    o_own, o_far, o_near, o_diag,
    g_own, g_far, g_near, g_diag,
    rows_ref, cots_ref, hidden_ref, inner_ref, dots_ref,
):
    bf16 = jnp.bfloat16
    f32 = jnp.float32
    count = x_own.shape[1]
    parts = [pl.ds(index * count, count) for index in range(4)]
    for part, block, cots in zip(
        parts, (x_own, x_far, x_near, x_diag), (c_own, c_far, c_near, c_diag)
    ):
        rows_ref[0, part, :] = block[0]
        cots_ref[0, part, :] = cots[0]
    rows = rows_ref[0]
    bare = cots_ref[0]
    logits = matmul(rows, router[...])
    raised = jnp.exp(logits - jnp.max(logits, -1, keepdims=True))
    wanted = first[0] + pl.program_id(0)
    spots = lax.broadcasted_iota(jnp.int32, logits.shape, 1)
    gate = jnp.sum(jnp.where(spots == wanted, raised, 0.0), -1, keepdims=True) / jnp.sum(
        raised, -1, keepdims=True
    )
    cots = (gate * bare.astype(f32)).astype(bf16)
    cots_ref[0] = cots
    out_sum = None
    for half in range(w_in.shape[0]):
        value, slope = gelu_both(matmul(rows, w_in[half]))
        hidden = value.astype(bf16)
        hidden_ref[half] = hidden
        inner = (matmul_t(cots, w_out[half]) * slope).astype(bf16)
        inner_ref[half] = inner
        out = matmul(hidden, w_out[half])
        grad = matmul_t(inner, w_in[half])
        out_sum = out if out_sum is None else out_sum + out
        grad_sum = grad if half == 0 else grad_sum + grad
    dots = jnp.sum(out_sum * bare.astype(f32), -1, keepdims=True)
    dots_ref[0] = jnp.broadcast_to(dots, dots_ref.shape[1:])
    for index, (out, grad) in enumerate(
        zip((o_own, o_far, o_near, o_diag), (g_own, g_far, g_near, g_diag))
    ):
        low = index * count
        out[0] = out_sum[low : low + count].astype(bf16)
        grad[0] = grad_sum[low : low + count].astype(bf16)


def experts(first, rows, cots, router, w_in, w_out):
    bf16 = jnp.bfloat16
    f32 = jnp.float32
    local_experts, count, _ = rows[0].shape
    slices, _, hidden_cols = w_in.shape
    halves = slices // local_experts
    total = 4 * count
    by_expert = pl.BlockSpec((1, count, D), lambda e: (e, 0, 0))
    by_expert_all = pl.BlockSpec((1, total, D), lambda e: (e, 0, 0))
    by_slice = lambda *shape: pl.BlockSpec((halves,) + shape, lambda e: (e, 0, 0))
    flops = 8 * slices * total * D * hidden_cols
    moved = 4 * slices * D * hidden_cols + 12 * local_experts * total * D
    return pl.pallas_call(
        expert_kernel,
        grid=(local_experts,),
        in_specs=[pl.BlockSpec(memory_space=pltpu.SMEM)]
        + [by_expert] * 8
        + [
            pl.BlockSpec((D, EXPERTS), lambda e: (0, 0)),
            by_slice(D, hidden_cols),
            by_slice(hidden_cols, D),
        ],
        out_specs=[by_expert] * 8
        + [
            by_expert_all,
            by_expert_all,
            by_slice(total, hidden_cols),
            by_slice(total, hidden_cols),
            pl.BlockSpec((1, total, 8), lambda e: (e, 0, 0)),
        ],
        out_shape=[shaped(bf16, local_experts, count, D)] * 8
        + [shaped(bf16, local_experts, total, D)] * 2
        + [shaped(bf16, slices, total, hidden_cols)] * 2
        + [shaped(f32, local_experts, total, 8)],
        cost_estimate=pl.CostEstimate(flops=flops, bytes_accessed=moved, transcendentals=0),
        compiler_params=pltpu.CompilerParams(
            vmem_limit_bytes=(28 if count <= 128 else 58) * MIB
        ),
    )(first, *rows, *cots, router, *in_hbm([w_in, w_out]))


def product_kernel(left, right, out_ref):
    for index in range(out_ref.shape[0]):
        out_ref[index] = t_matmul(
            left[min(index, left.shape[0] - 1)], right[min(index, right.shape[0] - 1)]
        )


def expert_products(left, right):
    slices = max(left.shape[0], right.shape[0])
    local_experts = min(left.shape[0], right.shape[0])
    shape = (left.shape[2], right.shape[2])
    block = lambda first, *rest: pl.BlockSpec((first // local_experts,) + rest, lambda e: (e, 0, 0))
    flops = 2 * slices * left.shape[1] * shape[0] * shape[1]
    return pl.pallas_call(
        product_kernel,
        grid=(local_experts,),
        in_specs=[block(*left.shape), block(*right.shape)],
        out_specs=block(slices, *shape),
        out_shape=shaped(jnp.float32, slices, *shape),
        cost_estimate=pl.CostEstimate(
            flops=flops,
            bytes_accessed=4 * slices * shape[0] * shape[1] + 2 * (left.size + right.size),
            transcendentals=0,
        ),
        compiler_params=pltpu.CompilerParams(
            vmem_limit_bytes=(16 if left.shape[1] <= 512 else 48) * MIB
        ),
    )(*in_hbm([left, right]))


def settle_kernel(own, near, far, regroup, out_ref):
    f32 = jnp.float32
    summed = own[...].astype(f32) + near[...].astype(f32) + far[...].astype(f32)
    out_ref[...] = t_matmul(regroup[...], summed.astype(jnp.bfloat16)).astype(jnp.bfloat16)


def finish_kernel(received, query_ref, key_ref, value_ref, output_ref, small_ref):
    f32 = jnp.float32
    width = query_ref.shape[1]
    total = received[0].astype(f32)
    for index in range(1, received.shape[0]):
        total = total + received[index].astype(f32)
    query_ref[...] = total[:, :width]
    key_ref[...] = total[:, width : 2 * width]
    value_ref[...] = total[:, 2 * width : 3 * width]
    output_ref[...] = total[:, 3 * width : 4 * width].T
    low = 4 * width
    lanes = small_ref.shape[1]
    small_ref[...] = (
        total[:, low : low + lanes] + total[:, low + HEAD_DIM : low + HEAD_DIM + lanes]
    )


def weight_blocks_kernel(query, key, value, router, gain1, bias1, gain2, bias2, out_ref):
    bf16 = jnp.bfloat16
    devices_on, seq_size, shard, lanes = out_ref.shape
    width = query.shape[1] // seq_size
    spots = lax.broadcasted_iota(jnp.int32, (8, shard), 0)
    vectors = jnp.zeros((8, shard), bf16)
    for index, vector in enumerate((gain1, bias1, gain2, bias2)):
        vectors = jnp.where(spots == index, vector[...], vectors)
    tail = lanes - 3 * width
    where_to = lax.broadcasted_iota(jnp.int32, (8, tail), 0) + EXPERTS
    placed = (lax.broadcasted_iota(jnp.int32, (8, tail), 1) == where_to).astype(bf16)
    rest = t_matmul(vectors, placed).astype(bf16)
    for part in range(seq_size):
        low = part * width
        for index, matrix in enumerate((query, key, value)):
            block = matrix[:, low : low + width]
            for copy in range(devices_on):
                out_ref[copy, part, :, index * width : (index + 1) * width] = block
        for copy in range(devices_on):
            out_ref[copy, part, :, 3 * width :] = rest
            out_ref[copy, part, :, 3 * width : 3 * width + EXPERTS] = router[...]


FAR = [(index, index ^ 2) for index in range(4)]
NEAR = [(index, index ^ 1) for index in range(4)]


def seq_gather(block):
    far = lax.ppermute(block, "seq", FAR)
    return (block, far, lax.ppermute(block, "seq", NEAR), lax.ppermute(far, "seq", NEAR))


def seq_reduce(own, far, near, diag):
    beside = lax.ppermute(diag, "seq", NEAR)
    pair = (far.astype(jnp.float32) + beside.astype(jnp.float32)).astype(far.dtype)
    return (own, lax.ppermute(near, "seq", NEAR), lax.ppermute(pair, "seq", FAR))


def body(
    block_in,
    expert_ids,
    ln1_gain,
    ln1_bias,
    w_query,
    w_key,
    w_value,
    w_output,
    ln2_gain,
    ln2_bias,
    w_router,
    w_expert_in,
    w_expert_out,
    cotangent,
):
    bf16 = jnp.bfloat16
    f32 = jnp.float32
    fsdp_size = lax.axis_size("fsdp")
    seq_size = lax.axis_size("seq")
    devices = fsdp_size * seq_size
    shard = w_query.shape[0]
    head_cols = D // seq_size
    local_slices = w_expert_in.shape[0]
    local_experts = max(1, local_slices // 2)
    halves = local_slices // local_experts
    copies = 2 // halves
    tokens_in = block_in[0]
    upstream = cotangent[0]
    chosen = expert_ids[0]
    token_count = chosen.shape[0]

    moves = [
        (fsdp_size * part + place, seq_size * place + part)
        for part in range(seq_size)
        for place in range(fsdp_size)
    ]
    w_out_rows = lax.ppermute(w_output, ("fsdp", "seq"), moves)
    w_out_rows = jnp.broadcast_to(w_out_rows, (fsdp_size, shard, D))
    w_out_rows = lax.all_to_all(w_out_rows, "fsdp", split_axis=0, concat_axis=0, tiled=True)
    w_out_rows = w_out_rows.reshape(head_cols, D)
    sent = call(
        weight_blocks_kernel,
        [shaped(bf16, fsdp_size, seq_size, shard, 3 * head_cols + EXPERTS + 4)],
        [w_query, w_key, w_value, w_router]
        + [v.reshape(1, shard) for v in (ln1_gain, ln1_bias, ln2_gain, ln2_bias)],
    )[0].reshape(devices, shard, -1)
    held = lax.all_to_all(sent, ("fsdp", "seq"), split_axis=0, concat_axis=0, tiled=True)
    held = held.reshape(D, -1)

    hot = (chosen.reshape(-1)[:, None] == jnp.arange(EXPERTS)[None, :]).astype(bf16)
    routes = token_count * TOP
    earlier = (jnp.arange(routes)[:, None] > jnp.arange(routes)[None, :]).astype(bf16)
    slot = jnp.sum(matmul(earlier, hot) * hot.astype(f32), 1).astype(jnp.int32)
    position = chosen * (CAP * copies) + slot.reshape(token_count, TOP)
    table_rows = EXPERTS * copies * CAP
    local_rows = local_experts * fsdp_size * CAP
    spot = jnp.arange(local_rows)
    source_of = (spot // CAP % fsdp_size) * (local_experts * CAP) + (
        spot // (CAP * fsdp_size) * CAP + spot % CAP
    )
    regroup = (source_of[:, None] == spot[None, :]).astype(bf16)

    def to_experts(table):
        table = table.reshape(fsdp_size, local_experts * CAP, D)
        received = lax.all_to_all(table, "fsdp", split_axis=0, concat_axis=0, tiled=True)
        grouped = matmul(regroup, received.reshape(local_rows, D)).astype(bf16)
        return seq_gather(grouped.reshape(local_experts, fsdp_size * CAP, D))

    def settle(partial, after):
        blocks = [part.reshape(local_rows, D) for part in seq_reduce(*partial)]
        return call(
            settle_kernel,
            [shaped(bf16, local_rows, D)],
            [*blocks, regroup],
            after=after,
            fresh=(1, 2),
            flops=2 * local_rows * local_rows * D,
        )[0]

    def from_experts(settled):
        returned = lax.all_to_all(
            settled.reshape(fsdp_size, local_experts * CAP, D),
            "fsdp",
            split_axis=0,
            concat_axis=0,
            tiled=True,
        )
        return returned.reshape(table_rows, D)

    image = token_count * seq_size
    columns = 3 * head_cols
    router = held[:, columns : columns + EXPERTS]
    normed_one, normed_in, qkv, head_mixed, logsum, vectors = call(
        attend_kernel,
        [
            shaped(f32, image, D),
            shaped(bf16, image, D),
            shaped(bf16, image, columns),
            shaped(bf16, image, head_cols),
            shaped(f32, image, 8),
            shaped(f32, 8, D),
        ],
        [*seq_gather(tokens_in), held],
        fresh=(1, 2, 3, 4),
        flops=2 * image * D * columns + 4 * image * image * head_cols,
    )
    out_partial = matmul(head_mixed, w_out_rows).astype(bf16)
    out_blocks = [out_partial[i * token_count : (i + 1) * token_count] for i in range(seq_size)]

    residual, expert_rows, router_probs, rows_table = call(
        functools.partial(route_kernel, copies=copies),
        [
            shaped(f32, token_count, D),
            shaped(bf16, token_count, D),
            shaped(f32, token_count, EXPERTS),
            shaped(bf16, table_rows, D),
        ],
        [tokens_in, *seq_reduce(*out_blocks), vectors, router, position],
        fresh=(1, 2, 3, 6),
    )
    spots = jnp.arange(table_rows)[None, None, :] - position[:, :, None]
    hits = (spots == 0) if copies == 1 else ((spots == 0) | (spots == CAP))
    cots_table = t_matmul(jnp.any(hits, 1).astype(bf16), upstream.astype(bf16)).astype(bf16)
    slot_cots = to_experts(cots_table)
    slot_rows = to_experts(rows_table)

    first = (lax.axis_index("fsdp") * local_slices // 2).astype(jnp.int32).reshape(1)
    results = experts(
        first,
        slot_rows,
        slot_cots,
        router,
        w_expert_in,
        w_expert_out,
    )
    out_parts, grad_parts = results[:4], results[4:8]
    all_rows, all_cots, hidden_act, grad_inner, dots = results[8:]
    grad_expert_in = expert_products(all_rows, grad_inner)
    grad_expert_out = expert_products(hidden_act, all_cots)
    me = lax.axis_index("seq")
    turned = jnp.array([0, 2, 1, 3])[me ^ jnp.arange(seq_size)]
    dots = dots[:, :, 0].reshape(local_experts, seq_size, fsdp_size, CAP)
    dots = jnp.take(dots.transpose(2, 1, 0, 3), turned, axis=1)
    dots = lax.all_to_all(
        dots.reshape(devices, 1, local_experts * CAP),
        ("fsdp", "seq"),
        split_axis=0,
        concat_axis=0,
        tiled=True,
    )
    route_dots = jnp.sum(dots.reshape(fsdp_size, seq_size, -1), 1).reshape(1, table_rows)
    grad_table = from_experts(settle(grad_parts, [grad_expert_in]))
    grad_residual, grad_res_half, small_sums, out_settled = call(
        functools.partial(combine_kernel, copies=copies),
        [
            shaped(f32, token_count, D),
            shaped(bf16, token_count, D),
            shaped(f32, D, EXPERTS + 4),
            shaped(bf16, local_rows, D),
        ],
        [
            residual,
            upstream,
            vectors,
            router,
            expert_rows,
            router_probs,
            chosen,
            position,
            route_dots,
            grad_table,
            *[block.reshape(local_rows, D) for block in seq_reduce(*out_parts)],
            regroup,
        ],
        after=[grad_expert_out],
        fresh=(6, 7, 8, 9, 11, 12),
    )

    out_table = from_experts(out_settled)
    block_out = call(
        functools.partial(block_out_kernel, copies=copies),
        [shaped(f32, token_count, D)],
        [residual, router_probs, chosen, position, out_table],
        fresh=(2, 3, 4),
    )[0]

    *gn_parts, grad_weights = call(
        attend_back_kernel,
        [shaped(bf16, token_count, D)] * 4
        + [shaped(bf16, D, 4 * head_cols + 2 * HEAD_DIM)],
        [
            *seq_gather(grad_res_half),
            w_out_rows,
            held,
            qkv,
            head_mixed,
            logsum,
            normed_one,
            normed_in,
            small_sums,
        ],
        fresh=(1, 2, 3, 4),
        scratch=[pltpu.VMEM((image, D), bf16), pltpu.VMEM((image, columns), bf16)],
        flops=4 * (4 * image * D * 4 * head_cols + 10 * image * image * head_cols),
    )
    grad_weights = held_back(grad_weights, out_table)
    grad_weights = lax.all_to_all(
        grad_weights.reshape(fsdp_size, D // fsdp_size, 4 * head_cols + 2 * HEAD_DIM),
        "fsdp",
        split_axis=0,
        concat_axis=0,
        tiled=True,
    )
    *grad_squares, small_sums = call(
        finish_kernel,
        [shaped(f32, D // fsdp_size, head_cols)] * 3
        + [shaped(f32, head_cols, D // fsdp_size), shaped(f32, D // fsdp_size, EXPERTS + 4)],
        [grad_weights],
        after=[block_out],
        fresh=(0,),
    )
    place = lax.axis_index("seq")
    for step, swap in ((2, FAR), (1, NEAR)):
        rows = small_sums.shape[0] // 2
        upper = (place // step) % 2
        away = lax.dynamic_slice_in_dim(small_sums, (1 - upper) * rows, rows)
        kept = lax.dynamic_slice_in_dim(small_sums, upper * rows, rows)
        small_sums = kept + lax.ppermute(away, "seq", swap)
    own, near, far = seq_reduce(*gn_parts)
    own_grad_normed = own.astype(f32) + near.astype(f32) + far.astype(f32)
    own_normed, own_inverse = norm_forward(tokens_in)
    grad_tokens = grad_residual + norm_backward(
        own_grad_normed * vectors[0], own_normed, own_inverse
    )
    return (
        block_out[None],
        grad_tokens[None],
        small_sums[:, EXPERTS],
        small_sums[:, EXPERTS + 1],
        *grad_squares,
        small_sums[:, EXPERTS + 2],
        small_sums[:, EXPERTS + 3],
        small_sums[:, :EXPERTS],
        grad_expert_in,
        grad_expert_out,
    )


def solution(mesh):
    return jax.shard_map(
        body,
        mesh=mesh,
        in_specs=(
            P("fsdp", "seq", None),
            P("fsdp", "seq", None),
            P(("fsdp", "seq")),
            P(("fsdp", "seq")),
            P(("fsdp", "seq"), None),
            P(("fsdp", "seq"), None),
            P(("fsdp", "seq"), None),
            P(("fsdp", "seq"), None),
            P(("fsdp", "seq")),
            P(("fsdp", "seq")),
            P(("fsdp", "seq"), None),
            P("fsdp", None, "seq"),
            P("fsdp", "seq", None),
            P("fsdp", "seq", None),
        ),
        out_specs=(
            P("fsdp", "seq", None),
            P("fsdp", "seq", None),
            P(("fsdp", "seq")),
            P(("fsdp", "seq")),
            P("fsdp", "seq"),
            P("fsdp", "seq"),
            P("fsdp", "seq"),
            P("seq", "fsdp"),
            P(("fsdp", "seq")),
            P(("fsdp", "seq")),
            P(("fsdp", "seq"), None),
            P("fsdp", None, "seq"),
            P("fsdp", "seq", None),
        ),
        check_vma=False,
    )
```

profile of v0, /device:TPU:0, one launch (start us, length us, event | category | flops | bytes accessed | tf_op | source)
XLA Modules:
  0.0 226.4 jit_solution(6691997627973306099)
XLA Ops:
  0.7 2.1 shard_map.246
  2.8 7.3 %all-to-all-start = ((bf16[32,24,612]{2,1,0:T(8,128)(2,1)}), bf16[32,24,612]{2,1,0:T(8,128)(2,1)S(1)}, u32[]{:S(2)}, u32[]{:S(2)}) async-start(bf16[32,24,612]{2,1,0:T(8,128)(2,1)} %bitcast.89), calls=%async_computation | async-start | bytes 1966080 | tf_op jit(solution)/shard_map/all_to_all | solution.py:534
  10.1 1.8 collective-permute-start
  12.0 0.7 collective-permute-start.3
  13.3 17.0 %collective-permute-done.refs_1_ = f32[128,768]{1,0:T(8,128)S(1)} collective-permute-done((f32[128,768]{1,0:T(8,128)S(1)}, f32[128,768]{1,0:T(8,128)S(1)}, u32[]{:S(2)}, u32[]{:S(2)}) %collective-permute-start) | collective-permute-done | bytes 393248 | tf_op jit(solution)/shard_map/ppermute | solution.py:477
  30.3 5.8 %all-to-all-done = bf16[32,24,612]{2,1,0:T(8,128)(2,1)S(1)} async-done(((bf16[32,24,612]{2,1,0:T(8,128)(2,1)}), bf16[32,24,612]{2,1,0:T(8,128)(2,1)S(1)}, u32[]{:S(2)}, u32[]{:S(2)}) %all-to-all-start) | async-done | bytes 940064 | tf_op jit(solution)/shard_map/all_to_all | solution.py:534
  36.1 0.8 broadcast_in_dim.20
  36.9 3.4 %all-to-all-start.1 = ((bf16[8,24,768]{2,1,0:T(8,128)(2,1)}), bf16[8,24,768]{2,1,0:T(8,128)(2,1)S(1)}, u32[]{:S(2)}, u32[]{:S(2)}) async-start(bf16[8,24,768]{2,1,0:T(8,128)(2,1)} %broadcast_in_dim.20), calls=%async_computation.1 | async-start | bytes 589824 | tf_op jit(solution)/shard_map/all_to_all | solution.py:526
  40.5 1.1 fusion.27
  41.6 4.8 %shard_map.247 = (f32[512,768]{1,0:T(8,128)}, bf16[512,768]{1,0:T(8,128)(2,1)}, bf16[512,576]{1,0:T(8,128)(2,1)}, bf16[512,192]{1,0:T(8,128)(2,1)}, f32[512,8]{1,0:T(8,128)}, /*index=5*/f32[8,768]{1,0:T(8,128)}) custom-call(f32[128,768]{1,0:T(8,128)} %bitcast.84, f32[128,768]{1,0:T(8,128)S(1)} %collective-permute-done.refs_1_, ...), custom_call_target="tpu_custom_call" | custom-call | flops 654311424 | bytes 2512896 | tf_op jit(solution)/shard_map/pallas_call | solution.py:78
  46.5 4.7 %all-to-all-done.1 = bf16[8,24,768]{2,1,0:T(8,128)(2,1)S(1)} async-done(((bf16[8,24,768]{2,1,0:T(8,128)(2,1)}), bf16[8,24,768]{2,1,0:T(8,128)(2,1)S(1)}, u32[]{:S(2)}, u32[]{:S(2)}) %all-to-all-start.1) | async-done | bytes 294944 | tf_op jit(solution)/shard_map/all_to_all | solution.py:526
  51.1 3.8 %all-to-all-start.3 = ((bf16[8,40,768]{2,1,0:T(8,128)(2,1)}), bf16[8,40,768]{2,1,0:T(8,128)(2,1)S(1)}, u32[]{:S(2)}, u32[]{:S(2)}) async-start(bf16[8,40,768]{2,1,0:T(8,128)(2,1)} %bitcast.15), calls=%async_computation.3 | async-start | bytes 983040 | tf_op jit(solution)/shard_map/all_to_all | solution.py:552
  54.9 1.3 convolution_convert_fusion
  56.3 0.5 collective-permute-start.4
  56.8 0.9 collective-permute-done.5
  58.1 0.8 slice.56.refs_5_.router.refs_3_
  58.9 6.0 %collective-permute-done.6.refs_3_ = bf16[128,768]{1,0:T(8,128)(2,1)S(1)} collective-permute-done((bf16[128,768]{1,0:T(8,128)(2,1)S(1)}, bf16[128,768]{1,0:T(8,128)(2,1)S(1)}, u32[]{:S(2)}, u32[]{:S(2)}) %collective-permute-start.6) | collective-permute-done | bytes 196640 | tf_op jit(solution)/shard_map/ppermute | solution.py:484
  64.8 2.5 %shard_map.248 = (f32[128,768]{1,0:T(8,128)}, bf16[128,768]{1,0:T(8,128)(2,1)}, f32[128,32]{1,0:T(8,128)}, bf16[320,768]{1,0:T(8,128)(2,1)}) custom-call(f32[128,768]{1,0:T(8,128)} %bitcast.85, bf16[128,768]{1,0:T(8,128)(2,1)S(1)} %get-tuple-element.95.refs_1_, bf16[128,768]{1,0:T(8,128)(2,1)S(1)} %collective-permute-done.4.refs_2_, ...), custom_call_target="tpu_custom_call" | custom-call | bytes 1057792 | tf_op jit(solution)/shard_map/pallas_call | solution.py:78
  67.3 1.6 all-to-all-done.3
  68.9 4.5 %all-to-all-start.2 = ((bf16[8,40,768]{2,1,0:T(8,128)(2,1)}), bf16[8,40,768]{2,1,0:T(8,128)(2,1)S(1)}, u32[]{:S(2)}, u32[]{:S(2)}) async-start(bf16[8,40,768]{2,1,0:T(8,128)(2,1)} %bitcast.98), calls=%async_computation.2 | async-start | bytes 983040 | tf_op jit(solution)/shard_map/all_to_all | solution.py:552
  73.5 0.5 convolution_convert_fusion.1
  74.3 12.5 %all-to-all-done.2 = bf16[8,40,768]{2,1,0:T(8,128)(2,1)S(1)} async-done(((bf16[8,40,768]{2,1,0:T(8,128)(2,1)}), bf16[8,40,768]{2,1,0:T(8,128)(2,1)S(1)}, u32[]{:S(2)}, u32[]{:S(2)}) %all-to-all-start.2) | async-done | bytes 491552 | tf_op jit(solution)/shard_map/all_to_all | solution.py:552
  86.8 0.5 convolution_convert_fusion.2
  87.2 0.4 collective-permute-start.7
  87.7 0.5 collective-permute-start.12
  88.2 10.6 %collective-permute-done.7.x_far = bf16[4,80,768]{2,1,0:T(8,128)(2,1)S(1)} collective-permute-done((bf16[4,80,768]{2,1,0:T(8,128)(2,1)S(1)}, bf16[4,80,768]{2,1,0:T(8,128)(2,1)S(1)}, u32[]{:S(2)}, u32[]{:S(2)}) %collective-permute-start.7) | collective-permute-done | bytes 491552 | tf_op jit(solution)/shard_map/ppermute | solution.py:477
  98.8 0.6 gather_fusion
  99.6 1.2 collective-permute-done.9.x_diag
  100.8 14.7 %shard_map.249 = (bf16[4,80,768]{2,1,0:T(8,128)(2,1)}, bf16[4,80,768]{2,1,0:T(8,128)(2,1)}, bf16[4,80,768]{2,1,0:T(8,128)(2,1)}, bf16[4,80,768]{2,1,0:T(8,128)(2...) custom-call(s32[1]{0:T(128)} %bitcast.11.first, ...), custom_call_target="tpu_custom_call" | custom-call | flops 6039797760 | bytes 21233664 | tf_op jit(solution)/shard_map/pallas_call | solution.py:367
  115.7 0.8 fusion.1.refs_3_.refs_13_
  117.1 0.6 collective-permute-done.14
  117.7 1.1 add_convert_fusion.1
  119.7 0.6 gather_fusion.1
  120.3 0.7 broadcast_select_fusion
  121.0 5.1 %all-to-all-start.4 = ((f32[32,1,40]{2,1,0:T(1,128)}), f32[32,1,40]{2,1,0:T(1,128)S(1)}, u32[]{:S(2)}, u32[]{:S(2)}) async-start(f32[32,1,40]{2,1,0:T(1,128)} %bitcast.22), calls=%async_computation.4 | async-start | bytes 32768 | tf_op jit(solution)/shard_map/all_to_all | solution.py:631
  126.1 7.6 %shard_map.250.refs_4_ = f32[8,768,384]{2,1,0:T(8,128)} custom-call(bf16[4,320,768]{2,1,0:T(8,128)(2,1)} %get-tuple-element.61.left, bf16[8,320,384]{2,1,0:T(8,128)(2,1)} %get-tuple-element.62.right), custom_call_target="tpu_custom_call" | custom-call | flops 1509949440 | bytes 13369344 | tf_op jit(solution)/shard_map/pallas_call | solution.py:409
  133.7 2.4 %shard_map.251 = bf16[320,768]{1,0:T(8,128)(2,1)} custom-call(bf16[320,768]{1,0:T(8,128)(2,1)} %bitcast.96, bf16[320,768]{1,0:T(8,128)(2,1)S(1)} %bitcast.80, bf16[320,768]{1,0:T(8,128)(2,1)S(1)} %bitcast.82, bf16[320,320]{1,0:T(8,128)(2,1)} %fusion.1.refs_3_.refs_13_, f32[8,768,384]{2,1,0:T(8,128)} %shard_map.250.refs_4_), custom_call_target="tpu_custom_call" | custom-call | flops 157286400 | bytes 1679360 | tf_op jit(solution)/shard_map/pallas_call | solution.py:78
  136.2 5.6 %all-to-all-start.5 = ((bf16[8,40,768]{2,1,0:T(8,128)(2,1)}), bf16[8,40,768]{2,1,0:T(8,128)(2,1)S(1)}, u32[]{:S(2)}, u32[]{:S(2)}) async-start(bf16[8,40,768]{2,1,0:T(8,128)(2,1)} %bitcast.91), calls=%async_computation.5 | async-start | bytes 983040 | tf_op jit(solution)/shard_map/all_to_all | solution.py:568
  142.0 1.6 collective-permute-start.18
  143.6 7.4 %shard_map.252.refs_14_ = f32[8,384,768]{2,1,0:T(8,128)} custom-call(bf16[8,320,384]{2,1,0:T(8,128)(2,1)} %get-tuple-element.67.left, bf16[4,320,768]{2,1,0:T(8,128)(2,1)} %get-tuple-element.68.right), custom_call_target="tpu_custom_call" | custom-call | flops 1509949440 | bytes 13369344 | tf_op jit(solution)/shard_map/pallas_call | solution.py:409
  151.1 4.6 %collective-permute-done.18 = bf16[4,80,768]{2,1,0:T(8,128)(2,1)S(1)} collective-permute-done((bf16[4,80,768]{2,1,0:T(8,128)(2,1)S(1)}, bf16[4,80,768]{2,1,0:T(8,128)(2,1)S(1)}, u32[]{:S(2)}, u32[]{:S(2)}) %collective-permute-start.18) | collective-permute-done | bytes 491552 | tf_op jit(solution)/shard_map/ppermute | solution.py:484
  155.9 4.2 %shard_map.253 = (f32[128,768]{1,0:T(8,128)}, bf16[128,768]{1,0:T(8,128)(2,1)}, f32[768,36]{1,0:T(8,128)}, bf16[320,768]{1,0:T(8,128)(2,1)}) custom-call(f32[128,768]{1,0:T(8,128)} %get-tuple-element.52.refs_0_, f32[128,768]{1,0:T(8,128)} %bitcast.93, f32[8,768]{1,0:T(8,128)} %get-tuple-element.51.refs_4_.refs_2_, ...), custom_call_target="tpu_custom_call" | custom-call | bytes 3247360 | tf_op jit(solution)/shard_map/pallas_call | solution.py:78
  160.1 1.5 collective-permute-start.19
  161.6 5.7 %all-to-all-start.6 = ((bf16[8,40,768]{2,1,0:T(8,128)(2,1)}), bf16[8,40,768]{2,1,0:T(8,128)(2,1)S(1)}, u32[]{:S(2)}, u32[]{:S(2)}) async-start(bf16[8,40,768]{2,1,0:T(8,128)(2,1)} %bitcast.97), calls=%async_computation.6 | async-start | bytes 983040 | tf_op jit(solution)/shard_map/all_to_all | solution.py:568
  167.3 0.5 collective-permute-start.21
  167.8 1.1 collective-permute-done.20.refs_2_
  169.0 9.0 %shard_map.255 = (bf16[128,768]{1,0:T(8,128)(2,1)}, bf16[128,768]{1,0:T(8,128)(2,1)}, bf16[128,768]{1,0:T(8,128)(2,1)}, bf16[128,768]{1,0:T(8,128)(2,1)}, bf16[768,896]{1,0:T(8,128)(2,1)}) custom-call(bf16[128,768]{1,0:T(8,128)(2,1)} %get-tuple-element.71.refs_0_, bf16[128,768]{1,0:T(8,128)(2,1)S(1)} %collective-permute-done.19.refs_1_, ...), custom_call_target="tpu_custom_call" | custom-call | flops 6845104128 | bytes 5294080 | tf_op jit(solution)/shard_map/pallas_call | solution.py:78
  178.0 2.7 %all-to-all-done.6 = bf16[8,40,768]{2,1,0:T(8,128)(2,1)S(1)} async-done(((bf16[8,40,768]{2,1,0:T(8,128)(2,1)}), bf16[8,40,768]{2,1,0:T(8,128)(2,1)S(1)}, u32[]{:S(2)}, u32[]{:S(2)}) %all-to-all-start.6) | async-done | bytes 491552 | tf_op jit(solution)/shard_map/all_to_all | solution.py:568
  180.7 0.8 copy-done.1
  181.6 3.8 %all-to-all-start.7 = ((bf16[8,96,896]{2,1,0:T(8,128)(2,1)}), bf16[8,96,896]{2,1,0:T(8,128)(2,1)S(1)}, u32[]{:S(2)}, u32[]{:S(2)}) async-start(bf16[8,96,896]{2,1,0:T(8,128)(2,1)} %bitcast.88), calls=%async_computation.7 | async-start | bytes 2752512 | tf_op jit(solution)/shard_map/all_to_all | solution.py:694
  185.8 0.6 collective-permute-start.22
  186.3 0.7 collective-permute-done.23
  187.0 0.6 collective-permute-start.24
  187.6 0.8 slice_reduce_fusion.5
  188.4 5.6 %collective-permute-done.24 = bf16[128,768]{1,0:T(8,128)(2,1)S(1)} collective-permute-done((bf16[128,768]{1,0:T(8,128)(2,1)S(1)}, bf16[128,768]{1,0:T(8,128)(2,1)S(1)}, u32[]{:S(2)}, u32[]{:S(2)}) %collective-permute-start.24) | collective-permute-done | bytes 196640 | tf_op jit(solution)/shard_map/ppermute | solution.py:484
  194.3 2.2 shard_map.254.refs_1_
  196.5 21.8 %all-to-all-done.7.refs_0_ = bf16[8,96,896]{2,1,0:T(8,128)(2,1)S(1)} async-done(((bf16[8,96,896]{2,1,0:T(8,128)(2,1)}), bf16[8,96,896]{2,1,0:T(8,128)(2,1)S(1)}, u32[]{:S(2)}, u32[]{:S(2)}) %all-to-all-start.7) | async-done | bytes 1376288 | tf_op jit(solution)/shard_map/all_to_all | solution.py:694
  218.2 0.9 shard_map.257
  219.2 0.7 constant_dynamic-slice_fusion.1
  219.9 0.5 collective-permute-start.25
  220.4 3.3 %collective-permute-done.25 = f32[48,36]{1,0:T(8,128)S(1)} collective-permute-done((f32[48,36]{1,0:T(8,128)S(1)}, f32[48,36]{1,0:T(8,128)S(1)}, u32[]{:S(2)}, u32[]{:S(2)}) %collective-permute-start.25) | collective-permute-done | bytes 6944 | tf_op jit(solution)/shard_map/ppermute | solution.py:715
  223.7 0.7 dynamic-slice_add_fusion
  224.5 0.9 add_bitcast_fusion
  225.7 0.7 slice_reduce_fusion.1
  (106 shorter events, 4.9 us)
Async XLA Ops:
  0.6 9.5 %copy-start.5 = (f32[1,128,768]{2,1,0:T(8,128)S(1)}, f32[1,128,768]{2,1,0:T(8,128)}, u32[]{:S(2)}) copy-start(f32[1,128,768]{2,1,0:T(8,128)} %param.15) | copy-start | bytes 1179652
  0.7 11.3 %copy-start.18 = (bf16[24,768]{1,0:T(8,128)(2,1)S(1)}, bf16[24,768]{1,0:T(8,128)(2,1)}, u32[]{:S(2)}) copy-start(bf16[24,768]{1,0:T(8,128)(2,1)} %param.22) | copy-start | bytes 110596
  0.7 12.0 %copy-start.14 = (s32[1,128,2]{1,2,0:T(2,128)S(1)}, s32[1,128,2]{1,2,0:T(2,128)}, u32[]{:S(2)}) copy-start(s32[1,128,2]{1,2,0:T(2,128)} %param.16) | copy-start | bytes 3076
  2.8 37.7 %copy-start.7 = (f32[1,128,768]{2,1,0:T(8,128)S(1)}, f32[1,128,768]{2,1,0:T(8,128)}, u32[]{:S(2)}) copy-start(f32[1,128,768]{2,1,0:T(8,128)} %param.28) | copy-start | bytes 1179652
  2.8 33.3 %all-to-all-start = ((bf16[32,24,612]{2,1,0:T(8,128)(2,1)}), bf16[32,24,612]{2,1,0:T(8,128)(2,1)S(1)}, u32[]{:S(2)}, u32[]{:S(2)}) async-start(bf16[32,24,612]{2,1,0:T(8,128)(2,1)} %bitcast.89), calls=%async_computation | async-start | bytes 1966080 | tf_op jit(solution)/shard_map/all_to_all | solution.py:534
  10.1 20.2 %collective-permute-start = (f32[128,768]{1,0:T(8,128)S(1)}, f32[128,768]{1,0:T(8,128)S(1)}, u32[]{:S(2)}, u32[]{:S(2)}) collective-permute-start(f32[128,768]{1,0:T(8,128)S(1)} %bitcast.86), channel_id=1, source_target_pairs={{0,2},{1,3},{2,0},{3,1},{4,6},{5,7},{6,4},{7,5},{8,10},{9,11},{10,... | collective-permute-start | bytes 1179656 | tf_op jit(solution)/shard_map/ppermute | solution.py:477
  12.0 29.6 %collective-permute-start.1 = (f32[128,768]{1,0:T(8,128)S(1)}, f32[128,768]{1,0:T(8,128)S(1)}, u32[]{:S(2)}, u32[]{:S(2)}) collective-permute-start(f32[128,768]{1,0:T(8,128)S(1)} %bitcast.87), channel_id=1, source_target_pairs={{0,1},{1,0},{2,3},{3,2},{4,5},{5,4},{6,7},{7,6},{8,9},{9,8},{10,11... | collective-permute-start | bytes 1179656 | tf_op jit(solution)/shard_map/ppermute | solution.py:478
  12.0 18.3 %collective-permute-start.3 = (bf16[24,768]{1,0:T(8,128)(2,1)S(1)}, bf16[24,768]{1,0:T(8,128)(2,1)S(1)}, u32[]{:S(2)}, u32[]{:S(2)}) collective-permute-start(bf16[24,768]{1,0:T(8,128)(2,1)S(1)} %copy-done.18), channel_id=1, source_target_pairs={{0,0},{1,4},{2,8},{3,12},{4,16},{5,20},{6,24},{7,28},{8,1},{9,5},{... | collective-permute-start | bytes 110600 | tf_op jit(solution)/shard_map/ppermute | solution.py:524
  30.3 11.3 %collective-permute-start.2 = (f32[128,768]{1,0:T(8,128)S(1)}, f32[128,768]{1,0:T(8,128)S(1)}, u32[]{:S(2)}, u32[]{:S(2)}) collective-permute-start(f32[128,768]{1,0:T(8,128)S(1)} %collective-permute-done.refs_1_), channel_id=1, source_target_pairs={{0,1},{1,0},{2,3},{3,2},{4,5},{5,4},{6,7},{7,6},{8,9},{9,8},{10,11... | collective-permute-start | bytes 1179656 | tf_op jit(solution)/shard_map/ppermute | solution.py:478
  36.1 21.9 %copy-start = (bf16[32,24,612]{2,1,0:T(8,128)(2,1)}, bf16[32,24,612]{2,1,0:T(8,128)(2,1)S(1)}, u32[]{:S(2)}) copy-start(bf16[32,24,612]{2,1,0:T(8,128)(2,1)S(1)} %all-to-all-done) | copy-start | bytes 2820100
  36.9 14.2 %all-to-all-start.1 = ((bf16[8,24,768]{2,1,0:T(8,128)(2,1)}), bf16[8,24,768]{2,1,0:T(8,128)(2,1)S(1)}, u32[]{:S(2)}, u32[]{:S(2)}) async-start(bf16[8,24,768]{2,1,0:T(8,128)(2,1)} %broadcast_in_dim.20), calls=%async_computation.1 | async-start | bytes 589824 | tf_op jit(solution)/shard_map/all_to_all | solution.py:526
  51.1 17.8 %all-to-all-start.3 = ((bf16[8,40,768]{2,1,0:T(8,128)(2,1)}), bf16[8,40,768]{2,1,0:T(8,128)(2,1)S(1)}, u32[]{:S(2)}, u32[]{:S(2)}) async-start(bf16[8,40,768]{2,1,0:T(8,128)(2,1)} %bitcast.15), calls=%async_computation.3 | async-start | bytes 983040 | tf_op jit(solution)/shard_map/all_to_all | solution.py:552
  56.2 1.5 collective-permute-start.5
  56.3 2.5 %collective-permute-start.4 = (bf16[128,768]{1,0:T(8,128)(2,1)S(1)}, bf16[128,768]{1,0:T(8,128)(2,1)S(1)}, u32[]{:S(2)}, u32[]{:S(2)}) collective-permute-start(bf16[128,768]{1,0:T(8,128)(2,1)S(1)} %get-tuple-element.94), channel_id=1, source_target_pairs={{0,1},{1,0},{2,3},{3,2},{4,5},{5,4},{6,7},{7,6},{8,9},{9,8},{10,11... | collective-permute-start | bytes 589832 | tf_op jit(solution)/shard_map/ppermute | solution.py:484
  57.8 7.0 %collective-permute-start.6 = (bf16[128,768]{1,0:T(8,128)(2,1)S(1)}, bf16[128,768]{1,0:T(8,128)(2,1)S(1)}, u32[]{:S(2)}, u32[]{:S(2)}) collective-permute-start(bf16[128,768]{1,0:T(8,128)(2,1)S(1)} %add_convert_fusion.3), channel_id=1, source_target_pairs={{0,2},{1,3},{2,0},{3,1},{4,6},{5,7},{6,4},{7,5},{8,10},{9,11},{10,... | collective-permute-start | bytes 589832 | tf_op jit(solution)/shard_map/ppermute | solution.py:484
  64.8 34.0 %copy-start.4 = (s32[4]{0:T(128)S(1)}, s32[4]{0:T(128)}, u32[]{:S(2)}) copy-start(s32[4]{0:T(128)} %constant.130.clone) | copy-start | bytes 52
  67.3 33.5 %copy-start.3 = (bf16[768,32]{1,0:T(8,128)(2,1)S(1)}, bf16[768,32]{1,0:T(8,128)(2,1)}, u32[]{:S(2)}) copy-start(bf16[768,32]{1,0:T(8,128)(2,1)} %slice.56.refs_5_.router.refs_3_) | copy-start | bytes 147460
  68.9 17.8 %all-to-all-start.2 = ((bf16[8,40,768]{2,1,0:T(8,128)(2,1)}), bf16[8,40,768]{2,1,0:T(8,128)(2,1)S(1)}, u32[]{:S(2)}, u32[]{:S(2)}) async-start(bf16[8,40,768]{2,1,0:T(8,128)(2,1)} %bitcast.98), calls=%async_computation.2 | async-start | bytes 983040 | tf_op jit(solution)/shard_map/all_to_all | solution.py:552
  73.9 13.7 %collective-permute-start.10 = (bf16[4,80,768]{2,1,0:T(8,128)(2,1)S(1)}, bf16[4,80,768]{2,1,0:T(8,128)(2,1)S(1)}, u32[]{:S(2)}, u32[]{:S(2)}) collective-permute-start(bf16[4,80,768]{2,1,0:T(8,128)(2,1)S(1)} %bitcast.74), channel_id=1, source_target_pairs={{0,2},{1,3},{2,0},{3,1},{4,6},{5,7},{6,4},{7,5},{8,10},{9,11},{10,... | collective-permute-start | bytes 1474568 | tf_op jit(solution)/shard_map/ppermute | solution.py:477
  87.2 11.6 %collective-permute-start.7 = (bf16[4,80,768]{2,1,0:T(8,128)(2,1)S(1)}, bf16[4,80,768]{2,1,0:T(8,128)(2,1)S(1)}, u32[]{:S(2)}, u32[]{:S(2)}) collective-permute-start(bf16[4,80,768]{2,1,0:T(8,128)(2,1)S(1)} %bitcast.77), channel_id=1, source_target_pairs={{0,2},{1,3},{2,0},{3,1},{4,6},{5,7},{6,4},{7,5},{8,10},{9,11},{10,... | collective-permute-start | bytes 1474568 | tf_op jit(solution)/shard_map/ppermute | solution.py:477
  87.7 11.9 %collective-permute-start.11 = (bf16[4,80,768]{2,1,0:T(8,128)(2,1)S(1)}, bf16[4,80,768]{2,1,0:T(8,128)(2,1)S(1)}, u32[]{:S(2)}, u32[]{:S(2)}) collective-permute-start(bf16[4,80,768]{2,1,0:T(8,128)(2,1)S(1)} %bitcast.75), channel_id=1, source_target_pairs={{0,1},{1,0},{2,3},{3,2},{4,5},{5,4},{6,7},{7,6},{8,9},{9,8},{10,11... | collective-permute-start | bytes 1474568 | tf_op jit(solution)/shard_map/ppermute | solution.py:478
  87.7 11.9 %collective-permute-start.12 = (bf16[4,80,768]{2,1,0:T(8,128)(2,1)S(1)}, bf16[4,80,768]{2,1,0:T(8,128)(2,1)}, u32[]{:S(2)}, u32[]{:S(2)}) collective-permute-start(bf16[4,80,768]{2,1,0:T(8,128)(2,1)S(1)} %collective-permute-done.10.c_far), channel_id=1, source_target_pairs={{0,1},{1,0},{2,3},{3,2},{4,5},{5,4},{6,7},{7,6},{8,9},{9,8},{10,11... | collective-permute-start | bytes 1474568 | tf_op jit(solution)/shard_map/ppermute | solution.py:478
  88.2 11.4 %collective-permute-start.8 = (bf16[4,80,768]{2,1,0:T(8,128)(2,1)S(1)}, bf16[4,80,768]{2,1,0:T(8,128)(2,1)}, u32[]{:S(2)}, u32[]{:S(2)}) collective-permute-start(bf16[4,80,768]{2,1,0:T(8,128)(2,1)S(1)} %bitcast.78), channel_id=1, source_target_pairs={{0,1},{1,0},{2,3},{3,2},{4,5},{5,4},{6,7},{7,6},{8,9},{9,8},{10,11... | collective-permute-start | bytes 1474568 | tf_op jit(solution)/shard_map/ppermute | solution.py:478
  98.8 2.0 collective-permute-start.9
  115.5 3.7 %copy-start.9 = (f32[4,320,8]{2,1,0:T(8,128)S(1)}, f32[4,320,8]{2,1,0:T(8,128)}, u32[]{:S(2)}) copy-start(f32[4,320,8]{2,1,0:T(8,128)} %get-tuple-element.56) | copy-start | bytes 122884
  115.5 2.1 collective-permute-start.14
  116.6 17.1 %collective-permute-start.13 = (bf16[4,80,768]{2,1,0:T(8,128)(2,1)}, bf16[4,80,768]{2,1,0:T(8,128)(2,1)S(1)}, u32[]{:S(2)}, u32[]{:S(2)}) collective-permute-start(bf16[4,80,768]{2,1,0:T(8,128)(2,1)} %get-tuple-element.58), channel_id=1, source_target_pairs={{0,1},{1,0},{2,3},{3,2},{4,5},{5,4},{6,7},{7,6},{8,9},{9,8},{10,11... | collective-permute-start | bytes 1474568 | tf_op jit(solution)/shard_map/ppermute | solution.py:484
  116.9 25.0 %collective-permute-start.17 = (bf16[4,80,768]{2,1,0:T(8,128)(2,1)}, bf16[4,80,768]{2,1,0:T(8,128)(2,1)S(1)}, u32[]{:S(2)}, u32[]{:S(2)}) collective-permute-start(bf16[4,80,768]{2,1,0:T(8,128)(2,1)} %get-tuple-element.66), channel_id=1, source_target_pairs={{0,1},{1,0},{2,3},{3,2},{4,5},{5,4},{6,7},{7,6},{8,9},{9,8},{10,11... | collective-permute-start | bytes 1474568 | tf_op jit(solution)/shard_map/ppermute | solution.py:482
  118.8 14.9 %collective-permute-start.15 = (bf16[4,80,768]{2,1,0:T(8,128)(2,1)S(1)}, bf16[4,80,768]{2,1,0:T(8,128)(2,1)S(1)}, u32[]{:S(2)}, u32[]{:S(2)}) collective-permute-start(bf16[4,80,768]{2,1,0:T(8,128)(2,1)S(1)} %add_convert_fusion.1), channel_id=1, source_target_pairs={{0,2},{1,3},{2,0},{3,1},{4,6},{5,7},{6,4},{7,5},{8,10},{9,11},{10,... | collective-permute-start | bytes 1474568 | tf_op jit(solution)/shard_map/ppermute | solution.py:484
  121.0 15.1 %all-to-all-start.4 = ((f32[32,1,40]{2,1,0:T(1,128)}), f32[32,1,40]{2,1,0:T(1,128)S(1)}, u32[]{:S(2)}, u32[]{:S(2)}) async-start(f32[32,1,40]{2,1,0:T(1,128)} %bitcast.22), calls=%async_computation.4 | async-start | bytes 32768 | tf_op jit(solution)/shard_map/all_to_all | solution.py:631
  133.7 8.1 %copy-start.15 = (bf16[4,80,768]{2,1,0:T(8,128)(2,1)S(1)}, bf16[4,80,768]{2,1,0:T(8,128)(2,1)}, u32[]{:S(2)}) copy-start(bf16[4,80,768]{2,1,0:T(8,128)(2,1)} %get-tuple-element.64) | copy-start | bytes 1474564
  133.7 8.2 %copy-start.10 = (bf16[4,80,768]{2,1,0:T(8,128)(2,1)S(1)}, bf16[4,80,768]{2,1,0:T(8,128)(2,1)}, u32[]{:S(2)}) copy-start(bf16[4,80,768]{2,1,0:T(8,128)(2,1)} %get-tuple-element.65) | copy-start | bytes 1474564
  136.2 19.7 %all-to-all-start.5 = ((bf16[8,40,768]{2,1,0:T(8,128)(2,1)}), bf16[8,40,768]{2,1,0:T(8,128)(2,1)S(1)}, u32[]{:S(2)}, u32[]{:S(2)}) async-start(bf16[8,40,768]{2,1,0:T(8,128)(2,1)} %bitcast.91), calls=%async_computation.5 | async-start | bytes 983040 | tf_op jit(solution)/shard_map/all_to_all | solution.py:568
  141.8 9.2 %collective-permute-start.16 = (bf16[4,80,768]{2,1,0:T(8,128)(2,1)S(1)}, bf16[4,80,768]{2,1,0:T(8,128)(2,1)S(1)}, u32[]{:S(2)}, u32[]{:S(2)}) collective-permute-start(bf16[4,80,768]{2,1,0:T(8,128)(2,1)S(1)} %copy-done.15), channel_id=1, source_target_pairs={{0,1},{1,0},{2,3},{3,2},{4,5},{5,4},{6,7},{7,6},{8,9},{9,8},{10,11... | collective-permute-start | bytes 1474568 | tf_op jit(solution)/shard_map/ppermute | solution.py:484
  142.0 13.7 %collective-permute-start.18 = (bf16[4,80,768]{2,1,0:T(8,128)(2,1)S(1)}, bf16[4,80,768]{2,1,0:T(8,128)(2,1)S(1)}, u32[]{:S(2)}, u32[]{:S(2)}) collective-permute-start(bf16[4,80,768]{2,1,0:T(8,128)(2,1)S(1)} %add_convert_fusion), channel_id=1, source_target_pairs={{0,2},{1,3},{2,0},{3,1},{4,6},{5,7},{6,4},{7,5},{8,10},{9,11},{10,... | collective-permute-start | bytes 1474568 | tf_op jit(solution)/shard_map/ppermute | solution.py:484
  160.1 7.2 %collective-permute-start.19 = (bf16[128,768]{1,0:T(8,128)(2,1)}, bf16[128,768]{1,0:T(8,128)(2,1)S(1)}, u32[]{:S(2)}, u32[]{:S(2)}) collective-permute-start(bf16[128,768]{1,0:T(8,128)(2,1)} %get-tuple-element.71.refs_0_), channel_id=1, source_target_pairs={{0,2},{1,3},{2,0},{3,1},{4,6},{5,7},{6,4},{7,5},{8,10},{9,11},{10,... | collective-permute-start | bytes 589832 | tf_op jit(solution)/shard_map/ppermute | solution.py:477
  161.6 19.2 %all-to-all-start.6 = ((bf16[8,40,768]{2,1,0:T(8,128)(2,1)}), bf16[8,40,768]{2,1,0:T(8,128)(2,1)S(1)}, u32[]{:S(2)}, u32[]{:S(2)}) async-start(bf16[8,40,768]{2,1,0:T(8,128)(2,1)} %bitcast.97), calls=%async_computation.6 | async-start | bytes 983040 | tf_op jit(solution)/shard_map/all_to_all | solution.py:568
  167.3 1.7 collective-permute-start.20
  167.3 1.7 collective-permute-start.21
  180.7 0.8 copy-start.1
  181.5 3.8 %copy-start.6 = (f32[1,128,768]{2,1,0:T(8,128)S(1)}, f32[1,128,768]{2,1,0:T(8,128)}, u32[]{:S(2)}) copy-start(f32[1,128,768]{2,1,0:T(8,128)} %param.15) | copy-start | bytes 1179652
  181.5 3.9 %copy-start.17 = (bf16[128,768]{1,0:T(8,128)(2,1)S(1)}, bf16[128,768]{1,0:T(8,128)(2,1)}, u32[]{:S(2)}) copy-start(bf16[128,768]{1,0:T(8,128)(2,1)} %get-tuple-element.80) | copy-start | bytes 589828
  181.5 4.2 %copy-start.16 = (bf16[128,768]{1,0:T(8,128)(2,1)S(1)}, bf16[128,768]{1,0:T(8,128)(2,1)}, u32[]{:S(2)}) copy-start(bf16[128,768]{1,0:T(8,128)(2,1)} %get-tuple-element.78) | copy-start | bytes 589828
  181.5 5.4 %copy-start.13 = (bf16[128,768]{1,0:T(8,128)(2,1)S(1)}, bf16[128,768]{1,0:T(8,128)(2,1)}, u32[]{:S(2)}) copy-start(bf16[128,768]{1,0:T(8,128)(2,1)} %get-tuple-element.79) | copy-start | bytes 589828
  181.5 12.5 %copy-start.8 = (bf16[128,768]{1,0:T(8,128)(2,1)S(1)}, bf16[128,768]{1,0:T(8,128)(2,1)}, u32[]{:S(2)}) copy-start(bf16[128,768]{1,0:T(8,128)(2,1)} %get-tuple-element.77) | copy-start | bytes 589828
  181.6 12.7 %copy-start.2 = (bf16[8,40,768]{2,1,0:T(8,128)(2,1)S(1)}, bf16[8,40,768]{2,1,0:T(8,128)(2,1)}, u32[]{:S(2)}) copy-start(bf16[8,40,768]{2,1,0:T(8,128)(2,1)} %copy-done.1) | copy-start | bytes 1474564
  181.6 36.7 %all-to-all-start.7 = ((bf16[8,96,896]{2,1,0:T(8,128)(2,1)}), bf16[8,96,896]{2,1,0:T(8,128)(2,1)S(1)}, u32[]{:S(2)}, u32[]{:S(2)}) async-start(bf16[8,96,896]{2,1,0:T(8,128)(2,1)} %bitcast.88), calls=%async_computation.7 | async-start | bytes 2752512 | tf_op jit(solution)/shard_map/all_to_all | solution.py:694
  185.5 1.5 collective-permute-start.23
  185.8 2.6 %collective-permute-start.22 = (bf16[128,768]{1,0:T(8,128)(2,1)S(1)}, bf16[128,768]{1,0:T(8,128)(2,1)S(1)}, u32[]{:S(2)}, u32[]{:S(2)}) collective-permute-start(bf16[128,768]{1,0:T(8,128)(2,1)S(1)} %copy-done.16), channel_id=1, source_target_pairs={{0,1},{1,0},{2,3},{3,2},{4,5},{5,4},{6,7},{7,6},{8,9},{9,8},{10,11... | collective-permute-start | bytes 589832 | tf_op jit(solution)/shard_map/ppermute | solution.py:484
  187.0 7.0 %collective-permute-start.24 = (bf16[128,768]{1,0:T(8,128)(2,1)S(1)}, bf16[128,768]{1,0:T(8,128)(2,1)S(1)}, u32[]{:S(2)}, u32[]{:S(2)}) collective-permute-start(bf16[128,768]{1,0:T(8,128)(2,1)S(1)} %add_convert_fusion.2), channel_id=1, source_target_pairs={{0,2},{1,3},{2,0},{3,1},{4,6},{5,7},{6,4},{7,5},{8,10},{9,11},{10,... | collective-permute-start | bytes 589832 | tf_op jit(solution)/shard_map/ppermute | solution.py:484
  194.0 30.4 %copy-start.11 = (f32[128,768]{1,0:T(8,128)S(1)}, f32[128,768]{1,0:T(8,128)}, u32[]{:S(2)}) copy-start(f32[128,768]{1,0:T(8,128)} %get-tuple-element.70) | copy-start | bytes 1179652
  219.9 3.8 %collective-permute-start.25 = (f32[48,36]{1,0:T(8,128)S(1)}, f32[48,36]{1,0:T(8,128)S(1)}, u32[]{:S(2)}, u32[]{:S(2)}) collective-permute-start(f32[48,36]{1,0:T(8,128)S(1)} %constant_dynamic-slice_fusion.1), channel_id=1, source_target_pairs={{0,2},{1,3},{2,0},{3,1},{4,6},{5,7},{6,4},{7,5},{8,10},{9,11},{10,... | collective-permute-start | bytes 20744 | tf_op jit(solution)/shard_map/ppermute | solution.py:715
  224.5 1.2 collective-permute-start.26
  225.7 0.7 copy-start.12
where the time goes:
time: 228 us; the launch traced here: 226 us
  waiting for transfers between devices  101 us (44%)
  Pallas kernels  57.8 us (25%)
  starting transfers between devices  50.4 us (22%)
  local copies, waits for them, and re-layouts  7.09 us (3%)
  other arithmetic  5.23 us (2%)
  matrix products  3.5 us (2%)
    pallas_call x8, Pallas kernels, call(): pl.pallas_call(inner, out_shape=outputs, in_specs=[WHOLE] * used + [pl.Bl...  28.2 us
    ppermute x4, waiting for transfers between devices, seq_gather(): far = lax.ppermute(block, 'seq', FAR)  27.7 us
    all_to_all x1, waiting for transfers between devices, body(): lax.all_to_all(grad_weights.reshape(fsdp_size, D // fsdp_size, 4 * head_c...  21.8 us
    ppermute x4, waiting for transfers between devices, seq_reduce(): lax.ppermute(pair, 'seq', FAR)  16.2 us
    pallas_call x2, Pallas kernels, expert_products(): pl.pallas_call(product_kernel, grid=(local_experts,), in_specs=[block(*le...  15 us
    pallas_call x1, Pallas kernels, experts(): pl.pallas_call(expert_kernel, grid=(local_experts,), in_specs=[pl.BlockSp...  14.7 us
    all_to_all x2, waiting for transfers between devices, to_experts(): lax.all_to_all(table, 'fsdp', split_axis=0, concat_axis=0, tiled=True)  14.1 us
    all_to_all x2, starting transfers between devices, from_experts(): lax.all_to_all(settled.reshape(fsdp_size, local_experts * CAP, D), 'fsdp'...  11.4 us
  transfers between devices with their start and end apart: 35, of which 20 were waited for; matrix products, arithmetic and copies ran while one was open for 6% of the time, Pallas kernels for 16%

commit v1 on v0

--- a/solution.py
+++ b/solution.py
@@ -64,21 +64,25 @@
 WHOLE = pl.BlockSpec(memory_space=pltpu.VMEM)
 
 
-def call(kernel, outputs, operands, after=(), fresh=(), scratch=(), flops=0, mib=20):
-    moved = sum(v.size * v.dtype.itemsize for v in operands)
+def call(kernel, outputs, operands, after=(), fresh=(), scalars=(), scratch=(), flops=0, mib=20, light=False):
+    moved = 0 if light else sum(v.size * v.dtype.itemsize for v in operands)
     used = len(operands)
 
     def inner(*refs):
         kernel(*refs[:used], *refs[used + len(after) :])
 
     operands = [
-        operand if index in fresh else in_hbm([operand])[0]
+        operand if index in fresh or index in scalars else in_hbm([operand])[0]
         for index, operand in enumerate(operands)
     ] + in_hbm(after)
     return pl.pallas_call(
         inner,
         out_shape=outputs,
-        in_specs=[WHOLE] * used + [pl.BlockSpec(memory_space=pl.ANY)] * len(after),
+        in_specs=[
+            pl.BlockSpec(memory_space=pltpu.SMEM) if index in scalars else WHOLE
+            for index in range(used)
+        ]
+        + [pl.BlockSpec(memory_space=pl.ANY)] * len(after),
         out_specs=[WHOLE] * len(outputs),
         scratch_shapes=scratch,
         cost_estimate=pl.CostEstimate(flops=flops, bytes_accessed=moved, transcendentals=0),
@@ -105,22 +109,32 @@
     )(*in_hbm([array]), other)
 
 
+def first_norm_kernel(tokens, normed_ref):
+    normed_ref[...] = norm_forward(tokens[...])[0].astype(jnp.bfloat16)
+
+
 def attend_kernel(
-    own, far, near, diag, held, normed_ref, normed_in_ref, qkv_ref, mixed_ref, logsum_ref, vec_ref
+    own, far, near, diag, held_own, held_other, parity,
+    normed_ref, normed_in_ref, qkv_ref, mixed_ref, logsum_ref, vec_ref, held_ref
 ):
     bf16 = jnp.bfloat16
     f32 = jnp.float32
     columns = qkv_ref.shape[1]
-    lanes = held.shape[1]
+    outer, _, rows, lanes = held_ref.shape
+    bit = parity[0]
+    for place in range(outer):
+        held_ref[place, bit] = held_own[place]
+        held_ref[place, 1 - bit] = held_other[place]
+    held = held_ref[...].reshape(outer * 2 * rows, lanes)
     wanted = lax.broadcasted_iota(jnp.int32, (8, lanes), 0) + (columns + EXPERTS)
     picker = (lax.broadcasted_iota(jnp.int32, (8, lanes), 1) == wanted).astype(bf16)
-    vectors = matmul_t(picker, held[...])
+    vectors = matmul_t(picker, held)
     vec_ref[...] = vectors
     count = own.shape[0]
     for index, block in enumerate((own, far, near, diag)):
-        normed, _ = norm_forward(block[...])
+        normed = block[...].astype(f32)
         rows = pl.ds(index * count, count)
-        normed_ref[rows, :] = normed
+        normed_ref[rows, :] = block[...]
         normed_in_ref[rows, :] = (normed * vectors[0:1] + vectors[1:2]).astype(bf16)
     qkv_ref[...] = matmul(normed_in_ref[...], held[:, :columns]).astype(bf16)
     width = columns // 3
@@ -192,7 +206,7 @@
         block[...] = grad_normed[index * count : (index + 1) * count].astype(bf16)
     dw_ref[:, :columns] = t_matmul(normed_in[...], gqkv_ref[...]).astype(bf16)
     dw_ref[:, columns : columns + width] = t_matmul(gr_ref[...], mixed[...]).astype(bf16)
-    gain_row = jnp.sum(grad_normed * normed[...], 0, keepdims=True)
+    gain_row = jnp.sum(grad_normed * normed[...].astype(f32), 0, keepdims=True)
     bias_row = jnp.sum(grad_normed, 0, keepdims=True)
     row = lax.broadcasted_iota(jnp.int32, (8, gain_row.shape[1]), 0)
     both = jnp.where(row == 0, gain_row, jnp.where(row == 1, bias_row, 0.0))
@@ -525,14 +539,36 @@
     w_out_rows = jnp.broadcast_to(w_out_rows, (fsdp_size, shard, D))
     w_out_rows = lax.all_to_all(w_out_rows, "fsdp", split_axis=0, concat_axis=0, tiled=True)
     w_out_rows = w_out_rows.reshape(head_cols, D)
+    lanes = 3 * head_cols + EXPERTS + 4
+    outer = fsdp_size // 2
+    parity = lax.axis_index("fsdp") % 2
     sent = call(
         weight_blocks_kernel,
-        [shaped(bf16, fsdp_size, seq_size, shard, 3 * head_cols + EXPERTS + 4)],
+        [shaped(bf16, outer, seq_size, shard, lanes)],
         [w_query, w_key, w_value, w_router]
         + [v.reshape(1, shard) for v in (ln1_gain, ln1_bias, ln2_gain, ln2_bias)],
-    )[0].reshape(devices, shard, -1)
-    held = lax.all_to_all(sent, ("fsdp", "seq"), split_axis=0, concat_axis=0, tiled=True)
-    held = held.reshape(D, -1)
+    )[0].reshape(devices // 2, shard, -1)
+    groups = [
+        [(2 * place + bit) * seq_size + part for place in range(outer) for part in range(seq_size)]
+        for bit in range(2)
+    ]
+    held_own = lax.all_to_all(
+        sent,
+        ("fsdp", "seq"),
+        split_axis=0,
+        concat_axis=0,
+        axis_index_groups=groups,
+        tiled=True,
+    )
+    image_rows = seq_size * shard
+    held_own = held_own.reshape(outer, image_rows, lanes)
+    held_other = lax.ppermute(held_own, "fsdp", [(i, i ^ 1) for i in range(fsdp_size)])
+    if image_rows % 16:
+        pairs = jnp.stack([held_own, held_other], 1)
+        pairs = jnp.where(parity == 0, pairs, pairs[:, ::-1]).reshape(2, 1, D // 2, lanes)
+        held_own, held_other = pairs[0], pairs[1]
+        parity = jnp.zeros((), jnp.int32)
+    parity = parity.astype(jnp.int32).reshape(1)
 
     hot = (chosen.reshape(-1)[:, None] == jnp.arange(EXPERTS)[None, :]).astype(bf16)
     routes = token_count * TOP
@@ -574,23 +610,29 @@
         )
         return returned.reshape(table_rows, D)
 
+    normed_blocks = seq_gather(
+        call(first_norm_kernel, [shaped(bf16, token_count, D)], [tokens_in])[0]
+    )
     image = token_count * seq_size
     columns = 3 * head_cols
-    router = held[:, columns : columns + EXPERTS]
-    normed_one, normed_in, qkv, head_mixed, logsum, vectors = call(
+    normed_one, normed_in, qkv, head_mixed, logsum, vectors, held = call(
         attend_kernel,
         [
-            shaped(f32, image, D),
+            shaped(bf16, image, D),
             shaped(bf16, image, D),
             shaped(bf16, image, columns),
             shaped(bf16, image, head_cols),
             shaped(f32, image, 8),
             shaped(f32, 8, D),
+            shaped(bf16, held_own.shape[0], 2, *held_own.shape[1:]),
         ],
-        [*seq_gather(tokens_in), held],
-        fresh=(1, 2, 3, 4),
-        flops=2 * image * D * columns + 4 * image * image * head_cols,
-    )
+        [*normed_blocks, held_own, held_other, parity],
+        fresh=(1, 2, 3, 4, 5),
+        scalars=(6,),
+        flops=6 * (2 * image * D * columns + 4 * image * image * head_cols),
+    )
+    held = held.reshape(D, lanes)
+    router = held[:, columns : columns + EXPERTS]
     out_partial = matmul(head_mixed, w_out_rows).astype(bf16)
     out_blocks = [out_partial[i * token_count : (i + 1) * token_count] for i in range(seq_size)]
 
@@ -604,6 +646,7 @@
         ],
         [tokens_in, *seq_reduce(*out_blocks), vectors, router, position],
         fresh=(1, 2, 3, 6),
+        light=True,
     )
     spots = jnp.arange(table_rows)[None, None, :] - position[:, :, None]
     hits = (spots == 0) if copies == 1 else ((spots == 0) | (spots == CAP))

time: 228 us -> 222 us (0.974)
  waiting for transfers between devices: 101 us -> 85 us
  starting transfers between devices: 50.4 us -> 59.2 us
    ppermute x4, waiting for transfers between devices: 27.7 us -> 9.43 us  [seq_gather(): far = lax.ppermute(block, 'seq', FAR)]
    ppermute x0 -> x1, waiting for transfers between devices: none -> 7.74 us  [body(): lax.ppermute(held_own, 'fsdp', [(i, i ^ 1) for i in range(fsdp_size)])]
    all_to_all x1, waiting for transfers between devices: 4.66 us -> 0.01 us  [body(): lax.all_to_all(w_out_rows, 'fsdp', split_axis=0, concat_axis=0, tiled=True)]
    all_to_all x1, waiting for transfers between devices: 5.84 us -> 9.06 us  [body(): lax.all_to_all(sent, ('fsdp', 'seq'), split_axis=0, concat_axis=0, axis_i...]
    ppermute x4, starting transfers between devices: 2.86 us -> 5.75 us  [seq_reduce(): lax.ppermute(pair, 'seq', FAR)]
    ppermute x4, starting transfers between devices: 4.12 us -> 6.86 us  [seq_gather(): far = lax.ppermute(block, 'seq', FAR)]
    ppermute x4, waiting for transfers between devices: 16.2 us -> 13.7 us  [seq_reduce(): lax.ppermute(pair, 'seq', FAR)]
    pallas_call x8 -> x9, Pallas kernels: 28.2 us -> 29.2 us  [call(): pl.pallas_call(inner, out_shape=outputs, in_specs=[pl.BlockSpec(memory_sp...]
  transfers between devices with their start and end apart: 35 -> 36, of which waited for: 20 -> 20; matrix products, arithmetic and copies ran while one was open for 6% -> 6% of each run, Pallas kernels for 16% -> 17%
where the time goes in v1:
time: 222 us; the launch traced here: 221 us
  waiting for transfers between devices  85 us (38%)
  starting transfers between devices  59.2 us (27%)
  Pallas kernels  58.8 us (26%)
  local copies, waits for them, and re-layouts  7.95 us (4%)
  other arithmetic  5.22 us (2%)
  matrix products  3.49 us (2%)
    pallas_call x9, Pallas kernels, call(): pl.pallas_call(inner, out_shape=outputs, in_specs=[pl.BlockSpec(memory_sp...  29.2 us
    all_to_all x1, waiting for transfers between devices, body(): lax.all_to_all(grad_weights.reshape(fsdp_size, D // fsdp_size, 4 * head_c...  21.5 us
    pallas_call x2, Pallas kernels, expert_products(): pl.pallas_call(product_kernel, grid=(local_experts,), in_specs=[block(*le...  15 us
    pallas_call x1, Pallas kernels, experts(): pl.pallas_call(expert_kernel, grid=(local_experts,), in_specs=[pl.BlockSp...  14.7 us
    ppermute x4, waiting for transfers between devices, seq_reduce(): lax.ppermute(pair, 'seq', FAR)  13.7 us
    all_to_all x2, waiting for transfers between devices, to_experts(): lax.all_to_all(table, 'fsdp', split_axis=0, concat_axis=0, tiled=True)  12 us
    all_to_all x2, starting transfers between devices, from_experts(): lax.all_to_all(settled.reshape(fsdp_size, local_experts * CAP, D), 'fsdp'...  11.4 us
    all_to_all x2, starting transfers between devices, to_experts(): lax.all_to_all(table, 'fsdp', split_axis=0, concat_axis=0, tiled=True)  9.84 us
  transfers between devices with their start and end apart: 36, of which 20 were waited for; matrix products, arithmetic and copies ran while one was open for 6% of the time, Pallas kernels for 17%

profile of v1, /device:TPU:0, one launch (start us, length us, event | category | flops | bytes accessed | tf_op | source)
XLA Modules:
  0.0 220.7 jit_solution(7791237122416466258)
XLA Ops:
  0.7 1.9 shard_map.247
  2.6 7.4 %all-to-all-start = ((bf16[16,24,612]{2,1,0:T(8,128)(2,1)}), bf16[16,24,612]{2,1,0:T(8,128)(2,1)S(1)}, u32[]{:S(2)}, u32[]{:S(2)}) async-start(bf16[16,24,612]{2,1,0:T(8,128)(2,1)} %bitcast.90), calls=%async_computation | async-start | bytes 983040 | tf_op jit(solution)/shard_map/all_to_all | solution.py:555
  10.0 1.9 shard_map.246.refs_0_
  11.9 1.9 collective-permute-start
  13.8 0.7 collective-permute-start.4
  15.1 9.1 %all-to-all-done = bf16[16,24,612]{2,1,0:T(8,128)(2,1)S(1)} async-done(((bf16[16,24,612]{2,1,0:T(8,128)(2,1)}), bf16[16,24,612]{2,1,0:T(8,128)(2,1)S(1)}, u32[]{:S(2)}, u32[]{:S(2)}) %all-to-all-start) | async-done | bytes 470048 | tf_op jit(solution)/shard_map/all_to_all | solution.py:555
  24.2 1.1 collective-permute-start.3
  25.5 0.7 broadcast_in_dim.20
  26.2 4.7 %all-to-all-start.1 = ((bf16[8,24,768]{2,1,0:T(8,128)(2,1)}), bf16[8,24,768]{2,1,0:T(8,128)(2,1)S(1)}, u32[]{:S(2)}, u32[]{:S(2)}) async-start(bf16[8,24,768]{2,1,0:T(8,128)(2,1)} %broadcast_in_dim.20), calls=%async_computation.1 | async-start | bytes 589824 | tf_op jit(solution)/shard_map/all_to_all | solution.py:540
  31.1 1.1 fusion.27
  32.4 7.7 %collective-permute-done.3.refs_5_ = bf16[4,96,612]{2,1,0:T(8,128)(2,1)S(1)} collective-permute-done((bf16[4,96,612]{2,1,0:T(8,128)(2,1)S(1)}, bf16[4,96,612]{2,1,0:T(8,128)(2,1)S(1)}, u32[]{:S(2)}, u32[]{:S(2)}) %collective-permute-start.3) | collective-permute-done | bytes 470048 | tf_op jit(solution)/shard_map/ppermute | solution.py:565
  40.1 4.3 %shard_map.248 = (bf16[512,768]{1,0:T(8,128)(2,1)}, bf16[512,768]{1,0:T(8,128)(2,1)}, bf16[512,576]{1,0:T(8,128)(2,1)}, bf16[512,192]{1,0:T(8,128)(2,1)}, f32[51...) custom-call(bf16[128,768]{1,0:T(8,128)(2,1)} %shard_map.246.refs_0_, ...), custom_call_target="tpu_custom_call" | custom-call | flops 3925868544 | bytes 1726468 | tf_op jit(solution)/shard_map/pallas_call | solution.py:78
  44.5 4.5 %all-to-all-start.3 = ((bf16[8,40,768]{2,1,0:T(8,128)(2,1)}), bf16[8,40,768]{2,1,0:T(8,128)(2,1)S(1)}, u32[]{:S(2)}, u32[]{:S(2)}) async-start(bf16[8,40,768]{2,1,0:T(8,128)(2,1)} %bitcast.17), calls=%async_computation.3 | async-start | bytes 983040 | tf_op jit(solution)/shard_map/all_to_all | solution.py:588
  49.0 1.3 convolution_convert_fusion
  50.9 0.9 collective-permute-done.6
  51.9 2.0 collective-permute-start.7
  53.8 1.7 slice.56.refs_5_.router.refs_3_
  55.6 3.5 %collective-permute-done.7.refs_3_ = bf16[128,768]{1,0:T(8,128)(2,1)S(1)} collective-permute-done((bf16[128,768]{1,0:T(8,128)(2,1)S(1)}, bf16[128,768]{1,0:T(8,128)(2,1)S(1)}, u32[]{:S(2)}, u32[]{:S(2)}) %collective-permute-start.7) | collective-permute-done | bytes 196640 | tf_op jit(solution)/shard_map/ppermute | solution.py:498
  59.1 2.5 %shard_map.249 = (f32[128,768]{1,0:T(8,128)}, bf16[128,768]{1,0:T(8,128)(2,1)}, f32[128,32]{1,0:T(8,128)}, bf16[320,768]{1,0:T(8,128)(2,1)}) custom-call(f32[128,768]{1,0:T(8,128)} %bitcast.86, bf16[128,768]{1,0:T(8,128)(2,1)S(1)} %get-tuple-element.97.refs_1_, bf16[128,768]{1,0:T(8,128)(2,1)S(1)} %collective-permute-done.5.refs_2_, ...), custom_call_target="tpu_custom_call" | custom-call | tf_op jit(solution)/shard_map/pallas_call | solution.py:78
  61.6 0.8 all-to-all-done.3
  62.4 5.3 %all-to-all-start.2 = ((bf16[8,40,768]{2,1,0:T(8,128)(2,1)}), bf16[8,40,768]{2,1,0:T(8,128)(2,1)S(1)}, u32[]{:S(2)}, u32[]{:S(2)}) async-start(bf16[8,40,768]{2,1,0:T(8,128)(2,1)} %bitcast.97), calls=%async_computation.2 | async-start | bytes 983040 | tf_op jit(solution)/shard_map/all_to_all | solution.py:588
  68.2 1.8 collective-permute-start.11
  70.0 11.2 %all-to-all-done.2 = bf16[8,40,768]{2,1,0:T(8,128)(2,1)S(1)} async-done(((bf16[8,40,768]{2,1,0:T(8,128)(2,1)}), bf16[8,40,768]{2,1,0:T(8,128)(2,1)S(1)}, u32[]{:S(2)}, u32[]{:S(2)}) %all-to-all-start.2) | async-done | bytes 491552 | tf_op jit(solution)/shard_map/all_to_all | solution.py:588
  81.7 1.6 collective-permute-start.8
  83.3 0.5 collective-permute-start.13
  83.8 9.4 %collective-permute-done.8.x_far = bf16[4,80,768]{2,1,0:T(8,128)(2,1)S(1)} collective-permute-done((bf16[4,80,768]{2,1,0:T(8,128)(2,1)S(1)}, bf16[4,80,768]{2,1,0:T(8,128)(2,1)S(1)}, u32[]{:S(2)}, u32[]{:S(2)}) %collective-permute-start.8) | collective-permute-done | bytes 491552 | tf_op jit(solution)/shard_map/ppermute | solution.py:491
  93.3 0.6 gather_fusion
  94.0 1.2 collective-permute-done.10.x_diag
  95.2 14.7 %shard_map.250 = (bf16[4,80,768]{2,1,0:T(8,128)(2,1)}, bf16[4,80,768]{2,1,0:T(8,128)(2,1)}, bf16[4,80,768]{2,1,0:T(8,128)(2,1)}, bf16[4,80,768]{2,1,0:T(8,128)(2...) custom-call(s32[1]{0:T(128)} %bitcast.13.first, ...), custom_call_target="tpu_custom_call" | custom-call | flops 6039797760 | bytes 21233664 | tf_op jit(solution)/shard_map/pallas_call | solution.py:381
  110.2 0.8 fusion.1.refs_3_.refs_13_
  111.5 0.6 collective-permute-done.15
  112.1 1.1 add_convert_fusion.1
  113.2 1.6 collective-permute-start.16
  115.3 0.6 gather_fusion.1
  116.0 0.7 broadcast_select_fusion
  116.6 4.0 %all-to-all-start.4 = ((f32[32,1,40]{2,1,0:T(1,128)}), f32[32,1,40]{2,1,0:T(1,128)S(1)}, u32[]{:S(2)}, u32[]{:S(2)}) async-start(f32[32,1,40]{2,1,0:T(1,128)} %bitcast.24), calls=%async_computation.4 | async-start | bytes 32768 | tf_op jit(solution)/shard_map/all_to_all | solution.py:674
  120.7 7.6 %shard_map.251.refs_4_ = f32[8,768,384]{2,1,0:T(8,128)} custom-call(bf16[4,320,768]{2,1,0:T(8,128)(2,1)} %get-tuple-element.63.left, bf16[8,320,384]{2,1,0:T(8,128)(2,1)} %get-tuple-element.64.right), custom_call_target="tpu_custom_call" | custom-call | flops 1509949440 | bytes 13369344 | tf_op jit(solution)/shard_map/pallas_call | solution.py:423
  128.3 2.4 %shard_map.252 = bf16[320,768]{1,0:T(8,128)(2,1)} custom-call(bf16[320,768]{1,0:T(8,128)(2,1)} %bitcast.95, bf16[320,768]{1,0:T(8,128)(2,1)S(1)} %bitcast.81, bf16[320,768]{1,0:T(8,128)(2,1)S(1)} %bitcast.83, bf16[320,320]{1,0:T(8,128)(2,1)} %fusion.1.refs_3_.refs_13_, f32[8,768,384]{2,1,0:T(8,128)} %shard_map.251.refs_4_), custom_call_target="tpu_custom_call" | custom-call | flops 157286400 | bytes 1679360 | tf_op jit(solution)/shard_map/pallas_call | solution.py:78
  130.8 5.6 %all-to-all-start.5 = ((bf16[8,40,768]{2,1,0:T(8,128)(2,1)}), bf16[8,40,768]{2,1,0:T(8,128)(2,1)S(1)}, u32[]{:S(2)}, u32[]{:S(2)}) async-start(bf16[8,40,768]{2,1,0:T(8,128)(2,1)} %bitcast.89), calls=%async_computation.5 | async-start | bytes 983040 | tf_op jit(solution)/shard_map/all_to_all | solution.py:604
  136.6 1.6 collective-permute-start.19
  138.2 7.4 %shard_map.253.refs_14_ = f32[8,384,768]{2,1,0:T(8,128)} custom-call(bf16[8,320,384]{2,1,0:T(8,128)(2,1)} %get-tuple-element.69.left, bf16[4,320,768]{2,1,0:T(8,128)(2,1)} %get-tuple-element.70.right), custom_call_target="tpu_custom_call" | custom-call | flops 1509949440 | bytes 13369344 | tf_op jit(solution)/shard_map/pallas_call | solution.py:423
  145.7 4.6 %collective-permute-done.19 = bf16[4,80,768]{2,1,0:T(8,128)(2,1)S(1)} collective-permute-done((bf16[4,80,768]{2,1,0:T(8,128)(2,1)S(1)}, bf16[4,80,768]{2,1,0:T(8,128)(2,1)S(1)}, u32[]{:S(2)}, u32[]{:S(2)}) %collective-permute-start.19) | collective-permute-done | bytes 491552 | tf_op jit(solution)/shard_map/ppermute | solution.py:498
  150.5 4.1 %shard_map.254 = (f32[128,768]{1,0:T(8,128)}, bf16[128,768]{1,0:T(8,128)(2,1)}, f32[768,36]{1,0:T(8,128)}, bf16[320,768]{1,0:T(8,128)(2,1)}) custom-call(f32[128,768]{1,0:T(8,128)} %get-tuple-element.54.refs_0_, f32[128,768]{1,0:T(8,128)} %bitcast.92, f32[8,768]{1,0:T(8,128)} %get-tuple-element.52.refs_4_.refs_2_, ...), custom_call_target="tpu_custom_call" | custom-call | bytes 3247360 | tf_op jit(solution)/shard_map/pallas_call | solution.py:78
  154.6 1.5 collective-permute-start.20
  156.1 5.7 %all-to-all-start.6 = ((bf16[8,40,768]{2,1,0:T(8,128)(2,1)}), bf16[8,40,768]{2,1,0:T(8,128)(2,1)S(1)}, u32[]{:S(2)}, u32[]{:S(2)}) async-start(bf16[8,40,768]{2,1,0:T(8,128)(2,1)} %bitcast.96), calls=%async_computation.6 | async-start | bytes 983040 | tf_op jit(solution)/shard_map/all_to_all | solution.py:604
  162.4 1.1 collective-permute-done.21.refs_2_
  163.6 8.8 %shard_map.256 = (bf16[128,768]{1,0:T(8,128)(2,1)}, bf16[128,768]{1,0:T(8,128)(2,1)}, bf16[128,768]{1,0:T(8,128)(2,1)}, bf16[128,768]{1,0:T(8,128)(2,1)}, bf16[768,896]{1,0:T(8,128)(2,1)}) custom-call(bf16[128,768]{1,0:T(8,128)(2,1)} %get-tuple-element.73.refs_0_, bf16[128,768]{1,0:T(8,128)(2,1)S(1)} %collective-permute-done.20.refs_1_, ...), custom_call_target="tpu_custom_call" | custom-call | flops 6845104128 | bytes 4507648 | tf_op jit(solution)/shard_map/pallas_call | solution.py:78
  172.4 2.9 %all-to-all-done.6 = bf16[8,40,768]{2,1,0:T(8,128)(2,1)S(1)} async-done(((bf16[8,40,768]{2,1,0:T(8,128)(2,1)}), bf16[8,40,768]{2,1,0:T(8,128)(2,1)S(1)}, u32[]{:S(2)}, u32[]{:S(2)}) %all-to-all-start.6) | async-done | bytes 491552 | tf_op jit(solution)/shard_map/all_to_all | solution.py:604
  175.3 0.8 copy-done
  176.1 3.8 %all-to-all-start.7 = ((bf16[8,96,896]{2,1,0:T(8,128)(2,1)}), bf16[8,96,896]{2,1,0:T(8,128)(2,1)S(1)}, u32[]{:S(2)}, u32[]{:S(2)}) async-start(bf16[8,96,896]{2,1,0:T(8,128)(2,1)} %bitcast.87), calls=%async_computation.7 | async-start | bytes 2752512 | tf_op jit(solution)/shard_map/all_to_all | solution.py:737
  180.3 0.6 collective-permute-start.23
  180.9 0.7 collective-permute-done.24
  181.6 0.6 collective-permute-start.25
  182.2 0.8 slice_reduce_fusion.5
  183.0 5.6 %collective-permute-done.25 = bf16[128,768]{1,0:T(8,128)(2,1)S(1)} collective-permute-done((bf16[128,768]{1,0:T(8,128)(2,1)S(1)}, bf16[128,768]{1,0:T(8,128)(2,1)S(1)}, u32[]{:S(2)}, u32[]{:S(2)}) %collective-permute-start.25) | collective-permute-done | bytes 196640 | tf_op jit(solution)/shard_map/ppermute | solution.py:498
  188.8 2.2 shard_map.255.refs_1_
  191.0 21.5 %all-to-all-done.7.refs_0_ = bf16[8,96,896]{2,1,0:T(8,128)(2,1)S(1)} async-done(((bf16[8,96,896]{2,1,0:T(8,128)(2,1)}), bf16[8,96,896]{2,1,0:T(8,128)(2,1)S(1)}, u32[]{:S(2)}, u32[]{:S(2)}) %all-to-all-start.7) | async-done | bytes 1376288 | tf_op jit(solution)/shard_map/all_to_all | solution.py:737
  212.6 0.9 shard_map.258
  213.5 0.7 constant_dynamic-slice_fusion.1
  214.2 0.5 collective-permute-start.26
  214.8 3.3 %collective-permute-done.26 = f32[48,36]{1,0:T(8,128)S(1)} collective-permute-done((f32[48,36]{1,0:T(8,128)S(1)}, f32[48,36]{1,0:T(8,128)S(1)}, u32[]{:S(2)}, u32[]{:S(2)}) %collective-permute-start.26) | collective-permute-done | bytes 6944 | tf_op jit(solution)/shard_map/ppermute | solution.py:758
  218.1 0.7 dynamic-slice_add_fusion
  218.8 0.9 add_bitcast_fusion
  220.0 0.7 slice_reduce_fusion.1
  (105 shorter events, 6.2 us)
Async XLA Ops:
  0.7 13.2 %copy-start.16 = (bf16[24,768]{1,0:T(8,128)(2,1)S(1)}, bf16[24,768]{1,0:T(8,128)(2,1)}, u32[]{:S(2)}) copy-start(bf16[24,768]{1,0:T(8,128)(2,1)} %param.22) | copy-start | bytes 110596
  0.7 13.8 %copy-start.12 = (s32[1,128,2]{1,2,0:T(2,128)S(1)}, s32[1,128,2]{1,2,0:T(2,128)}, u32[]{:S(2)}) copy-start(s32[1,128,2]{1,2,0:T(2,128)} %param.16) | copy-start | bytes 3076
  0.7 30.4 %copy-start.5 = (f32[1,128,768]{2,1,0:T(8,128)S(1)}, f32[1,128,768]{2,1,0:T(8,128)}, u32[]{:S(2)}) copy-start(f32[1,128,768]{2,1,0:T(8,128)} %param.28) | copy-start | bytes 1179652
  2.6 21.6 %all-to-all-start = ((bf16[16,24,612]{2,1,0:T(8,128)(2,1)}), bf16[16,24,612]{2,1,0:T(8,128)(2,1)S(1)}, u32[]{:S(2)}, u32[]{:S(2)}) async-start(bf16[16,24,612]{2,1,0:T(8,128)(2,1)} %bitcast.90), calls=%async_computation | async-start | bytes 983040 | tf_op jit(solution)/shard_map/all_to_all | solution.py:555
  11.9 19.0 %collective-permute-start = (bf16[128,768]{1,0:T(8,128)(2,1)}, bf16[128,768]{1,0:T(8,128)(2,1)S(1)}, u32[]{:S(2)}, u32[]{:S(2)}) collective-permute-start(bf16[128,768]{1,0:T(8,128)(2,1)} %shard_map.246.refs_0_), channel_id=1, source_target_pairs={{0,2},{1,3},{2,0},{3,1},{4,6},{5,7},{6,4},{7,5},{8,10},{9,11},{10,... | collective-permute-start | bytes 589832 | tf_op jit(solution)/shard_map/ppermute | solution.py:491
  13.8 18.3 %collective-permute-start.1 = (bf16[128,768]{1,0:T(8,128)(2,1)}, bf16[128,768]{1,0:T(8,128)(2,1)S(1)}, u32[]{:S(2)}, u32[]{:S(2)}) collective-permute-start(bf16[128,768]{1,0:T(8,128)(2,1)} %shard_map.246.refs_0_), channel_id=1, source_target_pairs={{0,1},{1,0},{2,3},{3,2},{4,5},{5,4},{6,7},{7,6},{8,9},{9,8},{10,11... | collective-permute-start | bytes 589832 | tf_op jit(solution)/shard_map/ppermute | solution.py:492
  13.8 11.6 %collective-permute-start.4 = (bf16[24,768]{1,0:T(8,128)(2,1)S(1)}, bf16[24,768]{1,0:T(8,128)(2,1)S(1)}, u32[]{:S(2)}, u32[]{:S(2)}) collective-permute-start(bf16[24,768]{1,0:T(8,128)(2,1)S(1)} %copy-done.16), channel_id=1, source_target_pairs={{0,0},{1,4},{2,8},{3,12},{4,16},{5,20},{6,24},{7,28},{8,1},{9,5},{... | collective-permute-start | bytes 110600 | tf_op jit(solution)/shard_map/ppermute | solution.py:538
  24.2 15.9 %collective-permute-start.3 = (bf16[4,96,612]{2,1,0:T(8,128)(2,1)S(1)}, bf16[4,96,612]{2,1,0:T(8,128)(2,1)S(1)}, u32[]{:S(2)}, u32[]{:S(2)}) collective-permute-start(bf16[4,96,612]{2,1,0:T(8,128)(2,1)S(1)} %bitcast.76), channel_id=1, source_target_pairs={{0,4},{4,0},{8,12},{12,8},{16,20},{20,16},{24,28},{28,24},{1,5},{5... | collective-permute-start | bytes 1410056 | tf_op jit(solution)/shard_map/ppermute | solution.py:565
  26.2 18.3 %all-to-all-start.1 = ((bf16[8,24,768]{2,1,0:T(8,128)(2,1)}), bf16[8,24,768]{2,1,0:T(8,128)(2,1)S(1)}, u32[]{:S(2)}, u32[]{:S(2)}) async-start(bf16[8,24,768]{2,1,0:T(8,128)(2,1)} %broadcast_in_dim.20), calls=%async_computation.1 | async-start | bytes 589824 | tf_op jit(solution)/shard_map/all_to_all | solution.py:540
  30.9 1.5 collective-permute-start.2
  44.5 17.9 %all-to-all-start.3 = ((bf16[8,40,768]{2,1,0:T(8,128)(2,1)}), bf16[8,40,768]{2,1,0:T(8,128)(2,1)S(1)}, u32[]{:S(2)}, u32[]{:S(2)}) async-start(bf16[8,40,768]{2,1,0:T(8,128)(2,1)} %bitcast.17), calls=%async_computation.3 | async-start | bytes 983040 | tf_op jit(solution)/shard_map/all_to_all | solution.py:588
  50.3 1.5 collective-permute-start.6
  50.4 5.2 %collective-permute-start.5 = (bf16[128,768]{1,0:T(8,128)(2,1)S(1)}, bf16[128,768]{1,0:T(8,128)(2,1)S(1)}, u32[]{:S(2)}, u32[]{:S(2)}) collective-permute-start(bf16[128,768]{1,0:T(8,128)(2,1)S(1)} %get-tuple-element.96), channel_id=1, source_target_pairs={{0,1},{1,0},{2,3},{3,2},{4,5},{5,4},{6,7},{7,6},{8,9},{9,8},{10,11... | collective-permute-start | bytes 589832 | tf_op jit(solution)/shard_map/ppermute | solution.py:498
  51.9 7.2 %collective-permute-start.7 = (bf16[128,768]{1,0:T(8,128)(2,1)S(1)}, bf16[128,768]{1,0:T(8,128)(2,1)S(1)}, u32[]{:S(2)}, u32[]{:S(2)}) collective-permute-start(bf16[128,768]{1,0:T(8,128)(2,1)S(1)} %add_convert_fusion.3), channel_id=1, source_target_pairs={{0,2},{1,3},{2,0},{3,1},{4,6},{5,7},{6,4},{7,5},{8,10},{9,11},{10,... | collective-permute-start | bytes 589832 | tf_op jit(solution)/shard_map/ppermute | solution.py:498
  59.1 34.2 %copy-start.3 = (s32[4]{0:T(128)S(1)}, s32[4]{0:T(128)}, u32[]{:S(2)}) copy-start(s32[4]{0:T(128)} %constant.134.clone) | copy-start | bytes 52
  61.6 33.7 %copy-start.2 = (bf16[768,32]{1,0:T(8,128)(2,1)S(1)}, bf16[768,32]{1,0:T(8,128)(2,1)}, u32[]{:S(2)}) copy-start(bf16[768,32]{1,0:T(8,128)(2,1)} %slice.56.refs_5_.router.refs_3_) | copy-start | bytes 147460
  62.4 18.8 %all-to-all-start.2 = ((bf16[8,40,768]{2,1,0:T(8,128)(2,1)}), bf16[8,40,768]{2,1,0:T(8,128)(2,1)S(1)}, u32[]{:S(2)}, u32[]{:S(2)}) async-start(bf16[8,40,768]{2,1,0:T(8,128)(2,1)} %bitcast.97), calls=%async_computation.2 | async-start | bytes 983040 | tf_op jit(solution)/shard_map/all_to_all | solution.py:588
  68.2 15.1 %collective-permute-start.11 = (bf16[4,80,768]{2,1,0:T(8,128)(2,1)S(1)}, bf16[4,80,768]{2,1,0:T(8,128)(2,1)S(1)}, u32[]{:S(2)}, u32[]{:S(2)}) collective-permute-start(bf16[4,80,768]{2,1,0:T(8,128)(2,1)S(1)} %bitcast.73), channel_id=1, source_target_pairs={{0,2},{1,3},{2,0},{3,1},{4,6},{5,7},{6,4},{7,5},{8,10},{9,11},{10,... | collective-permute-start | bytes 1474568 | tf_op jit(solution)/shard_map/ppermute | solution.py:491
  81.7 11.6 %collective-permute-start.8 = (bf16[4,80,768]{2,1,0:T(8,128)(2,1)S(1)}, bf16[4,80,768]{2,1,0:T(8,128)(2,1)S(1)}, u32[]{:S(2)}, u32[]{:S(2)}) collective-permute-start(bf16[4,80,768]{2,1,0:T(8,128)(2,1)S(1)} %bitcast.78), channel_id=1, source_target_pairs={{0,2},{1,3},{2,0},{3,1},{4,6},{5,7},{6,4},{7,5},{8,10},{9,11},{10,... | collective-permute-start | bytes 1474568 | tf_op jit(solution)/shard_map/ppermute | solution.py:491
  83.3 10.7 %collective-permute-start.12 = (bf16[4,80,768]{2,1,0:T(8,128)(2,1)S(1)}, bf16[4,80,768]{2,1,0:T(8,128)(2,1)S(1)}, u32[]{:S(2)}, u32[]{:S(2)}) collective-permute-start(bf16[4,80,768]{2,1,0:T(8,128)(2,1)S(1)} %bitcast.74), channel_id=1, source_target_pairs={{0,1},{1,0},{2,3},{3,2},{4,5},{5,4},{6,7},{7,6},{8,9},{9,8},{10,11... | collective-permute-start | bytes 1474568 | tf_op jit(solution)/shard_map/ppermute | solution.py:492
  83.3 10.7 %collective-permute-start.13 = (bf16[4,80,768]{2,1,0:T(8,128)(2,1)S(1)}, bf16[4,80,768]{2,1,0:T(8,128)(2,1)}, u32[]{:S(2)}, u32[]{:S(2)}) collective-permute-start(bf16[4,80,768]{2,1,0:T(8,128)(2,1)S(1)} %collective-permute-done.11.c_far), channel_id=1, source_target_pairs={{0,1},{1,0},{2,3},{3,2},{4,5},{5,4},{6,7},{7,6},{8,9},{9,8},{10,11... | collective-permute-start | bytes 1474568 | tf_op jit(solution)/shard_map/ppermute | solution.py:492
  83.8 10.2 %collective-permute-start.9 = (bf16[4,80,768]{2,1,0:T(8,128)(2,1)S(1)}, bf16[4,80,768]{2,1,0:T(8,128)(2,1)}, u32[]{:S(2)}, u32[]{:S(2)}) collective-permute-start(bf16[4,80,768]{2,1,0:T(8,128)(2,1)S(1)} %bitcast.79), channel_id=1, source_target_pairs={{0,1},{1,0},{2,3},{3,2},{4,5},{5,4},{6,7},{7,6},{8,9},{9,8},{10,11... | collective-permute-start | bytes 1474568 | tf_op jit(solution)/shard_map/ppermute | solution.py:492
  93.2 2.0 collective-permute-start.10
  109.9 4.9 %copy-start.7 = (f32[4,320,8]{2,1,0:T(8,128)S(1)}, f32[4,320,8]{2,1,0:T(8,128)}, u32[]{:S(2)}) copy-start(f32[4,320,8]{2,1,0:T(8,128)} %get-tuple-element.58) | copy-start | bytes 122884
  109.9 2.1 collective-permute-start.15
  111.0 17.3 %collective-permute-start.14 = (bf16[4,80,768]{2,1,0:T(8,128)(2,1)}, bf16[4,80,768]{2,1,0:T(8,128)(2,1)S(1)}, u32[]{:S(2)}, u32[]{:S(2)}) collective-permute-start(bf16[4,80,768]{2,1,0:T(8,128)(2,1)} %get-tuple-element.60), channel_id=1, source_target_pairs={{0,1},{1,0},{2,3},{3,2},{4,5},{5,4},{6,7},{7,6},{8,9},{9,8},{10,11... | collective-permute-start | bytes 1474568 | tf_op jit(solution)/shard_map/ppermute | solution.py:498
  111.3 25.1 %collective-permute-start.18 = (bf16[4,80,768]{2,1,0:T(8,128)(2,1)}, bf16[4,80,768]{2,1,0:T(8,128)(2,1)S(1)}, u32[]{:S(2)}, u32[]{:S(2)}) collective-permute-start(bf16[4,80,768]{2,1,0:T(8,128)(2,1)} %get-tuple-element.68), channel_id=1, source_target_pairs={{0,1},{1,0},{2,3},{3,2},{4,5},{5,4},{6,7},{7,6},{8,9},{9,8},{10,11... | collective-permute-start | bytes 1474568 | tf_op jit(solution)/shard_map/ppermute | solution.py:496
  113.2 15.1 %collective-permute-start.16 = (bf16[4,80,768]{2,1,0:T(8,128)(2,1)S(1)}, bf16[4,80,768]{2,1,0:T(8,128)(2,1)S(1)}, u32[]{:S(2)}, u32[]{:S(2)}) collective-permute-start(bf16[4,80,768]{2,1,0:T(8,128)(2,1)S(1)} %add_convert_fusion.1), channel_id=1, source_target_pairs={{0,2},{1,3},{2,0},{3,1},{4,6},{5,7},{6,4},{7,5},{8,10},{9,11},{10,... | collective-permute-start | bytes 1474568 | tf_op jit(solution)/shard_map/ppermute | solution.py:498
  116.6 14.1 %all-to-all-start.4 = ((f32[32,1,40]{2,1,0:T(1,128)}), f32[32,1,40]{2,1,0:T(1,128)S(1)}, u32[]{:S(2)}, u32[]{:S(2)}) async-start(f32[32,1,40]{2,1,0:T(1,128)} %bitcast.24), calls=%async_computation.4 | async-start | bytes 32768 | tf_op jit(solution)/shard_map/all_to_all | solution.py:674
  128.3 8.1 %copy-start.13 = (bf16[4,80,768]{2,1,0:T(8,128)(2,1)S(1)}, bf16[4,80,768]{2,1,0:T(8,128)(2,1)}, u32[]{:S(2)}) copy-start(bf16[4,80,768]{2,1,0:T(8,128)(2,1)} %get-tuple-element.66) | copy-start | bytes 1474564
  128.3 8.2 %copy-start.8 = (bf16[4,80,768]{2,1,0:T(8,128)(2,1)S(1)}, bf16[4,80,768]{2,1,0:T(8,128)(2,1)}, u32[]{:S(2)}) copy-start(bf16[4,80,768]{2,1,0:T(8,128)(2,1)} %get-tuple-element.67) | copy-start | bytes 1474564
  130.8 19.7 %all-to-all-start.5 = ((bf16[8,40,768]{2,1,0:T(8,128)(2,1)}), bf16[8,40,768]{2,1,0:T(8,128)(2,1)S(1)}, u32[]{:S(2)}, u32[]{:S(2)}) async-start(bf16[8,40,768]{2,1,0:T(8,128)(2,1)} %bitcast.89), calls=%async_computation.5 | async-start | bytes 983040 | tf_op jit(solution)/shard_map/all_to_all | solution.py:604
  136.4 9.3 %collective-permute-start.17 = (bf16[4,80,768]{2,1,0:T(8,128)(2,1)S(1)}, bf16[4,80,768]{2,1,0:T(8,128)(2,1)S(1)}, u32[]{:S(2)}, u32[]{:S(2)}) collective-permute-start(bf16[4,80,768]{2,1,0:T(8,128)(2,1)S(1)} %copy-done.13), channel_id=1, source_target_pairs={{0,1},{1,0},{2,3},{3,2},{4,5},{5,4},{6,7},{7,6},{8,9},{9,8},{10,11... | collective-permute-start | bytes 1474568 | tf_op jit(solution)/shard_map/ppermute | solution.py:498
  136.6 13.7 %collective-permute-start.19 = (bf16[4,80,768]{2,1,0:T(8,128)(2,1)S(1)}, bf16[4,80,768]{2,1,0:T(8,128)(2,1)S(1)}, u32[]{:S(2)}, u32[]{:S(2)}) collective-permute-start(bf16[4,80,768]{2,1,0:T(8,128)(2,1)S(1)} %add_convert_fusion), channel_id=1, source_target_pairs={{0,2},{1,3},{2,0},{3,1},{4,6},{5,7},{6,4},{7,5},{8,10},{9,11},{10,... | collective-permute-start | bytes 1474568 | tf_op jit(solution)/shard_map/ppermute | solution.py:498
  154.6 7.2 %collective-permute-start.20 = (bf16[128,768]{1,0:T(8,128)(2,1)}, bf16[128,768]{1,0:T(8,128)(2,1)S(1)}, u32[]{:S(2)}, u32[]{:S(2)}) collective-permute-start(bf16[128,768]{1,0:T(8,128)(2,1)} %get-tuple-element.73.refs_0_), channel_id=1, source_target_pairs={{0,2},{1,3},{2,0},{3,1},{4,6},{5,7},{6,4},{7,5},{8,10},{9,11},{10,... | collective-permute-start | bytes 589832 | tf_op jit(solution)/shard_map/ppermute | solution.py:491
  156.1 19.2 %all-to-all-start.6 = ((bf16[8,40,768]{2,1,0:T(8,128)(2,1)}), bf16[8,40,768]{2,1,0:T(8,128)(2,1)S(1)}, u32[]{:S(2)}, u32[]{:S(2)}) async-start(bf16[8,40,768]{2,1,0:T(8,128)(2,1)} %bitcast.96), calls=%async_computation.6 | async-start | bytes 983040 | tf_op jit(solution)/shard_map/all_to_all | solution.py:604
  161.9 1.7 collective-permute-start.21
  161.9 1.7 collective-permute-start.22
  175.3 0.8 copy-start
  176.1 3.8 %copy-start.4 = (f32[1,128,768]{2,1,0:T(8,128)S(1)}, f32[1,128,768]{2,1,0:T(8,128)}, u32[]{:S(2)}) copy-start(f32[1,128,768]{2,1,0:T(8,128)} %param.15) | copy-start | bytes 1179652
  176.1 3.9 %copy-start.15 = (bf16[128,768]{1,0:T(8,128)(2,1)S(1)}, bf16[128,768]{1,0:T(8,128)(2,1)}, u32[]{:S(2)}) copy-start(bf16[128,768]{1,0:T(8,128)(2,1)} %get-tuple-element.82) | copy-start | bytes 589828
  176.1 4.2 %copy-start.14 = (bf16[128,768]{1,0:T(8,128)(2,1)S(1)}, bf16[128,768]{1,0:T(8,128)(2,1)}, u32[]{:S(2)}) copy-start(bf16[128,768]{1,0:T(8,128)(2,1)} %get-tuple-element.80) | copy-start | bytes 589828
  176.1 5.4 %copy-start.11 = (bf16[128,768]{1,0:T(8,128)(2,1)S(1)}, bf16[128,768]{1,0:T(8,128)(2,1)}, u32[]{:S(2)}) copy-start(bf16[128,768]{1,0:T(8,128)(2,1)} %get-tuple-element.81) | copy-start | bytes 589828
  176.1 12.5 %copy-start.6 = (bf16[128,768]{1,0:T(8,128)(2,1)S(1)}, bf16[128,768]{1,0:T(8,128)(2,1)}, u32[]{:S(2)}) copy-start(bf16[128,768]{1,0:T(8,128)(2,1)} %get-tuple-element.79) | copy-start | bytes 589828
  176.1 12.7 %copy-start.1 = (bf16[8,40,768]{2,1,0:T(8,128)(2,1)S(1)}, bf16[8,40,768]{2,1,0:T(8,128)(2,1)}, u32[]{:S(2)}) copy-start(bf16[8,40,768]{2,1,0:T(8,128)(2,1)} %copy-done) | copy-start | bytes 1474564
  176.1 36.4 %all-to-all-start.7 = ((bf16[8,96,896]{2,1,0:T(8,128)(2,1)}), bf16[8,96,896]{2,1,0:T(8,128)(2,1)S(1)}, u32[]{:S(2)}, u32[]{:S(2)}) async-start(bf16[8,96,896]{2,1,0:T(8,128)(2,1)} %bitcast.87), calls=%async_computation.7 | async-start | bytes 2752512 | tf_op jit(solution)/shard_map/all_to_all | solution.py:737
  180.0 1.5 collective-permute-start.24
  180.3 2.6 %collective-permute-start.23 = (bf16[128,768]{1,0:T(8,128)(2,1)S(1)}, bf16[128,768]{1,0:T(8,128)(2,1)S(1)}, u32[]{:S(2)}, u32[]{:S(2)}) collective-permute-start(bf16[128,768]{1,0:T(8,128)(2,1)S(1)} %copy-done.14), channel_id=1, source_target_pairs={{0,1},{1,0},{2,3},{3,2},{4,5},{5,4},{6,7},{7,6},{8,9},{9,8},{10,11... | collective-permute-start | bytes 589832 | tf_op jit(solution)/shard_map/ppermute | solution.py:498
  181.6 7.0 %collective-permute-start.25 = (bf16[128,768]{1,0:T(8,128)(2,1)S(1)}, bf16[128,768]{1,0:T(8,128)(2,1)S(1)}, u32[]{:S(2)}, u32[]{:S(2)}) collective-permute-start(bf16[128,768]{1,0:T(8,128)(2,1)S(1)} %add_convert_fusion.2), channel_id=1, source_target_pairs={{0,2},{1,3},{2,0},{3,1},{4,6},{5,7},{6,4},{7,5},{8,10},{9,11},{10,... | collective-permute-start | bytes 589832 | tf_op jit(solution)/shard_map/ppermute | solution.py:498
  188.6 30.2 %copy-start.9 = (f32[128,768]{1,0:T(8,128)S(1)}, f32[128,768]{1,0:T(8,128)}, u32[]{:S(2)}) copy-start(f32[128,768]{1,0:T(8,128)} %get-tuple-element.72) | copy-start | bytes 1179652
  214.2 3.8 %collective-permute-start.26 = (f32[48,36]{1,0:T(8,128)S(1)}, f32[48,36]{1,0:T(8,128)S(1)}, u32[]{:S(2)}, u32[]{:S(2)}) collective-permute-start(f32[48,36]{1,0:T(8,128)S(1)} %constant_dynamic-slice_fusion.1), channel_id=1, source_target_pairs={{0,2},{1,3},{2,0},{3,1},{4,6},{5,7},{6,4},{7,5},{8,10},{9,11},{10,... | collective-permute-start | bytes 20744 | tf_op jit(solution)/shard_map/ppermute | solution.py:758
  218.8 1.2 collective-permute-start.27
  220.0 0.7 copy-start.10

commit v2 on v1

--- a/solution.py
+++ b/solution.py
@@ -115,7 +115,7 @@
 
 def attend_kernel(
     own, far, near, diag, held_own, held_other, parity,
-    normed_ref, normed_in_ref, qkv_ref, mixed_ref, logsum_ref, vec_ref, held_ref
+    normed_ref, normed_in_ref, qkv_ref, mixed_ref, logsum_ref, vec_ref, held_ref, router_ref
 ):
     bf16 = jnp.bfloat16
     f32 = jnp.float32
@@ -128,6 +128,7 @@
     held = held_ref[...].reshape(outer * 2 * rows, lanes)
     wanted = lax.broadcasted_iota(jnp.int32, (8, lanes), 0) + (columns + EXPERTS)
     picker = (lax.broadcasted_iota(jnp.int32, (8, lanes), 1) == wanted).astype(bf16)
+    router_ref[...] = held[:, columns : columns + EXPERTS]
     vectors = matmul_t(picker, held)
     vec_ref[...] = vectors
     count = own.shape[0]
@@ -407,14 +408,15 @@
     )(first, *rows, *cots, router, *in_hbm([w_in, w_out]))
 
 
-def product_kernel(left, right, out_ref):
+def product_kernel(left, right, *rest):
+    out_ref = rest[-1]
     for index in range(out_ref.shape[0]):
         out_ref[index] = t_matmul(
             left[min(index, left.shape[0] - 1)], right[min(index, right.shape[0] - 1)]
         )
 
 
-def expert_products(left, right):
+def expert_products(left, right, after=()):
     slices = max(left.shape[0], right.shape[0])
     local_experts = min(left.shape[0], right.shape[0])
     shape = (left.shape[2], right.shape[2])
@@ -423,7 +425,8 @@
     return pl.pallas_call(
         product_kernel,
         grid=(local_experts,),
-        in_specs=[block(*left.shape), block(*right.shape)],
+        in_specs=[block(*left.shape), block(*right.shape)]
+        + [pl.BlockSpec(memory_space=pl.ANY)] * len(after),
         out_specs=block(slices, *shape),
         out_shape=shaped(jnp.float32, slices, *shape),
         cost_estimate=pl.CostEstimate(
@@ -434,7 +437,7 @@
         compiler_params=pltpu.CompilerParams(
             vmem_limit_bytes=(16 if left.shape[1] <= 512 else 48) * MIB
         ),
-    )(*in_hbm([left, right]))
+    )(*in_hbm([left, right, *after]))
 
 
 def settle_kernel(own, near, far, regroup, out_ref):
@@ -485,6 +488,7 @@
 
 FAR = [(index, index ^ 2) for index in range(4)]
 NEAR = [(index, index ^ 1) for index in range(4)]
+ACROSS = [(index, index ^ 3) for index in range(4)]
 
 
 def seq_gather(block):
@@ -615,7 +619,7 @@
     )
     image = token_count * seq_size
     columns = 3 * head_cols
-    normed_one, normed_in, qkv, head_mixed, logsum, vectors, held = call(
+    normed_one, normed_in, qkv, head_mixed, logsum, vectors, held, router = call(
         attend_kernel,
         [
             shaped(bf16, image, D),
@@ -625,14 +629,14 @@
             shaped(f32, image, 8),
             shaped(f32, 8, D),
             shaped(bf16, held_own.shape[0], 2, *held_own.shape[1:]),
+            shaped(bf16, D, EXPERTS),
         ],
         [*normed_blocks, held_own, held_other, parity],
         fresh=(1, 2, 3, 4, 5),
         scalars=(6,),
-        flops=6 * (2 * image * D * columns + 4 * image * image * head_cols),
+        flops=3 * (2 * image * D * columns + 4 * image * image * head_cols),
     )
     held = held.reshape(D, lanes)
-    router = held[:, columns : columns + EXPERTS]
     out_partial = matmul(head_mixed, w_out_rows).astype(bf16)
     out_blocks = [out_partial[i * token_count : (i + 1) * token_count] for i in range(seq_size)]
 
@@ -665,7 +669,6 @@
     )
     out_parts, grad_parts = results[:4], results[4:8]
     all_rows, all_cots, hidden_act, grad_inner, dots = results[8:]
-    grad_expert_in = expert_products(all_rows, grad_inner)
     grad_expert_out = expert_products(hidden_act, all_cots)
     me = lax.axis_index("seq")
     turned = jnp.array([0, 2, 1, 3])[me ^ jnp.arange(seq_size)]
@@ -679,7 +682,7 @@
         tiled=True,
     )
     route_dots = jnp.sum(dots.reshape(fsdp_size, seq_size, -1), 1).reshape(1, table_rows)
-    grad_table = from_experts(settle(grad_parts, [grad_expert_in]))
+    grad_table = from_experts(settle(grad_parts, []))
     grad_residual, grad_res_half, small_sums, out_settled = call(
         functools.partial(combine_kernel, copies=copies),
         [
@@ -741,22 +744,21 @@
         concat_axis=0,
         tiled=True,
     )
+    own, near, far = seq_reduce(*gn_parts)
+    grad_expert_in = expert_products(all_rows, grad_inner, [far])
     *grad_squares, small_sums = call(
         finish_kernel,
         [shaped(f32, D // fsdp_size, head_cols)] * 3
         + [shaped(f32, head_cols, D // fsdp_size), shaped(f32, D // fsdp_size, EXPERTS + 4)],
         [grad_weights],
-        after=[block_out],
+        after=[block_out, grad_expert_in],
         fresh=(0,),
     )
-    place = lax.axis_index("seq")
-    for step, swap in ((2, FAR), (1, NEAR)):
-        rows = small_sums.shape[0] // 2
-        upper = (place // step) % 2
-        away = lax.dynamic_slice_in_dim(small_sums, (1 - upper) * rows, rows)
-        kept = lax.dynamic_slice_in_dim(small_sums, upper * rows, rows)
-        small_sums = kept + lax.ppermute(away, "seq", swap)
-    own, near, far = seq_reduce(*gn_parts)
+    pieces = []
+    for step, swap in ((0, None), (2, FAR), (1, NEAR), (3, ACROSS)):
+        piece = lax.dynamic_slice_in_dim(small_sums, (me ^ step) * shard, shard)
+        pieces.append(piece if swap is None else lax.ppermute(piece, "seq", swap))
+    small_sums = (pieces[0] + pieces[1]) + (pieces[2] + pieces[3])
     own_grad_normed = own.astype(f32) + near.astype(f32) + far.astype(f32)
     own_normed, own_inverse = norm_forward(tokens_in)
     grad_tokens = grad_residual + norm_backward(

time: 222 us -> 219 us (0.986)
  waiting for transfers between devices: 85 us -> 81.8 us
    all_to_all x1, waiting for transfers between devices: 21.5 us -> 12.3 us  [body(): lax.all_to_all(grad_weights.reshape(fsdp_size, D // fsdp_size, 4 * head_c...]
    ppermute x4, waiting for transfers between devices: 13.7 us -> 21.4 us  [seq_reduce(): lax.ppermute(pair, 'seq', FAR)]
  transfers between devices with their start and end apart: 36 -> 37, of which waited for: 20 -> 19; matrix products, arithmetic and copies ran while one was open for 6% -> 6% of each run, Pallas kernels for 17% -> 17%
where the time goes in v2:
time: 219 us; the launch traced here: 218 us
  waiting for transfers between devices  81.8 us (37%)
  starting transfers between devices  59.3 us (27%)
  Pallas kernels  59.1 us (27%)
  local copies, waits for them, and re-layouts  6.85 us (3%)
  other arithmetic  6.09 us (3%)
  matrix products  3.5 us (2%)
    pallas_call x9, Pallas kernels, call(): pl.pallas_call(inner, out_shape=outputs, in_specs=[pl.BlockSpec(memory_sp...  29.4 us
    ppermute x4, waiting for transfers between devices, seq_reduce(): lax.ppermute(pair, 'seq', FAR)  21.4 us
    pallas_call x2, Pallas kernels, expert_products(): pl.pallas_call(product_kernel, grid=(local_experts,), in_specs=[block(*le...  15 us
    pallas_call x1, Pallas kernels, experts(): pl.pallas_call(expert_kernel, grid=(local_experts,), in_specs=[pl.BlockSp...  14.7 us
    all_to_all x1, waiting for transfers between devices, body(): lax.all_to_all(grad_weights.reshape(fsdp_size, D // fsdp_size, 4 * head_c...  12.3 us
    all_to_all x2, waiting for transfers between devices, to_experts(): lax.all_to_all(table, 'fsdp', split_axis=0, concat_axis=0, tiled=True)  12 us
    all_to_all x2, starting transfers between devices, from_experts(): lax.all_to_all(settled.reshape(fsdp_size, local_experts * CAP, D), 'fsdp'...  10.9 us
    all_to_all x2, starting transfers between devices, to_experts(): lax.all_to_all(table, 'fsdp', split_axis=0, concat_axis=0, tiled=True)  9.71 us
  transfers between devices with their start and end apart: 37, of which 19 were waited for; matrix products, arithmetic and copies ran while one was open for 6% of the time, Pallas kernels for 17%

profile of v2, /device:TPU:0, one launch (start us, length us, event | category | flops | bytes accessed | tf_op | source)
XLA Modules:
  0.0 217.7 jit_solution(11855992486726011056)
XLA Ops:
  0.7 1.9 shard_map.247
  2.6 7.4 %all-to-all-start = ((bf16[16,24,612]{2,1,0:T(8,128)(2,1)}), bf16[16,24,612]{2,1,0:T(8,128)(2,1)S(1)}, u32[]{:S(2)}, u32[]{:S(2)}) async-start(bf16[16,24,612]{2,1,0:T(8,128)(2,1)} %bitcast.90), calls=%async_computation | async-start | bytes 983040 | tf_op jit(solution)/shard_map/all_to_all | solution.py:559
  10.0 1.9 shard_map.246.refs_0_
  11.9 1.9 collective-permute-start
  13.8 0.7 collective-permute-start.4
  15.1 9.1 %all-to-all-done = bf16[16,24,612]{2,1,0:T(8,128)(2,1)S(1)} async-done(((bf16[16,24,612]{2,1,0:T(8,128)(2,1)}), bf16[16,24,612]{2,1,0:T(8,128)(2,1)S(1)}, u32[]{:S(2)}, u32[]{:S(2)}) %all-to-all-start) | async-done | bytes 470048 | tf_op jit(solution)/shard_map/all_to_all | solution.py:559
  24.2 1.1 collective-permute-start.3
  25.4 0.8 broadcast_in_dim.20
  26.1 4.7 %all-to-all-start.1 = ((bf16[8,24,768]{2,1,0:T(8,128)(2,1)}), bf16[8,24,768]{2,1,0:T(8,128)(2,1)S(1)}, u32[]{:S(2)}, u32[]{:S(2)}) async-start(bf16[8,24,768]{2,1,0:T(8,128)(2,1)} %broadcast_in_dim.20), calls=%async_computation.1 | async-start | bytes 589824 | tf_op jit(solution)/shard_map/all_to_all | solution.py:544
  31.1 1.1 fusion.27
  32.4 7.7 %collective-permute-done.3.refs_5_ = bf16[4,96,612]{2,1,0:T(8,128)(2,1)S(1)} collective-permute-done((bf16[4,96,612]{2,1,0:T(8,128)(2,1)S(1)}, bf16[4,96,612]{2,1,0:T(8,128)(2,1)S(1)}, u32[]{:S(2)}, u32[]{:S(2)}) %collective-permute-start.3) | collective-permute-done | bytes 470048 | tf_op jit(solution)/shard_map/ppermute | solution.py:569
  40.1 4.6 %shard_map.248 = (bf16[512,768]{1,0:T(8,128)(2,1)}, bf16[512,768]{1,0:T(8,128)(2,1)}, bf16[512,576]{1,0:T(8,128)(2,1)}, bf16[512,192]{1,0:T(8,128)(2,1)}, f32[51...) custom-call(bf16[128,768]{1,0:T(8,128)(2,1)} %shard_map.246.refs_0_, ...), custom_call_target="tpu_custom_call" | custom-call | flops 1962934272 | bytes 1726468 | tf_op jit(solution)/shard_map/pallas_call | solution.py:78
  44.7 4.5 %all-to-all-start.3 = ((bf16[8,40,768]{2,1,0:T(8,128)(2,1)}), bf16[8,40,768]{2,1,0:T(8,128)(2,1)S(1)}, u32[]{:S(2)}, u32[]{:S(2)}) async-start(bf16[8,40,768]{2,1,0:T(8,128)(2,1)} %bitcast.16), calls=%async_computation.3 | async-start | bytes 983040 | tf_op jit(solution)/shard_map/all_to_all | solution.py:592
  49.3 1.3 convolution_convert_fusion
  51.2 0.9 collective-permute-done.6
  52.2 2.0 collective-permute-start.7
  54.1 5.2 %collective-permute-done.7.refs_3_ = bf16[128,768]{1,0:T(8,128)(2,1)S(1)} collective-permute-done((bf16[128,768]{1,0:T(8,128)(2,1)S(1)}, bf16[128,768]{1,0:T(8,128)(2,1)S(1)}, u32[]{:S(2)}, u32[]{:S(2)}) %collective-permute-start.7) | collective-permute-done | bytes 196640 | tf_op jit(solution)/shard_map/ppermute | solution.py:502
  59.4 2.5 %shard_map.249 = (f32[128,768]{1,0:T(8,128)}, bf16[128,768]{1,0:T(8,128)(2,1)}, f32[128,32]{1,0:T(8,128)}, bf16[320,768]{1,0:T(8,128)(2,1)}) custom-call(f32[128,768]{1,0:T(8,128)} %bitcast.86, bf16[128,768]{1,0:T(8,128)(2,1)S(1)} %get-tuple-element.99.refs_1_, bf16[128,768]{1,0:T(8,128)(2,1)S(1)} %collective-permute-done.5.refs_2_, ...), custom_call_target="tpu_custom_call" | custom-call | tf_op jit(solution)/shard_map/pallas_call | solution.py:78
  61.9 0.8 all-to-all-done.3
  62.7 5.2 %all-to-all-start.2 = ((bf16[8,40,768]{2,1,0:T(8,128)(2,1)}), bf16[8,40,768]{2,1,0:T(8,128)(2,1)S(1)}, u32[]{:S(2)}, u32[]{:S(2)}) async-start(bf16[8,40,768]{2,1,0:T(8,128)(2,1)} %bitcast.97), calls=%async_computation.2 | async-start | bytes 983040 | tf_op jit(solution)/shard_map/all_to_all | solution.py:592
  68.4 1.8 collective-permute-start.11
  70.2 11.2 %all-to-all-done.2 = bf16[8,40,768]{2,1,0:T(8,128)(2,1)S(1)} async-done(((bf16[8,40,768]{2,1,0:T(8,128)(2,1)}), bf16[8,40,768]{2,1,0:T(8,128)(2,1)S(1)}, u32[]{:S(2)}, u32[]{:S(2)}) %all-to-all-start.2) | async-done | bytes 491552 | tf_op jit(solution)/shard_map/all_to_all | solution.py:592
  81.8 1.6 collective-permute-start.8
  84.0 9.4 %collective-permute-done.8.x_far = bf16[4,80,768]{2,1,0:T(8,128)(2,1)S(1)} collective-permute-done((bf16[4,80,768]{2,1,0:T(8,128)(2,1)S(1)}, bf16[4,80,768]{2,1,0:T(8,128)(2,1)S(1)}, u32[]{:S(2)}, u32[]{:S(2)}) %collective-permute-start.8) | collective-permute-done | bytes 491552 | tf_op jit(solution)/shard_map/ppermute | solution.py:495
  93.4 2.0 collective-permute-done.10.x_diag
  95.4 14.7 %shard_map.250 = (bf16[4,80,768]{2,1,0:T(8,128)(2,1)}, bf16[4,80,768]{2,1,0:T(8,128)(2,1)}, bf16[4,80,768]{2,1,0:T(8,128)(2,1)}, bf16[4,80,768]{2,1,0:T(8,128)(2...) custom-call(s32[1]{0:T(128)} %bitcast.12.first, ...), custom_call_target="tpu_custom_call" | custom-call | flops 6039797760 | bytes 21233664 | tf_op jit(solution)/shard_map/pallas_call | solution.py:382
  110.3 0.6 gather_fusion
  111.0 0.8 fusion.1.refs_3_.refs_13_
  112.2 1.1 add_convert_fusion.1
  113.4 1.6 collective-permute-start.16
  115.6 0.6 gather_fusion.1
  116.3 0.7 broadcast_select_fusion
  116.9 4.0 %all-to-all-start.4 = ((f32[32,1,40]{2,1,0:T(1,128)}), f32[32,1,40]{2,1,0:T(1,128)S(1)}, u32[]{:S(2)}, u32[]{:S(2)}) async-start(f32[32,1,40]{2,1,0:T(1,128)} %bitcast.23), calls=%async_computation.4 | async-start | bytes 32768 | tf_op jit(solution)/shard_map/all_to_all | solution.py:677
  120.9 5.9 %collective-permute-done.16 = bf16[4,80,768]{2,1,0:T(8,128)(2,1)S(1)} collective-permute-done((bf16[4,80,768]{2,1,0:T(8,128)(2,1)S(1)}, bf16[4,80,768]{2,1,0:T(8,128)(2,1)S(1)}, u32[]{:S(2)}, u32[]{:S(2)}) %collective-permute-start.16) | collective-permute-done | bytes 491552 | tf_op jit(solution)/shard_map/ppermute | solution.py:502
  126.8 2.3 %shard_map.251 = bf16[320,768]{1,0:T(8,128)(2,1)} custom-call(bf16[320,768]{1,0:T(8,128)(2,1)} %bitcast.95, bf16[320,768]{1,0:T(8,128)(2,1)S(1)} %bitcast.81, bf16[320,768]{1,0:T(8,128)(2,1)S(1)} %bitcast.82, bf16[320,320]{1,0:T(8,128)(2,1)} %fusion.1.refs_3_.refs_13_), custom_call_target="tpu_custom_call" | custom-call | flops 157286400 | bytes 1679360 | tf_op jit(solution)/shard_map/pallas_call | solution.py:78
  129.2 4.9 %all-to-all-start.5 = ((bf16[8,40,768]{2,1,0:T(8,128)(2,1)}), bf16[8,40,768]{2,1,0:T(8,128)(2,1)S(1)}, u32[]{:S(2)}, u32[]{:S(2)}) async-start(bf16[8,40,768]{2,1,0:T(8,128)(2,1)} %bitcast.89), calls=%async_computation.5 | async-start | bytes 983040 | tf_op jit(solution)/shard_map/all_to_all | solution.py:608
  134.3 1.5 collective-permute-start.19
  135.7 7.4 %shard_map.252.refs_14_ = f32[8,384,768]{2,1,0:T(8,128)} custom-call(bf16[8,320,384]{2,1,0:T(8,128)(2,1)} %get-tuple-element.68.left, bf16[4,320,768]{2,1,0:T(8,128)(2,1)} %get-tuple-element.69.right), custom_call_target="tpu_custom_call" | custom-call | flops 1509949440 | bytes 13369344 | tf_op jit(solution)/shard_map/pallas_call | solution.py:425
  143.2 4.7 %collective-permute-done.19 = bf16[4,80,768]{2,1,0:T(8,128)(2,1)S(1)} collective-permute-done((bf16[4,80,768]{2,1,0:T(8,128)(2,1)S(1)}, bf16[4,80,768]{2,1,0:T(8,128)(2,1)S(1)}, u32[]{:S(2)}, u32[]{:S(2)}) %collective-permute-start.19) | collective-permute-done | bytes 491552 | tf_op jit(solution)/shard_map/ppermute | solution.py:502
  147.9 4.1 %shard_map.253 = (f32[128,768]{1,0:T(8,128)}, bf16[128,768]{1,0:T(8,128)(2,1)}, f32[768,36]{1,0:T(8,128)}, bf16[320,768]{1,0:T(8,128)(2,1)}) custom-call(f32[128,768]{1,0:T(8,128)} %get-tuple-element.55.refs_0_, f32[128,768]{1,0:T(8,128)} %bitcast.92, f32[8,768]{1,0:T(8,128)} %get-tuple-element.53.refs_4_.refs_2_, ...), custom_call_target="tpu_custom_call" | custom-call | bytes 3247360 | tf_op jit(solution)/shard_map/pallas_call | solution.py:78
  152.1 1.4 collective-permute-start.20
  153.5 6.0 %all-to-all-start.6 = ((bf16[8,40,768]{2,1,0:T(8,128)(2,1)}), bf16[8,40,768]{2,1,0:T(8,128)(2,1)S(1)}, u32[]{:S(2)}, u32[]{:S(2)}) async-start(bf16[8,40,768]{2,1,0:T(8,128)(2,1)} %bitcast.96), calls=%async_computation.6 | async-start | bytes 983040 | tf_op jit(solution)/shard_map/all_to_all | solution.py:608
  160.0 1.1 collective-permute-done.21.refs_2_
  161.2 8.8 %shard_map.255 = (bf16[128,768]{1,0:T(8,128)(2,1)}, bf16[128,768]{1,0:T(8,128)(2,1)}, bf16[128,768]{1,0:T(8,128)(2,1)}, bf16[128,768]{1,0:T(8,128)(2,1)}, bf16[768,896]{1,0:T(8,128)(2,1)}) custom-call(bf16[128,768]{1,0:T(8,128)(2,1)} %get-tuple-element.72.refs_0_, bf16[128,768]{1,0:T(8,128)(2,1)S(1)} %collective-permute-done.20.refs_1_, ...), custom_call_target="tpu_custom_call" | custom-call | flops 6845104128 | bytes 4507648 | tf_op jit(solution)/shard_map/pallas_call | solution.py:78
  170.0 2.9 %all-to-all-done.6 = bf16[8,40,768]{2,1,0:T(8,128)(2,1)S(1)} async-done(((bf16[8,40,768]{2,1,0:T(8,128)(2,1)}), bf16[8,40,768]{2,1,0:T(8,128)(2,1)S(1)}, u32[]{:S(2)}, u32[]{:S(2)}) %all-to-all-start.6) | async-done | bytes 491552 | tf_op jit(solution)/shard_map/all_to_all | solution.py:608
  172.9 0.8 copy-done
  173.7 3.8 %all-to-all-start.7 = ((bf16[8,96,896]{2,1,0:T(8,128)(2,1)}), bf16[8,96,896]{2,1,0:T(8,128)(2,1)S(1)}, u32[]{:S(2)}, u32[]{:S(2)}) async-start(bf16[8,96,896]{2,1,0:T(8,128)(2,1)} %bitcast.87), calls=%async_computation.7 | async-start | bytes 2752512 | tf_op jit(solution)/shard_map/all_to_all | solution.py:740
  177.9 1.2 collective-permute-done.24
  179.1 0.7 collective-permute-start.25
  179.8 0.8 slice_reduce_fusion.5
  180.6 5.6 %collective-permute-done.25.rest_0_ = bf16[128,768]{1,0:T(8,128)(2,1)S(1)} collective-permute-done((bf16[128,768]{1,0:T(8,128)(2,1)S(1)}, bf16[128,768]{1,0:T(8,128)(2,1)S(1)}, u32[]{:S(2)}, u32[]{:S(2)}) %collective-permute-start.25) | collective-permute-done | bytes 196640 | tf_op jit(solution)/shard_map/ppermute | solution.py:502
  186.2 0.7 copy-done.5
  186.8 7.7 %shard_map.257.refs_2_ = f32[8,768,384]{2,1,0:T(8,128)} custom-call(bf16[4,320,768]{2,1,0:T(8,128)(2,1)} %get-tuple-element.84.left, bf16[8,320,384]{2,1,0:T(8,128)(2,1)} %get-tuple-element.85.right, bf16[128,768]{1,0:T(8,128)(2,1)} %copy-done.5), custom_call_target="tpu_custom_call" | custom-call | flops 1509949440 | bytes 13369344 | tf_op jit(solution)/shard_map/pallas_call | solution.py:425
  194.5 1.2 fusion.6
  195.7 2.2 shard_map.254.refs_1_
  197.8 12.3 %all-to-all-done.7.refs_0_ = bf16[8,96,896]{2,1,0:T(8,128)(2,1)S(1)} async-done(((bf16[8,96,896]{2,1,0:T(8,128)(2,1)}), bf16[8,96,896]{2,1,0:T(8,128)(2,1)S(1)}, u32[]{:S(2)}, u32[]{:S(2)}) %all-to-all-start.7) | async-done | bytes 1376288 | tf_op jit(solution)/shard_map/all_to_all | solution.py:740
  210.1 0.9 shard_map.258
  211.1 0.7 constant_dynamic-slice_fusion.2
  211.8 0.7 collective-permute-start.28
  212.5 1.4 collective-permute-start.26
  213.9 0.9 add_bitcast_fusion
  214.9 1.3 collective-permute-done.26
  216.2 0.7 add_add_fusion
  216.9 0.7 slice_reduce_fusion.1
  (106 shorter events, 5.9 us)
Async XLA Ops:
  0.6 13.2 %copy-start.17 = (bf16[24,768]{1,0:T(8,128)(2,1)S(1)}, bf16[24,768]{1,0:T(8,128)(2,1)}, u32[]{:S(2)}) copy-start(bf16[24,768]{1,0:T(8,128)(2,1)} %param.22) | copy-start | bytes 110596
  0.7 13.8 %copy-start.14 = (s32[1,128,2]{1,2,0:T(2,128)S(1)}, s32[1,128,2]{1,2,0:T(2,128)}, u32[]{:S(2)}) copy-start(s32[1,128,2]{1,2,0:T(2,128)} %param.16) | copy-start | bytes 3076
  0.7 30.5 %copy-start.7 = (f32[1,128,768]{2,1,0:T(8,128)S(1)}, f32[1,128,768]{2,1,0:T(8,128)}, u32[]{:S(2)}) copy-start(f32[1,128,768]{2,1,0:T(8,128)} %param.28) | copy-start | bytes 1179652
  2.6 21.6 %all-to-all-start = ((bf16[16,24,612]{2,1,0:T(8,128)(2,1)}), bf16[16,24,612]{2,1,0:T(8,128)(2,1)S(1)}, u32[]{:S(2)}, u32[]{:S(2)}) async-start(bf16[16,24,612]{2,1,0:T(8,128)(2,1)} %bitcast.90), calls=%async_computation | async-start | bytes 983040 | tf_op jit(solution)/shard_map/all_to_all | solution.py:559
  11.9 18.9 %collective-permute-start = (bf16[128,768]{1,0:T(8,128)(2,1)}, bf16[128,768]{1,0:T(8,128)(2,1)S(1)}, u32[]{:S(2)}, u32[]{:S(2)}) collective-permute-start(bf16[128,768]{1,0:T(8,128)(2,1)} %shard_map.246.refs_0_), channel_id=1, source_target_pairs={{0,2},{1,3},{2,0},{3,1},{4,6},{5,7},{6,4},{7,5},{8,10},{9,11},{10,... | collective-permute-start | bytes 589832 | tf_op jit(solution)/shard_map/ppermute | solution.py:495
  13.8 18.4 %collective-permute-start.1 = (bf16[128,768]{1,0:T(8,128)(2,1)}, bf16[128,768]{1,0:T(8,128)(2,1)S(1)}, u32[]{:S(2)}, u32[]{:S(2)}) collective-permute-start(bf16[128,768]{1,0:T(8,128)(2,1)} %shard_map.246.refs_0_), channel_id=1, source_target_pairs={{0,1},{1,0},{2,3},{3,2},{4,5},{5,4},{6,7},{7,6},{8,9},{9,8},{10,11... | collective-permute-start | bytes 589832 | tf_op jit(solution)/shard_map/ppermute | solution.py:496
  13.8 11.5 %collective-permute-start.4 = (bf16[24,768]{1,0:T(8,128)(2,1)S(1)}, bf16[24,768]{1,0:T(8,128)(2,1)S(1)}, u32[]{:S(2)}, u32[]{:S(2)}) collective-permute-start(bf16[24,768]{1,0:T(8,128)(2,1)S(1)} %copy-done.17), channel_id=1, source_target_pairs={{0,0},{1,4},{2,8},{3,12},{4,16},{5,20},{6,24},{7,28},{8,1},{9,5},{... | collective-permute-start | bytes 110600 | tf_op jit(solution)/shard_map/ppermute | solution.py:542
  24.2 15.9 %collective-permute-start.3 = (bf16[4,96,612]{2,1,0:T(8,128)(2,1)S(1)}, bf16[4,96,612]{2,1,0:T(8,128)(2,1)S(1)}, u32[]{:S(2)}, u32[]{:S(2)}) collective-permute-start(bf16[4,96,612]{2,1,0:T(8,128)(2,1)S(1)} %bitcast.73), channel_id=1, source_target_pairs={{0,4},{4,0},{8,12},{12,8},{16,20},{20,16},{24,28},{28,24},{1,5},{5... | collective-permute-start | bytes 1410056 | tf_op jit(solution)/shard_map/ppermute | solution.py:569
  26.1 18.6 %all-to-all-start.1 = ((bf16[8,24,768]{2,1,0:T(8,128)(2,1)}), bf16[8,24,768]{2,1,0:T(8,128)(2,1)S(1)}, u32[]{:S(2)}, u32[]{:S(2)}) async-start(bf16[8,24,768]{2,1,0:T(8,128)(2,1)} %broadcast_in_dim.20), calls=%async_computation.1 | async-start | bytes 589824 | tf_op jit(solution)/shard_map/all_to_all | solution.py:544
  30.9 1.5 collective-permute-start.2
  44.7 17.9 %all-to-all-start.3 = ((bf16[8,40,768]{2,1,0:T(8,128)(2,1)}), bf16[8,40,768]{2,1,0:T(8,128)(2,1)S(1)}, u32[]{:S(2)}, u32[]{:S(2)}) async-start(bf16[8,40,768]{2,1,0:T(8,128)(2,1)} %bitcast.16), calls=%async_computation.3 | async-start | bytes 983040 | tf_op jit(solution)/shard_map/all_to_all | solution.py:592
  50.6 1.5 collective-permute-start.6
  50.7 3.4 %collective-permute-start.5 = (bf16[128,768]{1,0:T(8,128)(2,1)S(1)}, bf16[128,768]{1,0:T(8,128)(2,1)S(1)}, u32[]{:S(2)}, u32[]{:S(2)}) collective-permute-start(bf16[128,768]{1,0:T(8,128)(2,1)S(1)} %get-tuple-element.98), channel_id=1, source_target_pairs={{0,1},{1,0},{2,3},{3,2},{4,5},{5,4},{6,7},{7,6},{8,9},{9,8},{10,11... | collective-permute-start | bytes 589832 | tf_op jit(solution)/shard_map/ppermute | solution.py:502
  52.2 7.2 %collective-permute-start.7 = (bf16[128,768]{1,0:T(8,128)(2,1)S(1)}, bf16[128,768]{1,0:T(8,128)(2,1)S(1)}, u32[]{:S(2)}, u32[]{:S(2)}) collective-permute-start(bf16[128,768]{1,0:T(8,128)(2,1)S(1)} %add_convert_fusion.3), channel_id=1, source_target_pairs={{0,2},{1,3},{2,0},{3,1},{4,6},{5,7},{6,4},{7,5},{8,10},{9,11},{10,... | collective-permute-start | bytes 589832 | tf_op jit(solution)/shard_map/ppermute | solution.py:502
  59.4 36.0 %copy-start.2 = (bf16[768,32]{1,0:T(8,128)(2,1)S(1)}, bf16[768,32]{1,0:T(8,128)(2,1)}, u32[]{:S(2)}) copy-start(bf16[768,32]{1,0:T(8,128)(2,1)} %get-tuple-element.54.refs_5_.router.refs_3_) | copy-start | bytes 147460
  62.7 18.7 %all-to-all-start.2 = ((bf16[8,40,768]{2,1,0:T(8,128)(2,1)}), bf16[8,40,768]{2,1,0:T(8,128)(2,1)S(1)}, u32[]{:S(2)}, u32[]{:S(2)}) async-start(bf16[8,40,768]{2,1,0:T(8,128)(2,1)} %bitcast.97), calls=%async_computation.2 | async-start | bytes 983040 | tf_op jit(solution)/shard_map/all_to_all | solution.py:592
  68.4 15.1 %collective-permute-start.11 = (bf16[4,80,768]{2,1,0:T(8,128)(2,1)S(1)}, bf16[4,80,768]{2,1,0:T(8,128)(2,1)S(1)}, u32[]{:S(2)}, u32[]{:S(2)}) collective-permute-start(bf16[4,80,768]{2,1,0:T(8,128)(2,1)S(1)} %bitcast.75), channel_id=1, source_target_pairs={{0,2},{1,3},{2,0},{3,1},{4,6},{5,7},{6,4},{7,5},{8,10},{9,11},{10,... | collective-permute-start | bytes 1474568 | tf_op jit(solution)/shard_map/ppermute | solution.py:495
  81.8 11.6 %collective-permute-start.8 = (bf16[4,80,768]{2,1,0:T(8,128)(2,1)S(1)}, bf16[4,80,768]{2,1,0:T(8,128)(2,1)S(1)}, u32[]{:S(2)}, u32[]{:S(2)}) collective-permute-start(bf16[4,80,768]{2,1,0:T(8,128)(2,1)S(1)} %bitcast.78), channel_id=1, source_target_pairs={{0,2},{1,3},{2,0},{3,1},{4,6},{5,7},{6,4},{7,5},{8,10},{9,11},{10,... | collective-permute-start | bytes 1474568 | tf_op jit(solution)/shard_map/ppermute | solution.py:495
  83.4 10.0 %collective-permute-start.12 = (bf16[4,80,768]{2,1,0:T(8,128)(2,1)S(1)}, bf16[4,80,768]{2,1,0:T(8,128)(2,1)S(1)}, u32[]{:S(2)}, u32[]{:S(2)}) collective-permute-start(bf16[4,80,768]{2,1,0:T(8,128)(2,1)S(1)} %bitcast.76), channel_id=1, source_target_pairs={{0,1},{1,0},{2,3},{3,2},{4,5},{5,4},{6,7},{7,6},{8,9},{9,8},{10,11... | collective-permute-start | bytes 1474568 | tf_op jit(solution)/shard_map/ppermute | solution.py:496
  83.5 10.0 %collective-permute-start.13 = (bf16[4,80,768]{2,1,0:T(8,128)(2,1)S(1)}, bf16[4,80,768]{2,1,0:T(8,128)(2,1)}, u32[]{:S(2)}, u32[]{:S(2)}) collective-permute-start(bf16[4,80,768]{2,1,0:T(8,128)(2,1)S(1)} %collective-permute-done.11.c_far), channel_id=1, source_target_pairs={{0,1},{1,0},{2,3},{3,2},{4,5},{5,4},{6,7},{7,6},{8,9},{9,8},{10,11... | collective-permute-start | bytes 1474568 | tf_op jit(solution)/shard_map/ppermute | solution.py:496
  84.0 9.5 %collective-permute-start.9 = (bf16[4,80,768]{2,1,0:T(8,128)(2,1)S(1)}, bf16[4,80,768]{2,1,0:T(8,128)(2,1)}, u32[]{:S(2)}, u32[]{:S(2)}) collective-permute-start(bf16[4,80,768]{2,1,0:T(8,128)(2,1)S(1)} %bitcast.79), channel_id=1, source_target_pairs={{0,1},{1,0},{2,3},{3,2},{4,5},{5,4},{6,7},{7,6},{8,9},{9,8},{10,11... | collective-permute-start | bytes 1474568 | tf_op jit(solution)/shard_map/ppermute | solution.py:496
  93.4 2.0 collective-permute-start.10
  95.4 14.9 %copy-start.3 = (s32[4]{0:T(128)S(1)}, s32[4]{0:T(128)}, u32[]{:S(2)}) copy-start(s32[4]{0:T(128)} %constant.110.clone) | copy-start | bytes 52
  110.1 5.1 %copy-start.9 = (f32[4,320,8]{2,1,0:T(8,128)S(1)}, f32[4,320,8]{2,1,0:T(8,128)}, u32[]{:S(2)}) copy-start(f32[4,320,8]{2,1,0:T(8,128)} %get-tuple-element.59) | copy-start | bytes 122884
  110.1 2.1 collective-permute-start.15
  111.8 9.1 %collective-permute-start.14 = (bf16[4,80,768]{2,1,0:T(8,128)(2,1)}, bf16[4,80,768]{2,1,0:T(8,128)(2,1)S(1)}, u32[]{:S(2)}, u32[]{:S(2)}) collective-permute-start(bf16[4,80,768]{2,1,0:T(8,128)(2,1)} %get-tuple-element.61), channel_id=1, source_target_pairs={{0,1},{1,0},{2,3},{3,2},{4,5},{5,4},{6,7},{7,6},{8,9},{9,8},{10,11... | collective-permute-start | bytes 1474568 | tf_op jit(solution)/shard_map/ppermute | solution.py:502
  113.4 13.4 %collective-permute-start.16 = (bf16[4,80,768]{2,1,0:T(8,128)(2,1)S(1)}, bf16[4,80,768]{2,1,0:T(8,128)(2,1)S(1)}, u32[]{:S(2)}, u32[]{:S(2)}) collective-permute-start(bf16[4,80,768]{2,1,0:T(8,128)(2,1)S(1)} %add_convert_fusion.1), channel_id=1, source_target_pairs={{0,2},{1,3},{2,0},{3,1},{4,6},{5,7},{6,4},{7,5},{8,10},{9,11},{10,... | collective-permute-start | bytes 1474568 | tf_op jit(solution)/shard_map/ppermute | solution.py:502
  115.0 19.1 %collective-permute-start.18 = (bf16[4,80,768]{2,1,0:T(8,128)(2,1)}, bf16[4,80,768]{2,1,0:T(8,128)(2,1)S(1)}, u32[]{:S(2)}, u32[]{:S(2)}) collective-permute-start(bf16[4,80,768]{2,1,0:T(8,128)(2,1)} %get-tuple-element.67), channel_id=1, source_target_pairs={{0,1},{1,0},{2,3},{3,2},{4,5},{5,4},{6,7},{7,6},{8,9},{9,8},{10,11... | collective-permute-start | bytes 1474568 | tf_op jit(solution)/shard_map/ppermute | solution.py:500
  115.4 18.7 %copy-start.10 = (bf16[4,80,768]{2,1,0:T(8,128)(2,1)S(1)}, bf16[4,80,768]{2,1,0:T(8,128)(2,1)}, u32[]{:S(2)}) copy-start(bf16[4,80,768]{2,1,0:T(8,128)(2,1)} %get-tuple-element.66) | copy-start | bytes 1474564
  116.9 12.2 %all-to-all-start.4 = ((f32[32,1,40]{2,1,0:T(1,128)}), f32[32,1,40]{2,1,0:T(1,128)S(1)}, u32[]{:S(2)}, u32[]{:S(2)}) async-start(f32[32,1,40]{2,1,0:T(1,128)} %bitcast.23), calls=%async_computation.4 | async-start | bytes 32768 | tf_op jit(solution)/shard_map/all_to_all | solution.py:677
  129.2 18.8 %all-to-all-start.5 = ((bf16[8,40,768]{2,1,0:T(8,128)(2,1)}), bf16[8,40,768]{2,1,0:T(8,128)(2,1)S(1)}, u32[]{:S(2)}, u32[]{:S(2)}) async-start(bf16[8,40,768]{2,1,0:T(8,128)(2,1)} %bitcast.89), calls=%async_computation.5 | async-start | bytes 983040 | tf_op jit(solution)/shard_map/all_to_all | solution.py:608
  134.1 9.1 %collective-permute-start.17 = (bf16[4,80,768]{2,1,0:T(8,128)(2,1)}, bf16[4,80,768]{2,1,0:T(8,128)(2,1)S(1)}, u32[]{:S(2)}, u32[]{:S(2)}) collective-permute-start(bf16[4,80,768]{2,1,0:T(8,128)(2,1)} %get-tuple-element.65), channel_id=1, source_target_pairs={{0,1},{1,0},{2,3},{3,2},{4,5},{5,4},{6,7},{7,6},{8,9},{9,8},{10,11... | collective-permute-start | bytes 1474568 | tf_op jit(solution)/shard_map/ppermute | solution.py:502
  134.3 13.7 %collective-permute-start.19 = (bf16[4,80,768]{2,1,0:T(8,128)(2,1)S(1)}, bf16[4,80,768]{2,1,0:T(8,128)(2,1)S(1)}, u32[]{:S(2)}, u32[]{:S(2)}) collective-permute-start(bf16[4,80,768]{2,1,0:T(8,128)(2,1)S(1)} %add_convert_fusion), channel_id=1, source_target_pairs={{0,2},{1,3},{2,0},{3,1},{4,6},{5,7},{6,4},{7,5},{8,10},{9,11},{10,... | collective-permute-start | bytes 1474568 | tf_op jit(solution)/shard_map/ppermute | solution.py:502
  152.1 7.4 %collective-permute-start.20 = (bf16[128,768]{1,0:T(8,128)(2,1)}, bf16[128,768]{1,0:T(8,128)(2,1)S(1)}, u32[]{:S(2)}, u32[]{:S(2)}) collective-permute-start(bf16[128,768]{1,0:T(8,128)(2,1)} %get-tuple-element.72.refs_0_), channel_id=1, source_target_pairs={{0,2},{1,3},{2,0},{3,1},{4,6},{5,7},{6,4},{7,5},{8,10},{9,11},{10,... | collective-permute-start | bytes 589832 | tf_op jit(solution)/shard_map/ppermute | solution.py:495
  153.5 19.4 %all-to-all-start.6 = ((bf16[8,40,768]{2,1,0:T(8,128)(2,1)}), bf16[8,40,768]{2,1,0:T(8,128)(2,1)S(1)}, u32[]{:S(2)}, u32[]{:S(2)}) async-start(bf16[8,40,768]{2,1,0:T(8,128)(2,1)} %bitcast.96), calls=%async_computation.6 | async-start | bytes 983040 | tf_op jit(solution)/shard_map/all_to_all | solution.py:608
  159.5 1.7 collective-permute-start.21
  159.5 1.7 collective-permute-start.22
  172.9 0.8 copy-start
  173.7 3.8 %copy-start.4 = (f32[1,128,768]{2,1,0:T(8,128)S(1)}, f32[1,128,768]{2,1,0:T(8,128)}, u32[]{:S(2)}) copy-start(f32[1,128,768]{2,1,0:T(8,128)} %param.15) | copy-start | bytes 1179652
  173.7 3.9 %copy-start.16 = (bf16[128,768]{1,0:T(8,128)(2,1)S(1)}, bf16[128,768]{1,0:T(8,128)(2,1)}, u32[]{:S(2)}) copy-start(bf16[128,768]{1,0:T(8,128)(2,1)} %get-tuple-element.82) | copy-start | bytes 589828
  173.7 5.4 %copy-start.13 = (bf16[128,768]{1,0:T(8,128)(2,1)S(1)}, bf16[128,768]{1,0:T(8,128)(2,1)}, u32[]{:S(2)}) copy-start(bf16[128,768]{1,0:T(8,128)(2,1)} %get-tuple-element.81) | copy-start | bytes 589828
  173.7 6.2 %copy-start.15 = (bf16[128,768]{1,0:T(8,128)(2,1)S(1)}, bf16[128,768]{1,0:T(8,128)(2,1)}, u32[]{:S(2)}) copy-start(bf16[128,768]{1,0:T(8,128)(2,1)} %get-tuple-element.80) | copy-start | bytes 589828
  173.7 36.4 %all-to-all-start.7 = ((bf16[8,96,896]{2,1,0:T(8,128)(2,1)}), bf16[8,96,896]{2,1,0:T(8,128)(2,1)S(1)}, u32[]{:S(2)}, u32[]{:S(2)}) async-start(bf16[8,96,896]{2,1,0:T(8,128)(2,1)} %bitcast.87), calls=%async_computation.7 | async-start | bytes 2752512 | tf_op jit(solution)/shard_map/all_to_all | solution.py:740
  177.6 1.5 collective-permute-start.24
  179.1 7.0 %collective-permute-start.25 = (bf16[128,768]{1,0:T(8,128)(2,1)S(1)}, bf16[128,768]{1,0:T(8,128)(2,1)S(1)}, u32[]{:S(2)}, u32[]{:S(2)}) collective-permute-start(bf16[128,768]{1,0:T(8,128)(2,1)S(1)} %add_convert_fusion.2), channel_id=1, source_target_pairs={{0,2},{1,3},{2,0},{3,1},{4,6},{5,7},{6,4},{7,5},{8,10},{9,11},{10,... | collective-permute-start | bytes 589832 | tf_op jit(solution)/shard_map/ppermute | solution.py:502
  179.8 14.7 %collective-permute-start.23 = (bf16[128,768]{1,0:T(8,128)(2,1)S(1)}, bf16[128,768]{1,0:T(8,128)(2,1)S(1)}, u32[]{:S(2)}, u32[]{:S(2)}) collective-permute-start(bf16[128,768]{1,0:T(8,128)(2,1)S(1)} %copy-done.15), channel_id=1, source_target_pairs={{0,1},{1,0},{2,3},{3,2},{4,5},{5,4},{6,7},{7,6},{8,9},{9,8},{10,11... | collective-permute-start | bytes 589832 | tf_op jit(solution)/shard_map/ppermute | solution.py:502
  186.2 0.7 copy-start.5
  186.8 7.7 %copy-start.8 = (bf16[128,768]{1,0:T(8,128)(2,1)S(1)}, bf16[128,768]{1,0:T(8,128)(2,1)}, u32[]{:S(2)}) copy-start(bf16[128,768]{1,0:T(8,128)(2,1)} %get-tuple-element.79) | copy-start | bytes 589828
  186.8 8.8 %copy-start.1 = (bf16[8,40,768]{2,1,0:T(8,128)(2,1)S(1)}, bf16[8,40,768]{2,1,0:T(8,128)(2,1)}, u32[]{:S(2)}) copy-start(bf16[8,40,768]{2,1,0:T(8,128)(2,1)} %copy-done) | copy-start | bytes 1474564
  197.8 16.1 %copy-start.6 = (bf16[128,768]{1,0:T(8,128)(2,1)S(1)}, bf16[128,768]{1,0:T(8,128)(2,1)}, u32[]{:S(2)}) copy-start(bf16[128,768]{1,0:T(8,128)(2,1)} %copy-done.5) | copy-start | bytes 589828
  197.8 16.1 %copy-start.11 = (f32[128,768]{1,0:T(8,128)S(1)}, f32[128,768]{1,0:T(8,128)}, u32[]{:S(2)}) copy-start(f32[128,768]{1,0:T(8,128)} %get-tuple-element.71) | copy-start | bytes 1179652
  211.8 3.1 %collective-permute-start.27 = (f32[24,36]{1,0:T(8,128)S(1)}, f32[24,36]{1,0:T(8,128)S(1)}, u32[]{:S(2)}, u32[]{:S(2)}) collective-permute-start(f32[24,36]{1,0:T(8,128)S(1)} %get-tuple-element.102), channel_id=1, source_target_pairs={{0,1},{1,0},{2,3},{3,2},{4,5},{5,4},{6,7},{7,6},{8,9},{9,8},{10,11... | collective-permute-start | bytes 10376 | tf_op jit(solution)/shard_map/ppermute | solution.py:760
  211.8 3.1 %collective-permute-start.28 = (f32[24,36]{1,0:T(8,128)S(1)}, f32[24,36]{1,0:T(8,128)S(1)}, u32[]{:S(2)}, u32[]{:S(2)}) collective-permute-start(f32[24,36]{1,0:T(8,128)S(1)} %get-tuple-element.101), channel_id=1, source_target_pairs={{0,3},{1,2},{2,1},{3,0},{4,7},{5,6},{6,5},{7,4},{8,11},{9,10},{10,... | collective-permute-start | bytes 10376 | tf_op jit(solution)/shard_map/ppermute | solution.py:760
  212.5 3.7 %collective-permute-start.26 = (f32[24,36]{1,0:T(8,128)S(1)}, f32[24,36]{1,0:T(8,128)S(1)}, u32[]{:S(2)}, u32[]{:S(2)}) collective-permute-start(f32[24,36]{1,0:T(8,128)S(1)} %get-tuple-element.100), channel_id=1, source_target_pairs={{0,2},{1,3},{2,0},{3,1},{4,6},{5,7},{6,4},{7,5},{8,10},{9,11},{10,... | collective-permute-start | bytes 10376 | tf_op jit(solution)/shard_map/ppermute | solution.py:760
  216.9 0.7 copy-start.12

commit v3 on v2

--- a/solution.py
+++ b/solution.py
@@ -96,17 +96,6 @@
 
 def in_hbm(operands):
     return [pltpu.with_memory_space_constraint(operand, pltpu.HBM) for operand in operands]
-
-
-def held_back(array, other):
-    anywhere = pl.BlockSpec(memory_space=pl.ANY)
-    return pl.pallas_call(
-        lambda array_ref, other_ref, out_ref: None,
-        out_shape=shaped(array.dtype, *array.shape),
-        in_specs=[anywhere, anywhere],
-        out_specs=anywhere,
-        input_output_aliases={0: 0},
-    )(*in_hbm([array]), other)
 
 
 def first_norm_kernel(tokens, normed_ref):
@@ -669,7 +658,6 @@
     )
     out_parts, grad_parts = results[:4], results[4:8]
     all_rows, all_cots, hidden_act, grad_inner, dots = results[8:]
-    grad_expert_out = expert_products(hidden_act, all_cots)
     me = lax.axis_index("seq")
     turned = jnp.array([0, 2, 1, 3])[me ^ jnp.arange(seq_size)]
     dots = dots[:, :, 0].reshape(local_experts, seq_size, fsdp_size, CAP)
@@ -705,7 +693,6 @@
             *[block.reshape(local_rows, D) for block in seq_reduce(*out_parts)],
             regroup,
         ],
-        after=[grad_expert_out],
         fresh=(6, 7, 8, 9, 11, 12),
     )
 
@@ -736,7 +723,6 @@
         scratch=[pltpu.VMEM((image, D), bf16), pltpu.VMEM((image, columns), bf16)],
         flops=4 * (4 * image * D * 4 * head_cols + 10 * image * image * head_cols),
     )
-    grad_weights = held_back(grad_weights, out_table)
     grad_weights = lax.all_to_all(
         grad_weights.reshape(fsdp_size, D // fsdp_size, 4 * head_cols + 2 * HEAD_DIM),
         "fsdp",
@@ -746,12 +732,13 @@
     )
     own, near, far = seq_reduce(*gn_parts)
     grad_expert_in = expert_products(all_rows, grad_inner, [far])
+    grad_expert_out = expert_products(hidden_act, all_cots, [far])
     *grad_squares, small_sums = call(
         finish_kernel,
         [shaped(f32, D // fsdp_size, head_cols)] * 3
         + [shaped(f32, head_cols, D // fsdp_size), shaped(f32, D // fsdp_size, EXPERTS + 4)],
         [grad_weights],
-        after=[block_out, grad_expert_in],
+        after=[block_out, grad_expert_in, grad_expert_out],
         fresh=(0,),
     )
     pieces = []

time: 219 us -> 218 us (level)
    ppermute x4, waiting for transfers between devices: 21.4 us -> 28.4 us  [seq_reduce(): lax.ppermute(pair, 'seq', FAR)]
    all_to_all x1, waiting for transfers between devices: 12.3 us -> 5.87 us  [body(): lax.all_to_all(grad_weights.reshape(fsdp_size, D // fsdp_size, 4 * head_c...]
  transfers between devices with their start and end apart: 37 -> 37, of which waited for: 19 -> 20; matrix products, arithmetic and copies ran while one was open for 6% -> 5% of each run, Pallas kernels for 17% -> 17%
where the time goes in v3:
time: 218 us; the launch traced here: 217 us
  waiting for transfers between devices  82.7 us (38%)
  starting transfers between devices  59.4 us (27%)
  Pallas kernels  59.1 us (27%)
  local copies, waits for them, and re-layouts  6.08 us (3%)
  other arithmetic  5.16 us (2%)
  matrix products  3.52 us (2%)
    pallas_call x9, Pallas kernels, call(): pl.pallas_call(inner, out_shape=outputs, in_specs=[pl.BlockSpec(memory_sp...  29.4 us
    ppermute x4, waiting for transfers between devices, seq_reduce(): lax.ppermute(pair, 'seq', FAR)  28.4 us
    pallas_call x2, Pallas kernels, expert_products(): pl.pallas_call(product_kernel, grid=(local_experts,), in_specs=[block(*le...  15 us
    pallas_call x1, Pallas kernels, experts(): pl.pallas_call(expert_kernel, grid=(local_experts,), in_specs=[pl.BlockSp...  14.7 us
    all_to_all x2, waiting for transfers between devices, to_experts(): lax.all_to_all(table, 'fsdp', split_axis=0, concat_axis=0, tiled=True)  12 us
    all_to_all x2, starting transfers between devices, from_experts(): lax.all_to_all(settled.reshape(fsdp_size, local_experts * CAP, D), 'fsdp'...  10.9 us
    all_to_all x2, starting transfers between devices, to_experts(): lax.all_to_all(table, 'fsdp', split_axis=0, concat_axis=0, tiled=True)  9.71 us
    ppermute x4, waiting for transfers between devices, seq_gather(): far = lax.ppermute(block, 'seq', FAR)  9.43 us
  transfers between devices with their start and end apart: 37, of which 20 were waited for; matrix products, arithmetic and copies ran while one was open for 5% of the time, Pallas kernels for 17%

profile of v3, /device:TPU:0, one launch (start us, length us, event | category | flops | bytes accessed | tf_op | source)
XLA Modules:
  0.0 216.9 jit_solution(2734631018871591373)
XLA Ops:
  0.7 1.9 shard_map.247
  2.6 7.4 %all-to-all-start = ((bf16[16,24,612]{2,1,0:T(8,128)(2,1)}), bf16[16,24,612]{2,1,0:T(8,128)(2,1)S(1)}, u32[]{:S(2)}, u32[]{:S(2)}) async-start(bf16[16,24,612]{2,1,0:T(8,128)(2,1)} %bitcast.88), calls=%async_computation | async-start | bytes 983040 | tf_op jit(solution)/shard_map/all_to_all | solution.py:548
  10.0 1.9 shard_map.246.refs_0_
  11.9 1.9 collective-permute-start
  13.8 0.7 collective-permute-start.4
  15.1 9.1 %all-to-all-done = bf16[16,24,612]{2,1,0:T(8,128)(2,1)S(1)} async-done(((bf16[16,24,612]{2,1,0:T(8,128)(2,1)}), bf16[16,24,612]{2,1,0:T(8,128)(2,1)S(1)}, u32[]{:S(2)}, u32[]{:S(2)}) %all-to-all-start) | async-done | bytes 470048 | tf_op jit(solution)/shard_map/all_to_all | solution.py:548
  24.2 1.1 collective-permute-start.3
  25.4 0.8 broadcast_in_dim.20
  26.1 4.7 %all-to-all-start.1 = ((bf16[8,24,768]{2,1,0:T(8,128)(2,1)}), bf16[8,24,768]{2,1,0:T(8,128)(2,1)S(1)}, u32[]{:S(2)}, u32[]{:S(2)}) async-start(bf16[8,24,768]{2,1,0:T(8,128)(2,1)} %broadcast_in_dim.20), calls=%async_computation.1 | async-start | bytes 589824 | tf_op jit(solution)/shard_map/all_to_all | solution.py:533
  31.1 1.1 fusion.27
  32.4 7.7 %collective-permute-done.3.refs_5_ = bf16[4,96,612]{2,1,0:T(8,128)(2,1)S(1)} collective-permute-done((bf16[4,96,612]{2,1,0:T(8,128)(2,1)S(1)}, bf16[4,96,612]{2,1,0:T(8,128)(2,1)S(1)}, u32[]{:S(2)}, u32[]{:S(2)}) %collective-permute-start.3) | collective-permute-done | bytes 470048 | tf_op jit(solution)/shard_map/ppermute | solution.py:558
  40.1 4.6 %shard_map.248 = (bf16[512,768]{1,0:T(8,128)(2,1)}, bf16[512,768]{1,0:T(8,128)(2,1)}, bf16[512,576]{1,0:T(8,128)(2,1)}, bf16[512,192]{1,0:T(8,128)(2,1)}, f32[51...) custom-call(bf16[128,768]{1,0:T(8,128)(2,1)} %shard_map.246.refs_0_, ...), custom_call_target="tpu_custom_call" | custom-call | flops 1962934272 | bytes 1726468 | tf_op jit(solution)/shard_map/pallas_call | solution.py:78
  44.8 4.5 %all-to-all-start.3 = ((bf16[8,40,768]{2,1,0:T(8,128)(2,1)}), bf16[8,40,768]{2,1,0:T(8,128)(2,1)S(1)}, u32[]{:S(2)}, u32[]{:S(2)}) async-start(bf16[8,40,768]{2,1,0:T(8,128)(2,1)} %bitcast.16), calls=%async_computation.3 | async-start | bytes 983040 | tf_op jit(solution)/shard_map/all_to_all | solution.py:581
  49.3 1.3 convolution_convert_fusion
  50.7 0.5 collective-permute-start.5
  51.2 0.9 collective-permute-done.6
  52.2 1.9 collective-permute-start.7
  54.1 5.2 %collective-permute-done.7.refs_3_ = bf16[128,768]{1,0:T(8,128)(2,1)S(1)} collective-permute-done((bf16[128,768]{1,0:T(8,128)(2,1)S(1)}, bf16[128,768]{1,0:T(8,128)(2,1)S(1)}, u32[]{:S(2)}, u32[]{:S(2)}) %collective-permute-start.7) | collective-permute-done | bytes 196640 | tf_op jit(solution)/shard_map/ppermute | solution.py:491
  59.4 2.5 %shard_map.249 = (f32[128,768]{1,0:T(8,128)}, bf16[128,768]{1,0:T(8,128)(2,1)}, f32[128,32]{1,0:T(8,128)}, bf16[320,768]{1,0:T(8,128)(2,1)}) custom-call(f32[128,768]{1,0:T(8,128)} %bitcast.85, bf16[128,768]{1,0:T(8,128)(2,1)S(1)} %get-tuple-element.99.refs_1_, bf16[128,768]{1,0:T(8,128)(2,1)S(1)} %collective-permute-done.5.refs_2_, ...), custom_call_target="tpu_custom_call" | custom-call | tf_op jit(solution)/shard_map/pallas_call | solution.py:78
  61.9 0.8 all-to-all-done.3
  62.7 5.2 %all-to-all-start.2 = ((bf16[8,40,768]{2,1,0:T(8,128)(2,1)}), bf16[8,40,768]{2,1,0:T(8,128)(2,1)S(1)}, u32[]{:S(2)}, u32[]{:S(2)}) async-start(bf16[8,40,768]{2,1,0:T(8,128)(2,1)} %bitcast.96), calls=%async_computation.2 | async-start | bytes 983040 | tf_op jit(solution)/shard_map/all_to_all | solution.py:581
  68.4 1.8 collective-permute-start.11
  70.2 11.2 %all-to-all-done.2 = bf16[8,40,768]{2,1,0:T(8,128)(2,1)S(1)} async-done(((bf16[8,40,768]{2,1,0:T(8,128)(2,1)}), bf16[8,40,768]{2,1,0:T(8,128)(2,1)S(1)}, u32[]{:S(2)}, u32[]{:S(2)}) %all-to-all-start.2) | async-done | bytes 491552 | tf_op jit(solution)/shard_map/all_to_all | solution.py:581
  81.8 1.6 collective-permute-start.8
  83.5 0.5 collective-permute-start.13
  84.0 9.4 %collective-permute-done.8.x_far = bf16[4,80,768]{2,1,0:T(8,128)(2,1)S(1)} collective-permute-done((bf16[4,80,768]{2,1,0:T(8,128)(2,1)S(1)}, bf16[4,80,768]{2,1,0:T(8,128)(2,1)S(1)}, u32[]{:S(2)}, u32[]{:S(2)}) %collective-permute-start.8) | collective-permute-done | bytes 491552 | tf_op jit(solution)/shard_map/ppermute | solution.py:484
  93.4 2.0 collective-permute-done.10.x_diag
  95.4 14.7 %shard_map.250 = (bf16[4,80,768]{2,1,0:T(8,128)(2,1)}, bf16[4,80,768]{2,1,0:T(8,128)(2,1)}, bf16[4,80,768]{2,1,0:T(8,128)(2,1)}, bf16[4,80,768]{2,1,0:T(8,128)(2...) custom-call(s32[1]{0:T(128)} %bitcast.12.first, ...), custom_call_target="tpu_custom_call" | custom-call | flops 6039797760 | bytes 21233664 | tf_op jit(solution)/shard_map/pallas_call | solution.py:371
  110.3 0.6 gather_fusion
  111.0 0.8 fusion.1.refs_3_.refs_13_
  112.2 1.1 add_convert_fusion.1
  113.4 1.6 collective-permute-start.16
  115.6 0.6 gather_fusion.1
  116.3 0.7 broadcast_select_fusion
  116.9 4.0 %all-to-all-start.4 = ((f32[32,1,40]{2,1,0:T(1,128)}), f32[32,1,40]{2,1,0:T(1,128)S(1)}, u32[]{:S(2)}, u32[]{:S(2)}) async-start(f32[32,1,40]{2,1,0:T(1,128)} %bitcast.23), calls=%async_computation.4 | async-start | bytes 32768 | tf_op jit(solution)/shard_map/all_to_all | solution.py:665
  120.9 5.9 %collective-permute-done.16 = bf16[4,80,768]{2,1,0:T(8,128)(2,1)S(1)} collective-permute-done((bf16[4,80,768]{2,1,0:T(8,128)(2,1)S(1)}, bf16[4,80,768]{2,1,0:T(8,128)(2,1)S(1)}, u32[]{:S(2)}, u32[]{:S(2)}) %collective-permute-start.16) | collective-permute-done | bytes 491552 | tf_op jit(solution)/shard_map/ppermute | solution.py:491
  126.8 2.4 %shard_map.251 = bf16[320,768]{1,0:T(8,128)(2,1)} custom-call(bf16[320,768]{1,0:T(8,128)(2,1)} %bitcast.94, bf16[320,768]{1,0:T(8,128)(2,1)S(1)} %bitcast.80, bf16[320,768]{1,0:T(8,128)(2,1)S(1)} %bitcast.81, bf16[320,320]{1,0:T(8,128)(2,1)} %fusion.1.refs_3_.refs_13_), custom_call_target="tpu_custom_call" | custom-call | flops 157286400 | bytes 1679360 | tf_op jit(solution)/shard_map/pallas_call | solution.py:78
  129.2 4.9 %all-to-all-start.5 = ((bf16[8,40,768]{2,1,0:T(8,128)(2,1)}), bf16[8,40,768]{2,1,0:T(8,128)(2,1)S(1)}, u32[]{:S(2)}, u32[]{:S(2)}) async-start(bf16[8,40,768]{2,1,0:T(8,128)(2,1)} %bitcast.87), calls=%async_computation.5 | async-start | bytes 983040 | tf_op jit(solution)/shard_map/all_to_all | solution.py:597
  134.3 1.5 collective-permute-start.19
  136.2 11.8 %collective-permute-done.19 = bf16[4,80,768]{2,1,0:T(8,128)(2,1)S(1)} collective-permute-done((bf16[4,80,768]{2,1,0:T(8,128)(2,1)S(1)}, bf16[4,80,768]{2,1,0:T(8,128)(2,1)S(1)}, u32[]{:S(2)}, u32[]{:S(2)}) %collective-permute-start.19) | collective-permute-done | bytes 491552 | tf_op jit(solution)/shard_map/ppermute | solution.py:491
  148.0 4.1 %shard_map.252 = (f32[128,768]{1,0:T(8,128)}, bf16[128,768]{1,0:T(8,128)(2,1)}, f32[768,36]{1,0:T(8,128)}, bf16[320,768]{1,0:T(8,128)(2,1)}) custom-call(f32[128,768]{1,0:T(8,128)} %get-tuple-element.55.refs_0_, f32[128,768]{1,0:T(8,128)} %bitcast.90, f32[8,768]{1,0:T(8,128)} %get-tuple-element.53.refs_4_.refs_2_, ...), custom_call_target="tpu_custom_call" | custom-call | bytes 3247360 | tf_op jit(solution)/shard_map/pallas_call | solution.py:78
  152.1 1.4 collective-permute-start.20
  153.5 6.0 %all-to-all-start.6 = ((bf16[8,40,768]{2,1,0:T(8,128)(2,1)}), bf16[8,40,768]{2,1,0:T(8,128)(2,1)S(1)}, u32[]{:S(2)}, u32[]{:S(2)}) async-start(bf16[8,40,768]{2,1,0:T(8,128)(2,1)} %bitcast.95), calls=%async_computation.6 | async-start | bytes 983040 | tf_op jit(solution)/shard_map/all_to_all | solution.py:597
  160.0 1.1 collective-permute-done.21.refs_2_
  161.2 8.8 %shard_map.254 = (bf16[128,768]{1,0:T(8,128)(2,1)}, bf16[128,768]{1,0:T(8,128)(2,1)}, bf16[128,768]{1,0:T(8,128)(2,1)}, bf16[128,768]{1,0:T(8,128)(2,1)}, bf16[768,896]{1,0:T(8,128)(2,1)}) custom-call(bf16[128,768]{1,0:T(8,128)(2,1)} %get-tuple-element.70.refs_0_, bf16[128,768]{1,0:T(8,128)(2,1)S(1)} %collective-permute-done.20.refs_1_, ...), custom_call_target="tpu_custom_call" | custom-call | flops 6845104128 | bytes 4507648 | tf_op jit(solution)/shard_map/pallas_call | solution.py:78
  170.0 2.9 %all-to-all-done.6 = bf16[8,40,768]{2,1,0:T(8,128)(2,1)S(1)} async-done(((bf16[8,40,768]{2,1,0:T(8,128)(2,1)}), bf16[8,40,768]{2,1,0:T(8,128)(2,1)S(1)}, u32[]{:S(2)}, u32[]{:S(2)}) %all-to-all-start.6) | async-done | bytes 491552 | tf_op jit(solution)/shard_map/all_to_all | solution.py:597
  172.9 3.8 %all-to-all-start.7 = ((bf16[8,96,896]{2,1,0:T(8,128)(2,1)}), bf16[8,96,896]{2,1,0:T(8,128)(2,1)S(1)}, u32[]{:S(2)}, u32[]{:S(2)}) async-start(bf16[8,96,896]{2,1,0:T(8,128)(2,1)} %bitcast.92), calls=%async_computation.7 | async-start | bytes 2752512 | tf_op jit(solution)/shard_map/all_to_all | solution.py:726
  177.1 1.2 collective-permute-done.24
  178.4 0.7 collective-permute-start.25
  179.1 0.8 slice_reduce_fusion.5
  179.9 5.5 %collective-permute-done.25.rest_0_ = bf16[128,768]{1,0:T(8,128)(2,1)S(1)} collective-permute-done((bf16[128,768]{1,0:T(8,128)(2,1)S(1)}, bf16[128,768]{1,0:T(8,128)(2,1)S(1)}, u32[]{:S(2)}, u32[]{:S(2)}) %collective-permute-start.25) | collective-permute-done | bytes 196640 | tf_op jit(solution)/shard_map/ppermute | solution.py:491
  185.4 0.7 copy-done.3
  186.1 7.6 %shard_map.255.refs_2_ = f32[8,768,384]{2,1,0:T(8,128)} custom-call(bf16[4,320,768]{2,1,0:T(8,128)(2,1)} %get-tuple-element.82.left, bf16[8,320,384]{2,1,0:T(8,128)(2,1)} %get-tuple-element.83.right, bf16[128,768]{1,0:T(8,128)(2,1)} %copy-done.3), custom_call_target="tpu_custom_call" | custom-call | flops 1509949440 | bytes 13369344 | tf_op jit(solution)/shard_map/pallas_call | solution.py:414
  193.7 7.4 %shard_map.256.refs_3_ = f32[8,384,768]{2,1,0:T(8,128)} custom-call(bf16[8,320,384]{2,1,0:T(8,128)(2,1)} %get-tuple-element.84.left, bf16[4,320,768]{2,1,0:T(8,128)(2,1)} %get-tuple-element.85.right, bf16[128,768]{1,0:T(8,128)(2,1)} %copy-done.3), custom_call_target="tpu_custom_call" | custom-call | flops 1509949440 | bytes 13369344 | tf_op jit(solution)/shard_map/pallas_call | solution.py:414
  201.3 2.2 shard_map.253.refs_1_
  203.5 5.9 %all-to-all-done.7.refs_0_ = bf16[8,96,896]{2,1,0:T(8,128)(2,1)S(1)} async-done(((bf16[8,96,896]{2,1,0:T(8,128)(2,1)}), bf16[8,96,896]{2,1,0:T(8,128)(2,1)S(1)}, u32[]{:S(2)}, u32[]{:S(2)}) %all-to-all-start.7) | async-done | bytes 1376288 | tf_op jit(solution)/shard_map/all_to_all | solution.py:726
  209.4 0.9 shard_map.257
  210.3 0.7 constant_dynamic-slice_fusion.2
  211.0 0.7 collective-permute-start.28
  211.8 1.4 collective-permute-start.26
  213.2 0.9 add_bitcast_fusion
  214.2 1.3 collective-permute-done.26
  215.5 0.7 add_add_fusion
  216.2 0.7 slice_reduce_fusion.1
  (101 shorter events, 5.5 us)
Async XLA Ops:
  0.6 13.2 %copy-start.15 = (bf16[24,768]{1,0:T(8,128)(2,1)S(1)}, bf16[24,768]{1,0:T(8,128)(2,1)}, u32[]{:S(2)}) copy-start(bf16[24,768]{1,0:T(8,128)(2,1)} %param.22) | copy-start | bytes 110596
  0.7 13.8 %copy-start.12 = (s32[1,128,2]{1,2,0:T(2,128)S(1)}, s32[1,128,2]{1,2,0:T(2,128)}, u32[]{:S(2)}) copy-start(s32[1,128,2]{1,2,0:T(2,128)} %param.16) | copy-start | bytes 3076
  0.7 30.5 %copy-start.5 = (f32[1,128,768]{2,1,0:T(8,128)S(1)}, f32[1,128,768]{2,1,0:T(8,128)}, u32[]{:S(2)}) copy-start(f32[1,128,768]{2,1,0:T(8,128)} %param.28) | copy-start | bytes 1179652
  2.6 21.6 %all-to-all-start = ((bf16[16,24,612]{2,1,0:T(8,128)(2,1)}), bf16[16,24,612]{2,1,0:T(8,128)(2,1)S(1)}, u32[]{:S(2)}, u32[]{:S(2)}) async-start(bf16[16,24,612]{2,1,0:T(8,128)(2,1)} %bitcast.88), calls=%async_computation | async-start | bytes 983040 | tf_op jit(solution)/shard_map/all_to_all | solution.py:548
  11.9 18.9 %collective-permute-start = (bf16[128,768]{1,0:T(8,128)(2,1)}, bf16[128,768]{1,0:T(8,128)(2,1)S(1)}, u32[]{:S(2)}, u32[]{:S(2)}) collective-permute-start(bf16[128,768]{1,0:T(8,128)(2,1)} %shard_map.246.refs_0_), channel_id=1, source_target_pairs={{0,2},{1,3},{2,0},{3,1},{4,6},{5,7},{6,4},{7,5},{8,10},{9,11},{10,... | collective-permute-start | bytes 589832 | tf_op jit(solution)/shard_map/ppermute | solution.py:484
  13.8 18.4 %collective-permute-start.1 = (bf16[128,768]{1,0:T(8,128)(2,1)}, bf16[128,768]{1,0:T(8,128)(2,1)S(1)}, u32[]{:S(2)}, u32[]{:S(2)}) collective-permute-start(bf16[128,768]{1,0:T(8,128)(2,1)} %shard_map.246.refs_0_), channel_id=1, source_target_pairs={{0,1},{1,0},{2,3},{3,2},{4,5},{5,4},{6,7},{7,6},{8,9},{9,8},{10,11... | collective-permute-start | bytes 589832 | tf_op jit(solution)/shard_map/ppermute | solution.py:485
  13.8 11.5 %collective-permute-start.4 = (bf16[24,768]{1,0:T(8,128)(2,1)S(1)}, bf16[24,768]{1,0:T(8,128)(2,1)S(1)}, u32[]{:S(2)}, u32[]{:S(2)}) collective-permute-start(bf16[24,768]{1,0:T(8,128)(2,1)S(1)} %copy-done.15), channel_id=1, source_target_pairs={{0,0},{1,4},{2,8},{3,12},{4,16},{5,20},{6,24},{7,28},{8,1},{9,5},{... | collective-permute-start | bytes 110600 | tf_op jit(solution)/shard_map/ppermute | solution.py:531
  24.2 15.9 %collective-permute-start.3 = (bf16[4,96,612]{2,1,0:T(8,128)(2,1)S(1)}, bf16[4,96,612]{2,1,0:T(8,128)(2,1)S(1)}, u32[]{:S(2)}, u32[]{:S(2)}) collective-permute-start(bf16[4,96,612]{2,1,0:T(8,128)(2,1)S(1)} %bitcast.72), channel_id=1, source_target_pairs={{0,4},{4,0},{8,12},{12,8},{16,20},{20,16},{24,28},{28,24},{1,5},{5... | collective-permute-start | bytes 1410056 | tf_op jit(solution)/shard_map/ppermute | solution.py:558
  26.1 18.6 %all-to-all-start.1 = ((bf16[8,24,768]{2,1,0:T(8,128)(2,1)}), bf16[8,24,768]{2,1,0:T(8,128)(2,1)S(1)}, u32[]{:S(2)}, u32[]{:S(2)}) async-start(bf16[8,24,768]{2,1,0:T(8,128)(2,1)} %broadcast_in_dim.20), calls=%async_computation.1 | async-start | bytes 589824 | tf_op jit(solution)/shard_map/all_to_all | solution.py:533
  30.9 1.5 collective-permute-start.2
  44.8 17.9 %all-to-all-start.3 = ((bf16[8,40,768]{2,1,0:T(8,128)(2,1)}), bf16[8,40,768]{2,1,0:T(8,128)(2,1)S(1)}, u32[]{:S(2)}, u32[]{:S(2)}) async-start(bf16[8,40,768]{2,1,0:T(8,128)(2,1)} %bitcast.16), calls=%async_computation.3 | async-start | bytes 983040 | tf_op jit(solution)/shard_map/all_to_all | solution.py:581
  50.6 1.5 collective-permute-start.6
  50.7 3.4 %collective-permute-start.5 = (bf16[128,768]{1,0:T(8,128)(2,1)S(1)}, bf16[128,768]{1,0:T(8,128)(2,1)S(1)}, u32[]{:S(2)}, u32[]{:S(2)}) collective-permute-start(bf16[128,768]{1,0:T(8,128)(2,1)S(1)} %get-tuple-element.98), channel_id=1, source_target_pairs={{0,1},{1,0},{2,3},{3,2},{4,5},{5,4},{6,7},{7,6},{8,9},{9,8},{10,11... | collective-permute-start | bytes 589832 | tf_op jit(solution)/shard_map/ppermute | solution.py:491
  52.2 7.1 %collective-permute-start.7 = (bf16[128,768]{1,0:T(8,128)(2,1)S(1)}, bf16[128,768]{1,0:T(8,128)(2,1)S(1)}, u32[]{:S(2)}, u32[]{:S(2)}) collective-permute-start(bf16[128,768]{1,0:T(8,128)(2,1)S(1)} %add_convert_fusion.3), channel_id=1, source_target_pairs={{0,2},{1,3},{2,0},{3,1},{4,6},{5,7},{6,4},{7,5},{8,10},{9,11},{10,... | collective-permute-start | bytes 589832 | tf_op jit(solution)/shard_map/ppermute | solution.py:491
  59.4 36.0 %copy-start = (bf16[768,32]{1,0:T(8,128)(2,1)S(1)}, bf16[768,32]{1,0:T(8,128)(2,1)}, u32[]{:S(2)}) copy-start(bf16[768,32]{1,0:T(8,128)(2,1)} %get-tuple-element.54.refs_5_.router.refs_3_) | copy-start | bytes 147460
  62.7 18.7 %all-to-all-start.2 = ((bf16[8,40,768]{2,1,0:T(8,128)(2,1)}), bf16[8,40,768]{2,1,0:T(8,128)(2,1)S(1)}, u32[]{:S(2)}, u32[]{:S(2)}) async-start(bf16[8,40,768]{2,1,0:T(8,128)(2,1)} %bitcast.96), calls=%async_computation.2 | async-start | bytes 983040 | tf_op jit(solution)/shard_map/all_to_all | solution.py:581
  68.4 15.1 %collective-permute-start.11 = (bf16[4,80,768]{2,1,0:T(8,128)(2,1)S(1)}, bf16[4,80,768]{2,1,0:T(8,128)(2,1)S(1)}, u32[]{:S(2)}, u32[]{:S(2)}) collective-permute-start(bf16[4,80,768]{2,1,0:T(8,128)(2,1)S(1)} %bitcast.74), channel_id=1, source_target_pairs={{0,2},{1,3},{2,0},{3,1},{4,6},{5,7},{6,4},{7,5},{8,10},{9,11},{10,... | collective-permute-start | bytes 1474568 | tf_op jit(solution)/shard_map/ppermute | solution.py:484
  81.8 11.6 %collective-permute-start.8 = (bf16[4,80,768]{2,1,0:T(8,128)(2,1)S(1)}, bf16[4,80,768]{2,1,0:T(8,128)(2,1)S(1)}, u32[]{:S(2)}, u32[]{:S(2)}) collective-permute-start(bf16[4,80,768]{2,1,0:T(8,128)(2,1)S(1)} %bitcast.77), channel_id=1, source_target_pairs={{0,2},{1,3},{2,0},{3,1},{4,6},{5,7},{6,4},{7,5},{8,10},{9,11},{10,... | collective-permute-start | bytes 1474568 | tf_op jit(solution)/shard_map/ppermute | solution.py:484
  83.5 10.0 %collective-permute-start.12 = (bf16[4,80,768]{2,1,0:T(8,128)(2,1)S(1)}, bf16[4,80,768]{2,1,0:T(8,128)(2,1)S(1)}, u32[]{:S(2)}, u32[]{:S(2)}) collective-permute-start(bf16[4,80,768]{2,1,0:T(8,128)(2,1)S(1)} %bitcast.75), channel_id=1, source_target_pairs={{0,1},{1,0},{2,3},{3,2},{4,5},{5,4},{6,7},{7,6},{8,9},{9,8},{10,11... | collective-permute-start | bytes 1474568 | tf_op jit(solution)/shard_map/ppermute | solution.py:485
  83.5 10.0 %collective-permute-start.13 = (bf16[4,80,768]{2,1,0:T(8,128)(2,1)S(1)}, bf16[4,80,768]{2,1,0:T(8,128)(2,1)}, u32[]{:S(2)}, u32[]{:S(2)}) collective-permute-start(bf16[4,80,768]{2,1,0:T(8,128)(2,1)S(1)} %collective-permute-done.11.c_far), channel_id=1, source_target_pairs={{0,1},{1,0},{2,3},{3,2},{4,5},{5,4},{6,7},{7,6},{8,9},{9,8},{10,11... | collective-permute-start | bytes 1474568 | tf_op jit(solution)/shard_map/ppermute | solution.py:485
  84.0 9.5 %collective-permute-start.9 = (bf16[4,80,768]{2,1,0:T(8,128)(2,1)S(1)}, bf16[4,80,768]{2,1,0:T(8,128)(2,1)}, u32[]{:S(2)}, u32[]{:S(2)}) collective-permute-start(bf16[4,80,768]{2,1,0:T(8,128)(2,1)S(1)} %bitcast.78), channel_id=1, source_target_pairs={{0,1},{1,0},{2,3},{3,2},{4,5},{5,4},{6,7},{7,6},{8,9},{9,8},{10,11... | collective-permute-start | bytes 1474568 | tf_op jit(solution)/shard_map/ppermute | solution.py:485
  93.4 2.0 collective-permute-start.10
  95.4 14.9 %copy-start.1 = (s32[4]{0:T(128)S(1)}, s32[4]{0:T(128)}, u32[]{:S(2)}) copy-start(s32[4]{0:T(128)} %constant.110.clone) | copy-start | bytes 52
  110.1 5.1 %copy-start.7 = (f32[4,320,8]{2,1,0:T(8,128)S(1)}, f32[4,320,8]{2,1,0:T(8,128)}, u32[]{:S(2)}) copy-start(f32[4,320,8]{2,1,0:T(8,128)} %get-tuple-element.59) | copy-start | bytes 122884
  110.1 2.1 collective-permute-start.15
  111.8 9.1 %collective-permute-start.14 = (bf16[4,80,768]{2,1,0:T(8,128)(2,1)}, bf16[4,80,768]{2,1,0:T(8,128)(2,1)S(1)}, u32[]{:S(2)}, u32[]{:S(2)}) collective-permute-start(bf16[4,80,768]{2,1,0:T(8,128)(2,1)} %get-tuple-element.61), channel_id=1, source_target_pairs={{0,1},{1,0},{2,3},{3,2},{4,5},{5,4},{6,7},{7,6},{8,9},{9,8},{10,11... | collective-permute-start | bytes 1474568 | tf_op jit(solution)/shard_map/ppermute | solution.py:491
  113.4 13.4 %collective-permute-start.16 = (bf16[4,80,768]{2,1,0:T(8,128)(2,1)S(1)}, bf16[4,80,768]{2,1,0:T(8,128)(2,1)S(1)}, u32[]{:S(2)}, u32[]{:S(2)}) collective-permute-start(bf16[4,80,768]{2,1,0:T(8,128)(2,1)S(1)} %add_convert_fusion.1), channel_id=1, source_target_pairs={{0,2},{1,3},{2,0},{3,1},{4,6},{5,7},{6,4},{7,5},{8,10},{9,11},{10,... | collective-permute-start | bytes 1474568 | tf_op jit(solution)/shard_map/ppermute | solution.py:491
  115.0 19.1 %collective-permute-start.18 = (bf16[4,80,768]{2,1,0:T(8,128)(2,1)}, bf16[4,80,768]{2,1,0:T(8,128)(2,1)S(1)}, u32[]{:S(2)}, u32[]{:S(2)}) collective-permute-start(bf16[4,80,768]{2,1,0:T(8,128)(2,1)} %get-tuple-element.67), channel_id=1, source_target_pairs={{0,1},{1,0},{2,3},{3,2},{4,5},{5,4},{6,7},{7,6},{8,9},{9,8},{10,11... | collective-permute-start | bytes 1474568 | tf_op jit(solution)/shard_map/ppermute | solution.py:489
  115.4 18.7 %copy-start.8 = (bf16[4,80,768]{2,1,0:T(8,128)(2,1)S(1)}, bf16[4,80,768]{2,1,0:T(8,128)(2,1)}, u32[]{:S(2)}) copy-start(bf16[4,80,768]{2,1,0:T(8,128)(2,1)} %get-tuple-element.66) | copy-start | bytes 1474564
  116.9 12.3 %all-to-all-start.4 = ((f32[32,1,40]{2,1,0:T(1,128)}), f32[32,1,40]{2,1,0:T(1,128)S(1)}, u32[]{:S(2)}, u32[]{:S(2)}) async-start(f32[32,1,40]{2,1,0:T(1,128)} %bitcast.23), calls=%async_computation.4 | async-start | bytes 32768 | tf_op jit(solution)/shard_map/all_to_all | solution.py:665
  129.2 18.8 %all-to-all-start.5 = ((bf16[8,40,768]{2,1,0:T(8,128)(2,1)}), bf16[8,40,768]{2,1,0:T(8,128)(2,1)S(1)}, u32[]{:S(2)}, u32[]{:S(2)}) async-start(bf16[8,40,768]{2,1,0:T(8,128)(2,1)} %bitcast.87), calls=%async_computation.5 | async-start | bytes 983040 | tf_op jit(solution)/shard_map/all_to_all | solution.py:597
  134.1 2.1 collective-permute-start.17
  134.3 13.7 %collective-permute-start.19 = (bf16[4,80,768]{2,1,0:T(8,128)(2,1)S(1)}, bf16[4,80,768]{2,1,0:T(8,128)(2,1)S(1)}, u32[]{:S(2)}, u32[]{:S(2)}) collective-permute-start(bf16[4,80,768]{2,1,0:T(8,128)(2,1)S(1)} %add_convert_fusion), channel_id=1, source_target_pairs={{0,2},{1,3},{2,0},{3,1},{4,6},{5,7},{6,4},{7,5},{8,10},{9,11},{10,... | collective-permute-start | bytes 1474568 | tf_op jit(solution)/shard_map/ppermute | solution.py:491
  152.1 7.4 %collective-permute-start.20 = (bf16[128,768]{1,0:T(8,128)(2,1)}, bf16[128,768]{1,0:T(8,128)(2,1)S(1)}, u32[]{:S(2)}, u32[]{:S(2)}) collective-permute-start(bf16[128,768]{1,0:T(8,128)(2,1)} %get-tuple-element.70.refs_0_), channel_id=1, source_target_pairs={{0,2},{1,3},{2,0},{3,1},{4,6},{5,7},{6,4},{7,5},{8,10},{9,11},{10,... | collective-permute-start | bytes 589832 | tf_op jit(solution)/shard_map/ppermute | solution.py:484
  153.5 19.4 %all-to-all-start.6 = ((bf16[8,40,768]{2,1,0:T(8,128)(2,1)}), bf16[8,40,768]{2,1,0:T(8,128)(2,1)S(1)}, u32[]{:S(2)}, u32[]{:S(2)}) async-start(bf16[8,40,768]{2,1,0:T(8,128)(2,1)} %bitcast.95), calls=%async_computation.6 | async-start | bytes 983040 | tf_op jit(solution)/shard_map/all_to_all | solution.py:597
  159.5 1.7 collective-permute-start.21
  159.5 1.7 collective-permute-start.22
  170.0 6.7 %copy-start.2 = (f32[1,128,768]{2,1,0:T(8,128)S(1)}, f32[1,128,768]{2,1,0:T(8,128)}, u32[]{:S(2)}) copy-start(f32[1,128,768]{2,1,0:T(8,128)} %param.15) | copy-start | bytes 1179652
  170.0 6.8 %copy-start.14 = (bf16[128,768]{1,0:T(8,128)(2,1)S(1)}, bf16[128,768]{1,0:T(8,128)(2,1)}, u32[]{:S(2)}) copy-start(bf16[128,768]{1,0:T(8,128)(2,1)} %get-tuple-element.80) | copy-start | bytes 589828
  170.0 8.3 %copy-start.11 = (bf16[128,768]{1,0:T(8,128)(2,1)S(1)}, bf16[128,768]{1,0:T(8,128)(2,1)}, u32[]{:S(2)}) copy-start(bf16[128,768]{1,0:T(8,128)(2,1)} %get-tuple-element.79) | copy-start | bytes 589828
  172.9 6.9 %copy-start.13 = (bf16[128,768]{1,0:T(8,128)(2,1)S(1)}, bf16[128,768]{1,0:T(8,128)(2,1)}, u32[]{:S(2)}) copy-start(bf16[128,768]{1,0:T(8,128)(2,1)} %get-tuple-element.78) | copy-start | bytes 589828
  172.9 36.4 %all-to-all-start.7 = ((bf16[8,96,896]{2,1,0:T(8,128)(2,1)}), bf16[8,96,896]{2,1,0:T(8,128)(2,1)S(1)}, u32[]{:S(2)}, u32[]{:S(2)}) async-start(bf16[8,96,896]{2,1,0:T(8,128)(2,1)} %bitcast.92), calls=%async_computation.7 | async-start | bytes 2752512 | tf_op jit(solution)/shard_map/all_to_all | solution.py:726
  176.8 1.5 collective-permute-start.24
  178.4 7.0 %collective-permute-start.25 = (bf16[128,768]{1,0:T(8,128)(2,1)S(1)}, bf16[128,768]{1,0:T(8,128)(2,1)S(1)}, u32[]{:S(2)}, u32[]{:S(2)}) collective-permute-start(bf16[128,768]{1,0:T(8,128)(2,1)S(1)} %add_convert_fusion.2), channel_id=1, source_target_pairs={{0,2},{1,3},{2,0},{3,1},{4,6},{5,7},{6,4},{7,5},{8,10},{9,11},{10,... | collective-permute-start | bytes 589832 | tf_op jit(solution)/shard_map/ppermute | solution.py:491
  179.8 21.3 %collective-permute-start.23 = (bf16[128,768]{1,0:T(8,128)(2,1)S(1)}, bf16[128,768]{1,0:T(8,128)(2,1)S(1)}, u32[]{:S(2)}, u32[]{:S(2)}) collective-permute-start(bf16[128,768]{1,0:T(8,128)(2,1)S(1)} %copy-done.13), channel_id=1, source_target_pairs={{0,1},{1,0},{2,3},{3,2},{4,5},{5,4},{6,7},{7,6},{8,9},{9,8},{10,11... | collective-permute-start | bytes 589832 | tf_op jit(solution)/shard_map/ppermute | solution.py:491
  185.4 0.7 copy-start.3
  193.7 7.4 %copy-start.4 = (bf16[128,768]{1,0:T(8,128)(2,1)S(1)}, bf16[128,768]{1,0:T(8,128)(2,1)}, u32[]{:S(2)}) copy-start(bf16[128,768]{1,0:T(8,128)(2,1)} %copy-done.3) | copy-start | bytes 589828
  193.7 7.4 %copy-start.6 = (bf16[128,768]{1,0:T(8,128)(2,1)S(1)}, bf16[128,768]{1,0:T(8,128)(2,1)}, u32[]{:S(2)}) copy-start(bf16[128,768]{1,0:T(8,128)(2,1)} %get-tuple-element.77) | copy-start | bytes 589828
  203.5 9.7 %copy-start.9 = (f32[128,768]{1,0:T(8,128)S(1)}, f32[128,768]{1,0:T(8,128)}, u32[]{:S(2)}) copy-start(f32[128,768]{1,0:T(8,128)} %get-tuple-element.69) | copy-start | bytes 1179652
  211.0 3.1 %collective-permute-start.27 = (f32[24,36]{1,0:T(8,128)S(1)}, f32[24,36]{1,0:T(8,128)S(1)}, u32[]{:S(2)}, u32[]{:S(2)}) collective-permute-start(f32[24,36]{1,0:T(8,128)S(1)} %get-tuple-element.102), channel_id=1, source_target_pairs={{0,1},{1,0},{2,3},{3,2},{4,5},{5,4},{6,7},{7,6},{8,9},{9,8},{10,11... | collective-permute-start | bytes 10376 | tf_op jit(solution)/shard_map/ppermute | solution.py:747
  211.0 3.1 %collective-permute-start.28 = (f32[24,36]{1,0:T(8,128)S(1)}, f32[24,36]{1,0:T(8,128)S(1)}, u32[]{:S(2)}, u32[]{:S(2)}) collective-permute-start(f32[24,36]{1,0:T(8,128)S(1)} %get-tuple-element.101), channel_id=1, source_target_pairs={{0,3},{1,2},{2,1},{3,0},{4,7},{5,6},{6,5},{7,4},{8,11},{9,10},{10,... | collective-permute-start | bytes 10376 | tf_op jit(solution)/shard_map/ppermute | solution.py:747
  211.8 3.7 %collective-permute-start.26 = (f32[24,36]{1,0:T(8,128)S(1)}, f32[24,36]{1,0:T(8,128)S(1)}, u32[]{:S(2)}, u32[]{:S(2)}) collective-permute-start(f32[24,36]{1,0:T(8,128)S(1)} %get-tuple-element.100), channel_id=1, source_target_pairs={{0,2},{1,3},{2,0},{3,1},{4,6},{5,7},{6,4},{7,5},{8,10},{9,11},{10,... | collective-permute-start | bytes 10376 | tf_op jit(solution)/shard_map/ppermute | solution.py:747
  216.2 0.7 copy-start.10
